TPU v7x, 32 devices: a whole 2x2x4 slice. The times are simulated.
32 devices in a mesh: ri: 4 (over x, core), row: 2 (over y), col: 4 (over z).
Axes of the slice: x: 2, y: 2, z: 4, core: 2. Of those that a mesh axis runs over, the one named last changes fastest.
Arguments:
- three_centre: bfloat16 [32, 256, 2048], P('ri', 'row', 'col'), may hold values from -1 to 1
- density_band: bfloat16 [2048, 5, 128], P('col'), may hold values from -0.25 to 0.25
- band_mask: int32 [16, 5], P('col'), may hold values 0 or 1
Outputs:
- exchange: float32 [256, 256], P('col', 'row')
All inputs are finite; a program needn't handle non-finite values. No bound on the sum of `band_mask` on one device may be relied on, other than what follows from the above.
Results may differ from a plain program's by a relative error of at most 0.0029.
Values may be sent and summed in bfloat16 or wider, within the bound.
No kernel may reach another device: no remote copies, remote signals or barrier semaphores. Data moves between devices by JAX's collectives and lax.ppermute only.
A program may use at most 64 MiB of HBM per device.

v0:
```python
import jax
import jax.numpy as jnp
from jax import lax
from jax.sharding import PartitionSpec as P


def with_halo(block, sides, width):
    for axis, dim in sides:
        count = lax.axis_size(axis)
        forward = [(i, i + 1) for i in range(count - 1)]
        forward.append((count - 1, 0))
        backward = [(target, source) for source, target in forward]
        low = lax.ppermute(
            lax.slice_in_dim(block, block.shape[dim] - width, None, axis=dim), axis, forward
        )
        high = lax.ppermute(lax.slice_in_dim(block, 0, width, axis=dim), axis, backward)
        block = jnp.concatenate([low, block, high], axis=dim)
    return block


def per_device(three_centre, density_band, band_mask):
    band_count = density_band.shape[1]
    centre = band_count // 2
    col_orb = density_band.shape[2]
    blocks = band_mask.shape[0]
    funcs = three_centre.shape[0]
    rows = three_centre.shape[1]
    weights = jnp.repeat(band_mask.astype(jnp.float32), col_orb, axis=0)
    density = (density_band.astype(jnp.float32) * weights[:, :, None]).astype(jnp.bfloat16)
    tensor_ext = with_halo(three_centre, (("col", 2),), centre * col_orb)
    density_ext = with_halo(density, (("col", 0),), centre * col_orb)
    tensor_blocks = tensor_ext.reshape(funcs, rows, blocks + 2 * centre, col_orb)
    density_blocks = density_ext.reshape(blocks + 2 * centre, col_orb, band_count, col_orb)
    mixed = jnp.zeros((funcs, rows, blocks, col_orb), jnp.float32)
    for column in range(band_count):
        first = 2 * centre - column
        mixed = mixed + jnp.einsum(
            "pmbl,bls->pmbs",
            tensor_blocks[:, :, first : first + blocks],
            density_blocks[first : first + blocks, :, column, :],
            preferred_element_type=jnp.float32,
        )
    mixed_low = mixed.reshape(funcs, rows, blocks * col_orb).astype(jnp.bfloat16)
    terms = jnp.einsum(
        "pns,pms->nm",
        lax.all_gather(three_centre, "row", axis=1, tiled=True),
        mixed_low,
        preferred_element_type=jnp.float32,
    )
    summed = lax.psum_scatter(terms, "col", scatter_dimension=0, tiled=True)
    return lax.psum(summed, "ri")


def solution(mesh):
    placed = (P("ri", "row", "col"), P("col", None, None), P("col", None))
    return jax.shard_map(
        per_device, mesh=mesh, in_specs=placed, out_specs=P("col", "row"), check_vma=False
    )
```

profile of v0, /device:TPU:0, one launch (start us, length us, event | category | flops | bytes accessed | tf_op | source)
XLA Modules:
  0.0 98.2 jit_solution(13989789480066731833)
XLA Ops:
  6.5 1.7 %copy.25 = bf16[8,128,512]{1,2,0:T(8,128)(2,1)S(1)} copy(bf16[8,128,512]{2,1,0:T(8,128)(2,1)} %param.3) | data formatting | bytes 2097152 | tf_op args[0]
  8.3 3.1 %collective-permute-start.2 = (bf16[8,128,256]{1,2,0:T(8,128)(2,1)S(1)}, bf16[8,128,256]{1,2,0:T(8,128)(2,1)}, u32[]{:S(2)}, u32[]{:S(2)}) collective-permute-start(bf16[8,128,256]{1,2,0:T(8,128)(2,1)S(1)} %get-tuple-element.10), channel_id=1, source_target_pairs={{0,1},{1,2},{2,3},{3,0},{4,5},{5,6},{6,7},{7,4},{8,9},{9,10},{10,1... | collective-permute-start | bytes 1572872 | tf_op jit(solution)/shard_map/ppermute | solution.py:13
  11.4 2.1 %collective-permute-start.3 = (bf16[8,128,256]{1,2,0:T(8,128)(2,1)S(1)}, bf16[8,128,256]{1,2,0:T(8,128)(2,1)}, u32[]{:S(2)}, u32[]{:S(2)}) collective-permute-start(bf16[8,128,256]{1,2,0:T(8,128)(2,1)S(1)} %get-tuple-element.11), channel_id=1, source_target_pairs={{1,0},{2,1},{3,2},{0,3},{5,4},{6,5},{7,6},{4,7},{9,8},{10,9},{11,1... | collective-permute-start | bytes 1572872 | tf_op jit(solution)/shard_map/ppermute | solution.py:16
  13.5 0.1 copy.23
  13.7 0.4 multiply_convert_fusion
  14.1 0.8 fusion.12
  14.9 3.8 %collective-permute-start.1 = (bf16[256,5,128]{2,0,1:T(8,128)(2,1)S(1)}, bf16[256,5,128]{2,0,1:T(8,128)(2,1)}, u32[]{:S(2)}, u32[]{:S(2)}) collective-permute-start(bf16[256,5,128]{2,0,1:T(8,128)(2,1)S(1)} %get-tuple-element.13), channel_id=1, source_target_pairs={{1,0},{2,1},{3,2},{0,3},{5,4},{6,5},{7,6},{4,7},{9,8},{10,9},{11,1... | collective-permute-start | bytes 983048 | tf_op jit(solution)/shard_map/ppermute | solution.py:16
  18.8 25.8 %collective-permute-done = bf16[256,5,128]{2,0,1:T(8,128)(2,1)S(1)} collective-permute-done((bf16[256,5,128]{2,0,1:T(8,128)(2,1)}, bf16[256,5,128]{2,0,1:T(8,128)(2,1)S(1)}, u32[]{:S(2)}, u32[]{:S(2)}) %collective-permute-start) | collective-permute-done | bytes 327712 | tf_op jit(solution)/shard_map/ppermute | solution.py:13
  44.5 5.6 %collective-permute-done.1 = bf16[256,5,128]{2,0,1:T(8,128)(2,1)} collective-permute-done((bf16[256,5,128]{2,0,1:T(8,128)(2,1)S(1)}, bf16[256,5,128]{2,0,1:T(8,128)(2,1)}, u32[]{:S(2)}, u32[]{:S(2)}) %collective-permute-start.1) | collective-permute-done | bytes 327712 | tf_op jit(solution)/shard_map/ppermute | solution.py:16
  50.2 1.1 %pad_maximum_fusion.1 = bf16[1024,5,128]{2,0,1:T(8,128)(2,1)S(1)} fusion(bf16[256,5,128]{2,0,1:T(8,128)(2,1)} %collective-permute-done.1, bf16[512,5,128]{2,0,1:T(8,128)(2,1)S(1)} %multiply_convert_fusion, bf16[256,5,128]{2,0,1:T(8,128)(2,1)S(1)} %collective-permute-done), kind=kLoop, calls=%fused_computation.3 | loop fusion | flops 3932160 | bytes 2621440 | tf_op jit(solution)/shard_map/concatenate | solution.py:17
  51.3 1.4 %pad_maximum_fusion = bf16[8,128,1024]{1,2,0:T(8,128)(2,1)S(1)} fusion(bf16[8,128,256]{1,2,0:T(8,128)(2,1)} %collective-permute-done.3, bf16[8,128,512]{1,2,0:T(8,128)(2,1)S(1)} %copy.25, bf16[8,128,256]{1,2,0:T(8,128)(2,1)} %collective-permute-done.2), kind=kLoop, calls=%fused_computation | loop fusion | flops 6291456 | bytes 4194304 | tf_op jit(solution)/shard_map/concatenate | solution.py:17
  52.6 1.3 %fusion.10 = (bf16[8,128,4,128]{1,3,2,0:T(8,128)(2,1)S(1)}, bf16[8,128,4,128]{1,3,2,0:T(8,128)(2,1)S(1)}, bf16[8,128,4,128]{1,3,2,0:T(8,128)(2,1)S(1)}, bf16[8,1...) fusion(bf16[8,128,8,128]{1,3,2,0:T(8,128)(2,1)S(1)} %bitcast.54), kind=kLoop, calls=%fused_computation.22 | loop fusion | bytes 10485760 | tf_op jit(solution)/shard_map/slice | solution.py:39
  53.9 0.5 fusion.4
  54.4 0.5 fusion.6
  54.9 0.5 fusion.8
  55.4 0.5 fusion.2
  55.9 0.7 fusion
  56.6 0.1 copy.37
  56.8 2.4 %convolution_bitcast_fusion = f32[256,128]{0,1:T(8,128)S(1)} fusion(bf16[8,128,512]{1,2,0:T(8,128)(2,1)S(1)} %bitcast.55, bf16[8,256,512]{2,1,0:T(8,128)(2,1)} %all-gather.2.cloned.1.call-done), kind=kOutput, calls=%fused_computation.5 | convolution fusion | flops 268435456 | bytes 3276800 | tf_op jit(solution)/shard_map/pns,pms->nm/dot_general | solution.py:44
  59.2 0.7 copy.46
  59.9 19.2 %reduce-scatter.4.cloned.1.call-done = f32[64,128]{1,0:T(8,128)} async-done(((f32[256,128]{1,0:T(8,128)}), f32[64,128]{1,0:T(8,128)}) %reduce-scatter.4.cloned.1.call-update) | async-done | bytes 32784
  79.2 0.8 copy.47
  80.0 10.7 %psum.7 = f32[64,128]{0,1:T(8,128)S(1)} all-reduce(f32[64,128]{0,1:T(8,128)S(1)} %copy.47), channel_id=1, replica_groups=mesh['ri'=4,'row'=2,'col'=4] {'ri'}, use_global_device_ids=true, to_apply=%region_1.0 | all-reduce | flops 8192 | bytes 65536 | tf_op jit(solution)/shard_map/psum | solution.py:51
  90.7 0.7 copy.39
  (16 shorter events, 0.3 us)
Async XLA Ops:
  6.5 7.0 %copy-start.1 = (s32[4,5]{1,0:T(4,128)S(1)}, s32[4,5]{1,0:T(4,128)}, u32[]{:S(2)}) copy-start(s32[4,5]{1,0:T(4,128)} %param.5) | copy-start | bytes 244
  6.5 7.1 %copy-start = (bf16[512,5,128]{2,0,1:T(8,128)(2,1)S(1)}, bf16[512,5,128]{2,0,1:T(8,128)(2,1)}, u32[]{:S(2)}) copy-start(bf16[512,5,128]{2,0,1:T(8,128)(2,1)} %param.4) | copy-start | bytes 1966084
  6.5 50.2 %all-gather.2.cloned.1.call-start = ((), (), s32[]{:S(2)}) async-start(), calls=%async_computation.1 | async-start | bytes 3145728 | tf_op jit(solution)/shard_map/all_gather | solution.py:46
  8.3 42.9 %collective-permute-start.2 = (bf16[8,128,256]{1,2,0:T(8,128)(2,1)S(1)}, bf16[8,128,256]{1,2,0:T(8,128)(2,1)}, u32[]{:S(2)}, u32[]{:S(2)}) collective-permute-start(bf16[8,128,256]{1,2,0:T(8,128)(2,1)S(1)} %get-tuple-element.10), channel_id=1, source_target_pairs={{0,1},{1,2},{2,3},{3,0},{4,5},{5,6},{6,7},{7,4},{8,9},{9,10},{10,1... | collective-permute-start | bytes 1572872 | tf_op jit(solution)/shard_map/ppermute | solution.py:13
  11.4 39.8 %collective-permute-start.3 = (bf16[8,128,256]{1,2,0:T(8,128)(2,1)S(1)}, bf16[8,128,256]{1,2,0:T(8,128)(2,1)}, u32[]{:S(2)}, u32[]{:S(2)}) collective-permute-start(bf16[8,128,256]{1,2,0:T(8,128)(2,1)S(1)} %get-tuple-element.11), channel_id=1, source_target_pairs={{1,0},{2,1},{3,2},{0,3},{5,4},{6,5},{7,6},{4,7},{9,8},{10,9},{11,1... | collective-permute-start | bytes 1572872 | tf_op jit(solution)/shard_map/ppermute | solution.py:16
  14.9 29.7 %collective-permute-start = (bf16[256,5,128]{2,0,1:T(8,128)(2,1)}, bf16[256,5,128]{2,0,1:T(8,128)(2,1)S(1)}, u32[]{:S(2)}, u32[]{:S(2)}) collective-permute-start(bf16[256,5,128]{2,0,1:T(8,128)(2,1)} %get-tuple-element.12), channel_id=1, source_target_pairs={{0,1},{1,2},{2,3},{3,0},{4,5},{5,6},{6,7},{7,4},{8,9},{9,10},{10,1... | collective-permute-start | bytes 983048 | tf_op jit(solution)/shard_map/ppermute | solution.py:13
  14.9 35.3 %collective-permute-start.1 = (bf16[256,5,128]{2,0,1:T(8,128)(2,1)S(1)}, bf16[256,5,128]{2,0,1:T(8,128)(2,1)}, u32[]{:S(2)}, u32[]{:S(2)}) collective-permute-start(bf16[256,5,128]{2,0,1:T(8,128)(2,1)S(1)} %get-tuple-element.13), channel_id=1, source_target_pairs={{1,0},{2,1},{3,2},{0,3},{5,4},{6,5},{7,6},{4,7},{9,8},{10,9},{11,1... | collective-permute-start | bytes 983048 | tf_op jit(solution)/shard_map/ppermute | solution.py:16
  18.7 60.5 %reduce-scatter.4.cloned.1.call-start = ((), (), s32[]{:S(2)}) async-start(), calls=%async_computation.2 | async-start | bytes 163840
Sparse Core Ops, SparseCore 0:
  18.8 31.4 all-gather.1
  60.1 19.0 reduce-scatter.3
where the time goes:
time: 98.5 us; the launch traced here: 98.2 us
  waiting for transfers between devices  50.7 us (51%)
  between operations  13.5 us (14%)
  blocking collectives  10.7 us (11%)
  starting transfers between devices  9.04 us (9%)
  local copies, waits for them, and re-layouts  6.42 us (7%)
  matrix products  5.06 us (5%)
  other arithmetic  2.82 us (3%)
    ppermute x2, waiting for transfers between devices, with_halo(): lax.ppermute(lax.slice_in_dim(block, block.shape[dim] - width, None, axis...  25.8 us
    unnamed x3, waiting for transfers between devices  19.3 us
    psum x1, blocking collectives, per_device(): return lax.psum(summed, 'ri')  10.7 us
    ppermute x2, starting transfers between devices, with_halo(): lax.ppermute(lax.slice_in_dim(block, 0, width, axis=dim), axis, backward)  5.91 us
    ppermute x2, waiting for transfers between devices, with_halo(): lax.ppermute(lax.slice_in_dim(block, 0, width, axis=dim), axis, backward)  5.64 us
    unnamed x9, local copies, waits for them, and re-layouts  3.36 us
    ppermute x2, starting transfers between devices, with_halo(): lax.ppermute(lax.slice_in_dim(block, block.shape[dim] - width, None, axis...  3.08 us
    dot_general x5, matrix products, per_device(): jnp.einsum('pmbl,bls->pmbs', tensor_blocks[:, :, first:first + blocks], d...  2.66 us
  transfers between devices with their start and end apart: 6, of which 3 were waited for; matrix products, arithmetic and copies ran while one was open for 8% of the time, Pallas kernels for 0%

commit v1 on v0

v1 whole, which is shorter than its diff:
```python
import functools

import jax
import jax.numpy as jnp
from jax import lax
from jax.experimental import pallas as pl
from jax.experimental.pallas import tpu as pltpu
from jax.sharding import PartitionSpec as P

AXES = ("ri", "row", "col")
F32 = jnp.float32
BF16 = jnp.bfloat16


def move(value, sizes, target):
    pairs = []
    for i in range(sizes[0]):
        for j in range(sizes[1]):
            for k in range(sizes[2]):
                to = target(i, j, k)
                if to is not None:
                    pairs.append(((i * sizes[1] + j) * sizes[2] + k, (to[0] * sizes[1] + to[1]) * sizes[2] + to[2]))
    return lax.ppermute(value, AXES, pairs)


def owned(rows, cols):
    offsets = [(a, b) for a in range(rows) for b in range(cols)]
    half = len(offsets) // 2
    first = offsets[1:half] + offsets[:1]
    return first, offsets[half:]


def window_dot(parts, lo, hi):
    return jnp.concatenate([part[:, lo:hi] for part in parts], axis=0)


def exchange_kernel(plan, sizes, centre, edge_ref, *refs):
    n_row = sizes[1]
    own_ref = refs[0]
    others = refs[1:n_row]
    halo_ref = refs[n_row]
    halo_others = refs[n_row + 1 : 2 * n_row]
    dens_ref, mask_ref, keep_ref, give_ref, band_ref, kx_ref = refs[2 * n_row :]
    groups = (own_ref,) + others
    halos = (halo_ref,) + halo_others
    chunk, rows, cols = own_ref.shape
    band_count, unused, orb = dens_ref.shape
    blocks = cols // orb
    wide = centre * orb

    band_ref[...] = jnp.zeros_like(band_ref)
    for l in range(blocks):
        for c in range(band_count):
            s = l + c - centre
            if -centre <= s < blocks:
                block = dens_ref[c, l * orb : (l + 1) * orb, :]
                kept = mask_ref[l, c] != 0
                band_ref[(l + centre) * orb : (l + centre + 1) * orb, (s + centre) * orb : (s + centre + 1) * orb] = (
                    jnp.where(kept, block, jnp.zeros_like(block))
                )
    band_ref[:wide, wide : 2 * wide] = edge_ref[...]

    def body(p, total):
        window = jnp.concatenate(
            [jnp.concatenate([halo[p] for halo in halos], axis=0), jnp.concatenate([group[p] for group in groups], axis=0)],
            axis=1,
        )
        parts = []
        for lo in range(0, cols + wide, wide):
            l_lo = wide if lo == 0 else max(0, lo - 2 * wide + wide)
            l_hi = min(cols + wide, lo + 2 * wide)
            parts.append(
                jnp.dot(
                    window[:, l_lo:l_hi],
                    band_ref[l_lo:l_hi, lo : lo + wide],
                    preferred_element_type=F32,
                ).astype(BF16)
            )
        mixed = jnp.concatenate(parts, axis=1)
        return total + lax.dot_general(window, mixed, (((1,), (1,)), ((), ())), preferred_element_type=F32)

    total = jnp.zeros((n_row * rows, n_row * rows), F32)
    for p in range(chunk):
        total = body(p, total)
    for d in range(n_row):
        kx_ref[d] = total[:, d * rows : (d + 1) * rows]

    core = lax.rem(lax.axis_index("ri"), 2)
    row = lax.axis_index("row")
    col = lax.axis_index("col")
    out_rows = n_row * rows // sizes[2]
    per_group = rows // out_rows
    for ref, side in ((keep_ref, core), (give_ref, 1 - core)):
        for k, (zero, one) in enumerate(zip(*plan)):
            dr = jnp.where(side == 0, zero[0], one[0])
            to_col = col ^ jnp.where(side == 0, zero[1], one[1])
            start = ((to_col // per_group) ^ row) * rows + (to_col % per_group) * out_rows
            ref[k] = kx_ref[dr, pl.ds(pl.multiple_of(start, out_rows), out_rows), :]


def per_device(sizes, three_centre, density_band, band_mask):
    n_ri, n_row, n_col = sizes
    funcs, rows, cols = three_centre.shape
    band_count, orb = density_band.shape[1:]
    centre = band_count // 2
    wide = centre * orb
    chunk = funcs // n_row
    row = lax.axis_index("row")
    core = lax.rem(lax.axis_index("ri"), 2)
    plan = owned(n_row, n_col)

    chunks = three_centre.reshape(n_row, chunk, rows, cols)
    mine = lax.dynamic_index_in_dim(chunks, row, 0, keepdims=False)
    theirs = [lax.dynamic_index_in_dim(chunks, row ^ d, 0, keepdims=False) for d in range(1, n_row)]
    density = jnp.transpose(density_band, (1, 0, 2))

    last = cols - wide
    lines = []
    for j in range(centre):
        line = []
        for s in range(centre):
            c = s - j + 2 * centre
            if c < band_count:
                block = density[c, last + j * orb : last + (j + 1) * orb, :]
                line.append(jnp.where(band_mask[cols // orb - centre + j, c] != 0, block, jnp.zeros_like(block)))
            else:
                line.append(jnp.zeros((orb, orb), BF16))
        lines.append(jnp.concatenate(line, axis=1))
    edge = jnp.concatenate(lines, axis=0)

    others = [
        move(theirs[d - 1], sizes, lambda i, j, k, d=d: (i, j ^ d, k)) for d in range(1, n_row)
    ]
    halo_others = [
        move(theirs[d - 1][:, :, last:], sizes, lambda i, j, k, d=d: (i, j ^ d, (k + 1) % n_col))
        for d in range(1, n_row)
    ]
    packed = jnp.concatenate([mine[:, :, last:].reshape(chunk * rows, wide), edge], axis=0)
    packed = move(packed, sizes, lambda i, j, k: (i, j, (k + 1) % n_col))
    halo = packed[: chunk * rows].reshape(chunk, rows, wide)
    edge = packed[chunk * rows :]

    half = n_row * n_col // 2
    out_rows = n_row * rows // n_col
    vmem = pl.BlockSpec(memory_space=pltpu.VMEM)
    window = cols + wide
    keep, give = pl.pallas_call(
        functools.partial(exchange_kernel, plan, sizes, centre),
        out_shape=[jax.ShapeDtypeStruct((half, out_rows, rows), F32)] * 2,
        in_specs=[vmem] * (2 * n_row + 2) + [pl.BlockSpec(memory_space=pltpu.SMEM)],
        out_specs=[vmem] * 2,
        scratch_shapes=[
            pltpu.VMEM((window, window), BF16),
            pltpu.VMEM((n_row, n_row * rows, rows), F32),
        ],
        compiler_params=pltpu.CompilerParams(vmem_limit_bytes=32 * 1024 * 1024),
    )(edge, mine, *others, halo, *halo_others, density, band_mask)

    got = move(give, sizes, lambda i, j, k: (i ^ 1, j, k))
    pieces = keep + got
    total = jnp.where(core == 0, pieces[half - 1], 0.0)
    for n, (zero, one) in enumerate(zip(*plan)):
        def target(i, j, k):
            dr, dc = one if i % 2 else zero
            return None if (dr, dc) == (0, 0) else (i, j ^ dr, k ^ dc)

        total = total + move(pieces[n], sizes, target)
    result = total
    for d in range(1, n_ri):
        result = result + move(total, sizes, lambda i, j, k, d=d: (i ^ d, j, k))
    return result


def solution(mesh):
    sizes = tuple(mesh.shape[axis] for axis in AXES)
    placed = (P("ri", "row", "col"), P("col", None, None), P("col", None))
    return jax.shard_map(
        functools.partial(per_device, sizes), mesh=mesh, in_specs=placed, out_specs=P("col", "row"), check_vma=False
    )
```

time: 98.5 us -> 46.2 us (0.47)
  waiting for transfers between devices: 50.7 us -> 22.5 us
  between operations: 13.5 us -> 2.02 us
  blocking collectives: 10.7 us -> 0 us
  starting transfers between devices: 9.04 us -> 16.5 us
  matrix products: 5.06 us -> 0 us
  local copies, waits for them, and re-layouts: 6.42 us -> 2.08 us
  Pallas kernels: 0 us -> 2.37 us
  other arithmetic: 2.82 us -> 0.7 us
    unnamed x3 -> x0, waiting for transfers between devices: 19.3 us -> none
    psum x1 -> x0, blocking collectives: 10.7 us -> none  [per_device(): return lax.psum(summed, 'ri')]
    ppermute x4 -> x11, waiting for transfers between devices: 31.4 us -> 22.5 us  [move(): return lax.ppermute(value, AXES, pairs)]
    ppermute x4 -> x11, starting transfers between devices: 8.99 us -> 16.5 us  [move(): return lax.ppermute(value, AXES, pairs)]
    dot_general x6 -> x0, matrix products: 5.06 us -> none  [the longest x5 2.66 us: per_device(): jnp.einsum('pmbl,bls->pmbs', tensor_blocks[:, :, first:first + blocks], d...]
    unnamed x9 -> x4, local copies, waits for them, and re-layouts: 3.36 us -> 0.01 us
    concatenate x2 -> x1, other arithmetic: 2.42 us -> 0.03 us  [per_device(): jnp.concatenate([mine[:, :, last:].reshape(chunk * rows, wide), edge], ax...]
    pallas_call x0 -> x1, Pallas kernels: none -> 2.37 us  [per_device(): pl.pallas_call(functools.partial(exchange_kernel, plan, sizes, centre), o...]
  transfers between devices with their start and end apart: 6 -> 11, of which waited for: 3 -> 6; matrix products, arithmetic and copies ran while one was open for 8% -> 2% of each run, Pallas kernels for 0% -> 0%
where the time goes in v1:
time: 46.2 us; the launch traced here: 46.1 us
  waiting for transfers between devices  22.5 us (49%)
  starting transfers between devices  16.5 us (36%)
  Pallas kernels  2.37 us (5%)
  local copies, waits for them, and re-layouts  2.08 us (5%)
  between operations  2.02 us (4%)
  other arithmetic  0.7 us (2%)
    ppermute x11, waiting for transfers between devices, move(): return lax.ppermute(value, AXES, pairs)  22.5 us
    ppermute x11, starting transfers between devices, move(): return lax.ppermute(value, AXES, pairs)  16.5 us
    pallas_call x1, Pallas kernels, per_device(): pl.pallas_call(functools.partial(exchange_kernel, plan, sizes, centre), o...  2.37 us
    squeeze x1, local copies, waits for them, and re-layouts, per_device(): lax.dynamic_index_in_dim(chunks, row ^ d, 0, keepdims=False)  1.33 us
  transfers between devices with their start and end apart: 11, of which 6 were waited for; matrix products, arithmetic and copies ran while one was open for 2% of the time, Pallas kernels for 0%

profile of v1, /device:TPU:0, one launch (start us, length us, event | category | flops | bytes accessed | tf_op | source)
XLA Modules:
  0.0 46.1 jit_solution(14800219629236828498)
XLA Ops:
  0.0 1.3 %dynamic-slice_bitcast_fusion = (bf16[4,128,512]{2,1,0:T(8,128)(2,1)S(1)}, bf16[4,128,512]{2,1,0:T(8,128)(2,1)S(1)}) fusion(bf16[2,4,128,512]{3,2,1,0:T(8,128)(2,1)} %bitcast.31, s32[]{:T(128)S(6)} %select_n.55, s32[]{:T(128)S(6)} %select_n.45), kind=kLoop, calls=%fused_computation.4 | loop fusion | bytes 2097160 | tf_op jit(solution)/shard_map/jit(dynamic_index_in_dim)/squeeze | solution.py:114
  1.3 3.0 %collective-permute-start.1 = (bf16[4,128,512]{2,1,0:T(8,128)(2,1)S(1)}, bf16[4,128,512]{2,1,0:T(8,128)(2,1)S(1)}, u32[]{:S(2)}, u32[]{:S(2)}) collective-permute-start(bf16[4,128,512]{2,1,0:T(8,128)(2,1)S(1)} %get-tuple-element.9), channel_id=1, source_target_pairs={{0,4},{1,5},{2,6},{3,7},{4,0},{5,1},{6,2},{7,3},{8,12},{9,13},{10,... | collective-permute-start | bytes 1572872 | tf_op jit(solution)/shard_map/ppermute | solution.py:23
  4.4 0.7 %fusion.7 = (s32[1,1]{1,0:T(1,128)}, s32[1,1]{1,0:T(1,128)}, s32[1,1]{1,0:T(1,128)}) fusion(s32[4,5]{1,0:T(4,128)S(1)} %copy-done.1), kind=kLoop, calls=%fused_computation.20 | loop fusion | bytes 24 | tf_op jit(solution)/shard_map/slice | solution.py:125
  7.0 1.6 %collective-permute-start = (bf16[768,256]{1,0:T(8,128)(2,1)S(1)}, bf16[768,256]{1,0:T(8,128)(2,1)S(1)}, u32[]{:S(2)}, u32[]{:S(2)}) collective-permute-start(bf16[768,256]{1,0:T(8,128)(2,1)S(1)} %fusion.3), channel_id=1, source_target_pairs={{0,1},{1,2},{2,3},{3,0},{4,5},{5,6},{6,7},{7,4},{8,9},{9,10},{10,1... | collective-permute-start | bytes 1179656 | tf_op jit(solution)/shard_map/ppermute | solution.py:23
  8.7 1.6 %collective-permute-start.2 = (bf16[4,128,256]{2,1,0:T(8,128)(2,1)S(1)}, bf16[4,128,256]{2,1,0:T(8,128)(2,1)S(1)}, u32[]{:S(2)}, u32[]{:S(2)}) collective-permute-start(bf16[4,128,256]{2,1,0:T(8,128)(2,1)S(1)} %slice.63), channel_id=1, source_target_pairs={{0,5},{1,6},{2,7},{3,4},{4,1},{5,2},{6,3},{7,0},{8,13},{9,14},{10,... | collective-permute-start | bytes 786440 | tf_op jit(solution)/shard_map/ppermute | solution.py:23
  10.2 10.7 %collective-permute-done = bf16[768,256]{1,0:T(8,128)(2,1)S(1)} collective-permute-done((bf16[768,256]{1,0:T(8,128)(2,1)S(1)}, bf16[768,256]{1,0:T(8,128)(2,1)S(1)}, u32[]{:S(2)}, u32[]{:S(2)}) %collective-permute-start) | collective-permute-done | bytes 393248 | tf_op jit(solution)/shard_map/ppermute | solution.py:23
  21.0 4.1 %collective-permute-done.2.refs_3_ = bf16[4,128,256]{2,1,0:T(8,128)(2,1)S(1)} collective-permute-done((bf16[4,128,256]{2,1,0:T(8,128)(2,1)S(1)}, bf16[4,128,256]{2,1,0:T(8,128)(2,1)S(1)}, u32[]{:S(2)}, u32[]{:S(2)}) %collective-permute-start.2) | collective-permute-done | bytes 262176 | tf_op jit(solution)/shard_map/ppermute | solution.py:23
  25.1 0.0 collective-permute-done.1.refs_1_
  25.1 2.4 %shard_map.37 = (f32[4,64,128]{2,1,0:T(8,128)S(1)}, f32[4,64,128]{2,1,0:T(8,128)S(1)}) custom-call(bf16[256,256]{1,0:T(8,128)(2,1)S(1)} %slice.61.edge_ref, bf16[4,128,512]{2,1,0:T(8,128)(2,1)S(1)} %get-tuple-element.10.refs_0_, bf16[4,128,512]{2,1,0:T(8,128)(2,1)S(1)} %collective-permute-done.1.refs_1_, bf16[4,128,256]{2,1,0:T(8,128)(2,1)S(1)} %bitcast.27, ...), custom_call_target="tpu_custom_call" | custom-call | tf_op jit(solution)/shard_map/pallas_call | solution.py:147
  27.5 0.1 collective-permute-start.3
  27.5 1.3 %collective-permute-done.3 = f32[4,64,128]{2,1,0:T(8,128)S(1)} collective-permute-done((f32[4,64,128]{2,1,0:T(8,128)S(1)}, f32[4,64,128]{2,1,0:T(8,128)S(1)}, u32[]{:S(2)}, u32[]{:S(2)}) %collective-permute-start.3) | collective-permute-done | bytes 131104 | tf_op jit(solution)/shard_map/ppermute | solution.py:23
  28.9 0.1 collective-permute-start.4
  29.0 2.3 %collective-permute-start.5 = (f32[64,128]{1,0:T(8,128)S(1)}, f32[64,128]{1,0:T(8,128)S(1)}, u32[]{:S(2)}, u32[]{:S(2)}) collective-permute-start(f32[64,128]{1,0:T(8,128)S(1)} %get-tuple-element.16), channel_id=1, source_target_pairs={{0,2},{1,3},{2,0},{3,1},{4,6},{5,7},{6,4},{7,5},{8,13},{9,12},{10,... | collective-permute-start | bytes 98312 | tf_op jit(solution)/shard_map/ppermute | solution.py:23
  31.3 2.1 %collective-permute-start.6 = (f32[64,128]{1,0:T(8,128)S(1)}, f32[64,128]{1,0:T(8,128)S(1)}, u32[]{:S(2)}, u32[]{:S(2)}) collective-permute-start(f32[64,128]{1,0:T(8,128)S(1)} %get-tuple-element.15), channel_id=1, source_target_pairs={{0,3},{1,2},{2,1},{3,0},{4,7},{5,6},{6,5},{7,4},{8,14},{9,15},{10,... | collective-permute-start | bytes 98312 | tf_op jit(solution)/shard_map/ppermute | solution.py:23
  33.4 0.7 %collective-permute-start.7 = (f32[64,128]{1,0:T(8,128)S(1)}, f32[64,128]{1,0:T(8,128)S(1)}, u32[]{:S(2)}, u32[]{:S(2)}) collective-permute-start(f32[64,128]{1,0:T(8,128)S(1)} %get-tuple-element.17), channel_id=1, source_target_pairs={{8,15},{9,14},{10,13},{11,12},{12,11},{13,10},{14,9},{15,8},{24,31... | collective-permute-start | bytes 98312 | tf_op jit(solution)/shard_map/ppermute | solution.py:23
  34.0 0.0 collective-permute-done.4
  34.0 0.0 collective-permute-done.5
  34.0 2.9 %collective-permute-done.6 = f32[64,128]{1,0:T(8,128)S(1)} collective-permute-done((f32[64,128]{1,0:T(8,128)S(1)}, f32[64,128]{1,0:T(8,128)S(1)}, u32[]{:S(2)}, u32[]{:S(2)}) %collective-permute-start.6) | collective-permute-done | bytes 32800 | tf_op jit(solution)/shard_map/ppermute | solution.py:23
  37.0 0.0 collective-permute-done.7
  37.0 4.5 %collective-permute-start.10 = (f32[64,128]{1,0:T(8,128)S(1)}, f32[64,128]{1,0:T(8,128)S(1)}, u32[]{:S(2)}, u32[]{:S(2)}) collective-permute-start(f32[64,128]{1,0:T(8,128)S(1)} %add_add_fusion.1), channel_id=1, source_target_pairs={{0,24},{1,25},{2,26},{3,27},{4,28},{5,29},{6,30},{7,31},{8,16},{9,... | collective-permute-start | bytes 98312 | tf_op jit(solution)/shard_map/ppermute | solution.py:23
  41.5 0.5 %collective-permute-start.9 = (f32[64,128]{1,0:T(8,128)S(1)}, f32[64,128]{1,0:T(8,128)S(1)}, u32[]{:S(2)}, u32[]{:S(2)}) collective-permute-start(f32[64,128]{1,0:T(8,128)S(1)} %add_add_fusion.1), channel_id=1, source_target_pairs={{0,16},{1,17},{2,18},{3,19},{4,20},{5,21},{6,22},{7,23},{8,24},{9,... | collective-permute-start | bytes 98312 | tf_op jit(solution)/shard_map/ppermute | solution.py:23
  42.1 1.2 %collective-permute-done.10 = f32[64,128]{1,0:T(8,128)S(1)} collective-permute-done((f32[64,128]{1,0:T(8,128)S(1)}, f32[64,128]{1,0:T(8,128)S(1)}, u32[]{:S(2)}, u32[]{:S(2)}) %collective-permute-start.10) | collective-permute-done | bytes 32800 | tf_op jit(solution)/shard_map/ppermute | solution.py:23
  43.2 2.2 %collective-permute-done.9 = f32[64,128]{1,0:T(8,128)S(1)} collective-permute-done((f32[64,128]{1,0:T(8,128)S(1)}, f32[64,128]{1,0:T(8,128)S(1)}, u32[]{:S(2)}, u32[]{:S(2)}) %collective-permute-start.9) | collective-permute-done | bytes 32800 | tf_op jit(solution)/shard_map/ppermute | solution.py:23
  45.4 0.6 %add_add_fusion = f32[64,128]{1,0:T(8,128)} fusion(f32[64,128]{1,0:T(8,128)S(1)} %collective-permute-done.10, f32[64,128]{1,0:T(8,128)S(1)} %collective-permute-done.9, f32[64,128]{1,0:T(8,128)S(1)} %add_add_fusion.1, f32[64,128]{1,0:T(8,128)S(1)} %collective-permute-done.8), kind=kLoop, calls=%fused_computation.18 | loop fusion | flops 24576 | bytes 163840 | tf_op jit(solution)/shard_map/add | solution.py:170
  (15 shorter events, 0.2 us)
Async XLA Ops:
  0.0 4.4 %copy-start.1 = (s32[4,5]{1,0:T(4,128)S(1)}, s32[4,5]{1,0:T(4,128)}, u32[]{:S(2)}) copy-start(s32[4,5]{1,0:T(4,128)} %refs_5_.1) | copy-start | bytes 244
  0.0 6.9 %copy-start = (bf16[512,5,128]{2,0,1:T(8,128)(2,1)S(1)}, bf16[512,5,128]{2,0,1:T(8,128)(2,1)}, u32[]{:S(2)}) copy-start(bf16[512,5,128]{2,0,1:T(8,128)(2,1)} %param.4) | copy-start | bytes 1966084
  1.3 23.7 %collective-permute-start.1 = (bf16[4,128,512]{2,1,0:T(8,128)(2,1)S(1)}, bf16[4,128,512]{2,1,0:T(8,128)(2,1)S(1)}, u32[]{:S(2)}, u32[]{:S(2)}) collective-permute-start(bf16[4,128,512]{2,1,0:T(8,128)(2,1)S(1)} %get-tuple-element.9), channel_id=1, source_target_pairs={{0,4},{1,5},{2,6},{3,7},{4,0},{5,1},{6,2},{7,3},{8,12},{9,13},{10,... | collective-permute-start | bytes 1572872 | tf_op jit(solution)/shard_map/ppermute | solution.py:23
  7.0 13.9 %collective-permute-start = (bf16[768,256]{1,0:T(8,128)(2,1)S(1)}, bf16[768,256]{1,0:T(8,128)(2,1)S(1)}, u32[]{:S(2)}, u32[]{:S(2)}) collective-permute-start(bf16[768,256]{1,0:T(8,128)(2,1)S(1)} %fusion.3), channel_id=1, source_target_pairs={{0,1},{1,2},{2,3},{3,0},{4,5},{5,6},{6,7},{7,4},{8,9},{9,10},{10,1... | collective-permute-start | bytes 1179656 | tf_op jit(solution)/shard_map/ppermute | solution.py:23
  8.7 16.4 %collective-permute-start.2 = (bf16[4,128,256]{2,1,0:T(8,128)(2,1)S(1)}, bf16[4,128,256]{2,1,0:T(8,128)(2,1)S(1)}, u32[]{:S(2)}, u32[]{:S(2)}) collective-permute-start(bf16[4,128,256]{2,1,0:T(8,128)(2,1)S(1)} %slice.63), channel_id=1, source_target_pairs={{0,5},{1,6},{2,7},{3,4},{4,1},{5,2},{6,3},{7,0},{8,13},{9,14},{10,... | collective-permute-start | bytes 786440 | tf_op jit(solution)/shard_map/ppermute | solution.py:23
  27.5 1.4 %collective-permute-start.3 = (f32[4,64,128]{2,1,0:T(8,128)S(1)}, f32[4,64,128]{2,1,0:T(8,128)S(1)}, u32[]{:S(2)}, u32[]{:S(2)}) collective-permute-start(f32[4,64,128]{2,1,0:T(8,128)S(1)} %get-tuple-element.8), channel_id=1, source_target_pairs={{0,8},{1,9},{2,10},{3,11},{4,12},{5,13},{6,14},{7,15},{8,0},{9,1},... | collective-permute-start | bytes 393224 | tf_op jit(solution)/shard_map/ppermute | solution.py:23
  28.9 5.1 %collective-permute-start.4 = (f32[64,128]{1,0:T(8,128)S(1)}, f32[64,128]{1,0:T(8,128)S(1)}, u32[]{:S(2)}, u32[]{:S(2)}) collective-permute-start(f32[64,128]{1,0:T(8,128)S(1)} %get-tuple-element.14), channel_id=1, source_target_pairs={{0,1},{1,0},{2,3},{3,2},{4,5},{5,4},{6,7},{7,6},{8,12},{9,13},{10,... | collective-permute-start | bytes 98312 | tf_op jit(solution)/shard_map/ppermute | solution.py:23
  29.0 5.1 %collective-permute-start.5 = (f32[64,128]{1,0:T(8,128)S(1)}, f32[64,128]{1,0:T(8,128)S(1)}, u32[]{:S(2)}, u32[]{:S(2)}) collective-permute-start(f32[64,128]{1,0:T(8,128)S(1)} %get-tuple-element.16), channel_id=1, source_target_pairs={{0,2},{1,3},{2,0},{3,1},{4,6},{5,7},{6,4},{7,5},{8,13},{9,12},{10,... | collective-permute-start | bytes 98312 | tf_op jit(solution)/shard_map/ppermute | solution.py:23
  31.3 5.7 %collective-permute-start.6 = (f32[64,128]{1,0:T(8,128)S(1)}, f32[64,128]{1,0:T(8,128)S(1)}, u32[]{:S(2)}, u32[]{:S(2)}) collective-permute-start(f32[64,128]{1,0:T(8,128)S(1)} %get-tuple-element.15), channel_id=1, source_target_pairs={{0,3},{1,2},{2,1},{3,0},{4,7},{5,6},{6,5},{7,4},{8,14},{9,15},{10,... | collective-permute-start | bytes 98312 | tf_op jit(solution)/shard_map/ppermute | solution.py:23
  33.4 3.6 %collective-permute-start.7 = (f32[64,128]{1,0:T(8,128)S(1)}, f32[64,128]{1,0:T(8,128)S(1)}, u32[]{:S(2)}, u32[]{:S(2)}) collective-permute-start(f32[64,128]{1,0:T(8,128)S(1)} %get-tuple-element.17), channel_id=1, source_target_pairs={{8,15},{9,14},{10,13},{11,12},{12,11},{13,10},{14,9},{15,8},{24,31... | collective-permute-start | bytes 98312 | tf_op jit(solution)/shard_map/ppermute | solution.py:23
  37.0 6.2 %collective-permute-start.10 = (f32[64,128]{1,0:T(8,128)S(1)}, f32[64,128]{1,0:T(8,128)S(1)}, u32[]{:S(2)}, u32[]{:S(2)}) collective-permute-start(f32[64,128]{1,0:T(8,128)S(1)} %add_add_fusion.1), channel_id=1, source_target_pairs={{0,24},{1,25},{2,26},{3,27},{4,28},{5,29},{6,30},{7,31},{8,16},{9,... | collective-permute-start | bytes 98312 | tf_op jit(solution)/shard_map/ppermute | solution.py:23
  41.5 1.7 %collective-permute-start.8 = (f32[64,128]{1,0:T(8,128)S(1)}, f32[64,128]{1,0:T(8,128)S(1)}, u32[]{:S(2)}, u32[]{:S(2)}) collective-permute-start(f32[64,128]{1,0:T(8,128)S(1)} %add_add_fusion.1), channel_id=1, source_target_pairs={{0,8},{1,9},{2,10},{3,11},{4,12},{5,13},{6,14},{7,15},{8,0},{9,1},... | collective-permute-start | bytes 98312 | tf_op jit(solution)/shard_map/ppermute | solution.py:23
  41.5 3.9 %collective-permute-start.9 = (f32[64,128]{1,0:T(8,128)S(1)}, f32[64,128]{1,0:T(8,128)S(1)}, u32[]{:S(2)}, u32[]{:S(2)}) collective-permute-start(f32[64,128]{1,0:T(8,128)S(1)} %add_add_fusion.1), channel_id=1, source_target_pairs={{0,16},{1,17},{2,18},{3,19},{4,20},{5,21},{6,22},{7,23},{8,24},{9,... | collective-permute-start | bytes 98312 | tf_op jit(solution)/shard_map/ppermute | solution.py:23

commit v2 on v1

v2 whole, which is shorter than its diff:
```python
import functools

import jax
import jax.numpy as jnp
from jax import lax
from jax.experimental import pallas as pl
from jax.experimental.pallas import tpu as pltpu
from jax.sharding import PartitionSpec as P

AXES = ("ri", "row", "col")
F32 = jnp.float32
BF16 = jnp.bfloat16
VMEM = pl.BlockSpec(memory_space=pltpu.VMEM)
SMEM = pl.BlockSpec(memory_space=pltpu.SMEM)
PARAMS = pltpu.CompilerParams(vmem_limit_bytes=32 * 1024 * 1024)


def move(value, sizes, target):
    pairs = []
    for i in range(sizes[0]):
        for j in range(sizes[1]):
            for k in range(sizes[2]):
                to = target(i, j, k)
                if to is not None:
                    pairs.append(((i * sizes[1] + j) * sizes[2] + k, (to[0] * sizes[1] + to[1]) * sizes[2] + to[2]))
    return lax.ppermute(value, AXES, pairs)


def after(value, *earlier):
    return lax.optimization_barrier((value,) + earlier)[0]


def owned(rows, cols):
    offsets = [(a, b) for a in range(rows) for b in range(cols)]
    half = len(offsets) // 2
    first = offsets[1:half] + offsets[:1]
    return first, offsets[half:]


def times(a, b):
    return jnp.dot(a, b, preferred_element_type=F32)


def times_turned(a, b):
    return lax.dot_general(a, b, (((1,), (1,)), ((), ())), preferred_element_type=F32)


def density_kernel(centre, mask_ref, dens_ref, local_ref, back_ref, edge_ref, whole_ref):
    band_count, cols, orb = dens_ref.shape
    blocks = cols // orb
    local_ref[...] = jnp.zeros_like(local_ref)
    back_ref[...] = jnp.zeros_like(back_ref)
    whole_ref[...] = jnp.zeros_like(whole_ref)
    for l in range(blocks):
        for c in range(band_count):
            block = dens_ref[c, l * orb : (l + 1) * orb, :]
            block = jnp.where(mask_ref[l, c] != 0, block, jnp.zeros_like(block))
            s = l + c - centre
            if s < 0:
                back_ref[l * orb : (l + 1) * orb, (s + centre) * orb : (s + centre + 1) * orb] = block
            elif s < blocks:
                local_ref[l * orb : (l + 1) * orb, s * orb : (s + 1) * orb] = block
            else:
                first = l - blocks + centre
                whole_ref[first * orb : (first + 1) * orb, (s - blocks) * orb : (s - blocks + 1) * orb] = block
    half = edge_ref.shape[0]
    core = lax.rem(lax.axis_index("ri"), 2)
    edge_ref[...] = whole_ref[pl.ds(pl.multiple_of(core * half, half), half), :]


def inner_kernel(count, wide, *refs):
    own_ref = refs[0]
    rests = refs[1:count]
    edges = refs[count : 2 * count - 1]
    local_ref, total_ref, open_ref = refs[2 * count - 1 :]
    chunk, rows, cols = own_ref.shape
    total = None
    for p in range(chunk):
        left = jnp.concatenate([own_ref[p, :, : cols - wide]] + [ref[p] for ref in rests], axis=0)
        right = jnp.concatenate([own_ref[p, :, cols - wide :]] + [ref[p] for ref in edges], axis=0)
        held = jnp.concatenate([left, right], axis=1)
        mixed = []
        for lo in range(0, cols, wide):
            l_lo, l_hi = max(0, lo - wide), min(cols, lo + 2 * wide)
            mixed.append(times(held[:, l_lo:l_hi], local_ref[l_lo:l_hi, lo : lo + wide]))
        open_ref[p] = mixed[0]
        closed = jnp.concatenate([part.astype(BF16) for part in mixed[1:]], axis=1)
        part = times_turned(held[:, wide:], closed)
        total = part if total is None else total + part
    total_ref[...] = total


def outer_kernel(count, plan, sizes, *refs):
    own_ref = refs[0]
    rests = refs[1:count]
    halos = refs[count : 2 * count]
    back_ref, mine_ref, partner_ref, inner_ref, open_ref, keep_ref, give_ref, edge_ref, kx_ref = refs[2 * count :]
    chunk, rows, wide = halos[0].shape
    half = mine_ref.shape[0]
    core = lax.rem(lax.axis_index("ri"), 2)
    row = lax.axis_index("row")
    col = lax.axis_index("col")
    edge_ref[pl.ds(pl.multiple_of(core * half, half), half), :] = mine_ref[...]
    edge_ref[pl.ds(pl.multiple_of((1 - core) * half, half), half), :] = partner_ref[...]
    total = inner_ref[...]
    for p in range(chunk):
        near = jnp.concatenate([own_ref[p, :, :wide]] + [ref[p, :, :wide] for ref in rests], axis=0)
        halo = jnp.concatenate([ref[p] for ref in halos], axis=0)
        mixed = (open_ref[p] + times(halo, edge_ref[...])).astype(BF16)
        behind = times(near, back_ref[...]).astype(BF16)
        total = total + times_turned(
            jnp.concatenate([near, halo], axis=1), jnp.concatenate([mixed, behind], axis=1)
        )
    for d in range(count):
        kx_ref[d] = total[:, d * rows : (d + 1) * rows]
    out_rows = count * rows // sizes[2]
    per_group = rows // out_rows
    for ref, side in ((give_ref, 1 - core), (keep_ref, core)):
        for k, (zero, one) in enumerate(zip(*plan)):
            dr = jnp.where(side == 0, zero[0], one[0])
            to_col = col ^ jnp.where(side == 0, zero[1], one[1])
            start = ((to_col // per_group) ^ row) * rows + (to_col % per_group) * out_rows
            ref[k] = kx_ref[dr, pl.ds(pl.multiple_of(start, out_rows), out_rows), :]


def per_device(sizes, three_centre, density_band, band_mask):
    n_ri, n_row, n_col = sizes
    funcs, rows, cols = three_centre.shape
    band_count, orb = density_band.shape[1:]
    centre = band_count // 2
    wide = centre * orb
    last = cols - wide
    chunk = funcs // n_row
    row = lax.axis_index("row")
    core = lax.rem(lax.axis_index("ri"), 2)
    plan = owned(n_row, n_col)

    def forward(i, j, k):
        return i, j, (k + 1) % n_col

    def pick(index, lo, hi):
        cut = lax.dynamic_slice(three_centre, (index * chunk, 0, lo), (chunk, rows, hi - lo))
        return cut

    edges = [move(pick(row ^ d, last, cols), sizes, lambda i, j, k, d=d: (i, j ^ d, k)) for d in range(1, n_row)]
    halos = [move(pick(row, last, cols), sizes, forward)]
    mine = pick(row, 0, cols)

    local, back, edge = pl.pallas_call(
        functools.partial(density_kernel, centre),
        out_shape=[
            jax.ShapeDtypeStruct((cols, cols), BF16),
            jax.ShapeDtypeStruct((wide, wide), BF16),
            jax.ShapeDtypeStruct((wide // 2, wide), BF16),
        ],
        in_specs=[SMEM, VMEM],
        out_specs=[VMEM] * 3,
        scratch_shapes=[pltpu.VMEM((wide, wide), BF16)],
        compiler_params=PARAMS,
        cost_estimate=pl.CostEstimate(flops=10**10, bytes_accessed=1, transcendentals=0),
    )(band_mask, jnp.transpose(density_band, (1, 0, 2)))
    edge = move(edge, sizes, forward)
    partner = move(edge, sizes, lambda i, j, k: (i ^ 1, j, k))

    rests = [
        move(after(pick(row ^ d, 0, last), edges[d - 1]), sizes, lambda i, j, k, d=d: (i, j ^ d, k))
        for d in range(1, n_row)
    ]
    halos += [move(part, sizes, forward) for part in edges]

    whole = n_row * rows
    total, open_part = pl.pallas_call(
        functools.partial(inner_kernel, n_row, wide),
        out_shape=[jax.ShapeDtypeStruct((whole, whole), F32), jax.ShapeDtypeStruct((chunk, whole, wide), F32)],
        in_specs=[VMEM] * (2 * n_row),
        out_specs=[VMEM] * 2,
        compiler_params=PARAMS,
        cost_estimate=pl.CostEstimate(flops=1, bytes_accessed=1, transcendentals=0),
    )(mine, *rests, *edges, local)

    half = n_row * n_col // 2
    out_rows = whole // n_col
    keep, give = pl.pallas_call(
        functools.partial(outer_kernel, n_row, plan, sizes),
        out_shape=[jax.ShapeDtypeStruct((half, out_rows, rows), F32)] * 2,
        in_specs=[VMEM] * (2 * n_row + 5),
        out_specs=[VMEM] * 2,
        scratch_shapes=[pltpu.VMEM((wide, wide), BF16), pltpu.VMEM((n_row, whole, rows), F32)],
        compiler_params=PARAMS,
        cost_estimate=pl.CostEstimate(flops=1, bytes_accessed=1, transcendentals=0),
    )(mine, *rests, *halos, back, edge, partner, total, open_part)

    got = move(give, sizes, lambda i, j, k: (i ^ 1, j, k))
    pieces = keep + got
    total = jnp.where(core == 0, pieces[half - 1], 0.0)
    for n, (zero, one) in enumerate(zip(*plan)):
        def target(i, j, k):
            dr, dc = one if i % 2 else zero
            return None if (dr, dc) == (0, 0) else (i, j ^ dr, k ^ dc)

        total = total + move(pieces[n], sizes, target)
    result = total
    for d in range(2, n_ri, 2):
        result = result + move(total, sizes, lambda i, j, k, d=d: (i ^ d, j, k))
    return result + move(result, sizes, lambda i, j, k: (i ^ 1, j, k))


def solution(mesh):
    sizes = tuple(mesh.shape[axis] for axis in AXES)
    placed = (P("ri", "row", "col"), P("col", None, None), P("col", None))
    return jax.shard_map(
        functools.partial(per_device, sizes), mesh=mesh, in_specs=placed, out_specs=P("col", "row"), check_vma=False
    )
```

time: 46.2 us -> 41.2 us (0.89)
  waiting for transfers between devices: 22.5 us -> 19.4 us
  between operations: 2.02 us -> 0.09 us
  local copies, waits for them, and re-layouts: 2.08 us -> 1.28 us
  Pallas kernels: 2.37 us -> 2.91 us
    ppermute x11 -> x13, waiting for transfers between devices: 22.5 us -> 19.4 us  [move(): return lax.ppermute(value, AXES, pairs)]
    squeeze x1 -> x0, local copies, waits for them, and re-layouts: 1.33 us -> none  [per_device(): lax.dynamic_index_in_dim(chunks, row ^ d, 0, keepdims=False)]
    dynamic_slice x0 -> x2, local copies, waits for them, and re-layouts: none -> 1.26 us  [pick(): lax.dynamic_slice(three_centre, (index * chunk, 0, lo), (chunk, rows, hi...]
    slice x5 -> x0, local copies, waits for them, and re-layouts: 0.72 us -> none  [the longest x1 0.66 us: per_device(): band_mask[cols // orb - centre + j, c] != 0]
    add x0 -> x1, other arithmetic: none -> 0.62 us  [per_device(): return result + move(result, sizes, lambda i, j, k: (i ^ 1, j, k))]
    add x1, other arithmetic: 0.62 us -> 0.01 us  [per_device(): result = result + move(total, sizes, lambda i, j, k, d=d: (i ^ d, j, k))]
    pallas_call x1 -> x3, Pallas kernels: 2.37 us -> 2.91 us  [the longest x1 1.09 us: per_device(): pl.pallas_call(functools.partial(inner_kernel, n_row, wide), out_shape=[j...]
    ppermute x11 -> x13, starting transfers between devices: 16.5 us -> 16.7 us  [move(): return lax.ppermute(value, AXES, pairs)]
  transfers between devices with their start and end apart: 11 -> 13, of which waited for: 6 -> 8; matrix products, arithmetic and copies ran while one was open for 2% -> 0% of each run, Pallas kernels for 0% -> 5%
where the time goes in v2:
time: 41.2 us; the launch traced here: 41.1 us
  waiting for transfers between devices  19.4 us (47%)
  starting transfers between devices  16.7 us (41%)
  Pallas kernels  2.91 us (7%)
  local copies, waits for them, and re-layouts  1.28 us (3%)
  other arithmetic  0.65 us (2%)
    ppermute x13, waiting for transfers between devices, move(): return lax.ppermute(value, AXES, pairs)  19.4 us
    ppermute x13, starting transfers between devices, move(): return lax.ppermute(value, AXES, pairs)  16.7 us
    dynamic_slice x2, local copies, waits for them, and re-layouts, pick(): lax.dynamic_slice(three_centre, (index * chunk, 0, lo), (chunk, rows, hi...  1.26 us
    pallas_call x1, Pallas kernels, per_device(): pl.pallas_call(functools.partial(inner_kernel, n_row, wide), out_shape=[j...  1.09 us
    pallas_call x1, Pallas kernels, per_device(): pl.pallas_call(functools.partial(outer_kernel, n_row, plan, sizes), out_s...  1.06 us
  transfers between devices with their start and end apart: 13, of which 8 were waited for; matrix products, arithmetic and copies ran while one was open for 0% of the time, Pallas kernels for 5%

profile of v2, /device:TPU:0, one launch (start us, length us, event | category | flops | bytes accessed | tf_op | source)
XLA Modules:
  0.0 41.1 jit_solution(8588175778522749135)
XLA Ops:
  0.0 1.2 %constant_dynamic-slice_fusion = (bf16[4,128,256]{2,1,0:T(8,128)(2,1)S(1)}, bf16[4,128,256]{2,1,0:T(8,128)(2,1)S(1)}, bf16[4,128,256]{2,1,0:T(8,128)(2,1)S(1)}) fusion(bf16[8,128,512]{2,1,0:T(8,128)(2,1)} %param.3, s32[]{:T(128)S(6)} %select_n.17, s32[]{:T(128)S(6)} %select_n.18), kind=kLoop, calls=%fused_computation.5 | loop fusion | bytes 1572872 | tf_op jit(solution)/shard_map/dynamic_slice | solution.py:142
  1.2 3.0 %collective-permute-start = (bf16[4,128,256]{2,1,0:T(8,128)(2,1)S(1)}, bf16[4,128,256]{2,1,0:T(8,128)(2,1)S(1)}, u32[]{:S(2)}, u32[]{:S(2)}) collective-permute-start(bf16[4,128,256]{2,1,0:T(8,128)(2,1)S(1)} %get-tuple-element.23), channel_id=1, source_target_pairs={{0,4},{1,5},{2,6},{3,7},{4,0},{5,1},{6,2},{7,3},{8,12},{9,13},{10,... | collective-permute-start | bytes 786440 | tf_op jit(solution)/shard_map/ppermute | solution.py:26
  4.3 1.6 %collective-permute-start.2 = (bf16[4,128,256]{2,1,0:T(8,128)(2,1)S(1)}, bf16[4,128,256]{2,1,0:T(8,128)(2,1)S(1)}, u32[]{:S(2)}, u32[]{:S(2)}) collective-permute-start(bf16[4,128,256]{2,1,0:T(8,128)(2,1)S(1)} %get-tuple-element.21), channel_id=1, source_target_pairs={{0,1},{1,2},{2,3},{3,0},{4,5},{5,6},{6,7},{7,4},{8,9},{9,10},{10,1... | collective-permute-start | bytes 786440 | tf_op jit(solution)/shard_map/ppermute | solution.py:26
  5.8 4.7 %collective-permute-done.refs_2_ = bf16[4,128,256]{2,1,0:T(8,128)(2,1)S(1)} collective-permute-done((bf16[4,128,256]{2,1,0:T(8,128)(2,1)S(1)}, bf16[4,128,256]{2,1,0:T(8,128)(2,1)S(1)}, u32[]{:S(2)}, u32[]{:S(2)}) %collective-permute-start) | collective-permute-done | bytes 262176 | tf_op jit(solution)/shard_map/ppermute | solution.py:26
  10.6 1.7 %collective-permute-start.1 = (bf16[4,128,256]{2,1,0:T(8,128)(2,1)S(1)}, bf16[4,128,256]{2,1,0:T(8,128)(2,1)S(1)}, u32[]{:S(2)}, u32[]{:S(2)}) collective-permute-start(bf16[4,128,256]{2,1,0:T(8,128)(2,1)S(1)} %get-tuple-element.13), channel_id=1, source_target_pairs={{0,4},{1,5},{2,6},{3,7},{4,0},{5,1},{6,2},{7,3},{8,12},{9,13},{10,... | collective-permute-start | bytes 786440 | tf_op jit(solution)/shard_map/ppermute | solution.py:26
  12.3 1.6 %collective-permute-start.3 = (bf16[4,128,256]{2,1,0:T(8,128)(2,1)S(1)}, bf16[4,128,256]{2,1,0:T(8,128)(2,1)S(1)}, u32[]{:S(2)}, u32[]{:S(2)}) collective-permute-start(bf16[4,128,256]{2,1,0:T(8,128)(2,1)S(1)} %collective-permute-done.refs_2_), channel_id=1, source_target_pairs={{0,1},{1,2},{2,3},{3,0},{4,5},{5,6},{6,7},{7,4},{8,9},{9,10},{10,1... | collective-permute-start | bytes 786440 | tf_op jit(solution)/shard_map/ppermute | solution.py:26
  13.9 0.8 %shard_map.37 = (bf16[512,512]{1,0:T(8,128)(2,1)S(1)}, bf16[256,256]{1,0:T(8,128)(2,1)S(1)}, bf16[128,256]{1,0:T(8,128)(2,1)S(1)}) custom-call(s32[4,5]{1,0:T(4,128)S(1)} %copy-done.1, bf16[5,512,128]{2,1,0:T(8,128)(2,1)S(1)} %bitcast.11), custom_call_target="tpu_custom_call" | custom-call | flops 10000000000 | bytes 1 | tf_op jit(solution)/shard_map/pallas_call | solution.py:149
  14.7 1.6 %collective-permute-start.4 = (bf16[128,256]{1,0:T(8,128)(2,1)S(1)}, bf16[128,256]{1,0:T(8,128)(2,1)S(1)}, u32[]{:S(2)}, u32[]{:S(2)}) collective-permute-start(bf16[128,256]{1,0:T(8,128)(2,1)S(1)} %get-tuple-element.15), channel_id=1, source_target_pairs={{0,1},{1,2},{2,3},{3,0},{4,5},{5,6},{6,7},{7,4},{8,9},{9,10},{10,1... | collective-permute-start | bytes 196616 | tf_op jit(solution)/shard_map/ppermute | solution.py:26
  16.3 6.2 %collective-permute-done.4.refs_5_ = bf16[128,256]{1,0:T(8,128)(2,1)S(1)} collective-permute-done((bf16[128,256]{1,0:T(8,128)(2,1)S(1)}, bf16[128,256]{1,0:T(8,128)(2,1)S(1)}, u32[]{:S(2)}, u32[]{:S(2)}) %collective-permute-start.4) | collective-permute-done | bytes 65568 | tf_op jit(solution)/shard_map/ppermute | solution.py:26
  22.5 1.1 %shard_map.38 = (f32[256,256]{1,0:T(8,128)S(1)}, f32[4,256,256]{2,1,0:T(8,128)S(1)}) custom-call(bf16[4,128,512]{2,1,0:T(8,128)(2,1)S(1)} %constant_dynamic-slice_fusion.3.refs_0_, bf16[4,128,256]{2,1,0:T(8,128)(2,1)S(1)} %collective-permute-done.1.refs_1_, bf16[4,128,256]{2,1,0:T(8,128)(2,1)S(1)} %collective-permute-done.refs_2_, ...), custom_call_target="tpu_custom_call" | custom-call | flops 1 | bytes 1 | tf_op jit(solution)/shard_map/pallas_call | solution.py:172
  23.6 0.1 collective-permute-done.5.refs_6_
  23.7 1.1 %shard_map.39 = (f32[4,64,128]{2,1,0:T(8,128)S(1)}, f32[4,64,128]{2,1,0:T(8,128)S(1)}) custom-call(bf16[4,128,512]{2,1,0:T(8,128)(2,1)S(1)} %constant_dynamic-slice_fusion.3.refs_0_, bf16[4,128,256]{2,1,0:T(8,128)(2,1)S(1)} %collective-permute-done.1.refs_1_, bf16[4,128,256]{2,1,0:T(8,128)(2,1)S(1)} %collective-permute-done.2.refs_2_, ...), custom_call_target="tpu_custom_call" | custom-call | flops 1 | bytes 1 | tf_op jit(solution)/shard_map/pallas_call | solution.py:183
  24.8 0.5 %collective-permute-start.6 = (f32[4,64,128]{2,1,0:T(8,128)S(1)}, f32[4,64,128]{2,1,0:T(8,128)S(1)}, u32[]{:S(2)}, u32[]{:S(2)}) collective-permute-start(f32[4,64,128]{2,1,0:T(8,128)S(1)} %get-tuple-element.20), channel_id=1, source_target_pairs={{0,8},{1,9},{2,10},{3,11},{4,12},{5,13},{6,14},{7,15},{8,0},{9,1},... | collective-permute-start | bytes 393224 | tf_op jit(solution)/shard_map/ppermute | solution.py:26
  25.3 1.0 %collective-permute-done.6 = f32[4,64,128]{2,1,0:T(8,128)S(1)} collective-permute-done((f32[4,64,128]{2,1,0:T(8,128)S(1)}, f32[4,64,128]{2,1,0:T(8,128)S(1)}, u32[]{:S(2)}, u32[]{:S(2)}) %collective-permute-start.6) | collective-permute-done | bytes 131104 | tf_op jit(solution)/shard_map/ppermute | solution.py:26
  26.3 0.7 %collective-permute-start.10 = (f32[64,128]{1,0:T(8,128)S(1)}, f32[64,128]{1,0:T(8,128)S(1)}, u32[]{:S(2)}, u32[]{:S(2)}) collective-permute-start(f32[64,128]{1,0:T(8,128)S(1)} %get-tuple-element.27), channel_id=1, source_target_pairs={{8,15},{9,14},{10,13},{11,12},{12,11},{13,10},{14,9},{15,8},{24,31... | collective-permute-start | bytes 98312 | tf_op jit(solution)/shard_map/ppermute | solution.py:26
  27.0 0.1 collective-permute-start.7
  27.1 2.3 %collective-permute-start.8 = (f32[64,128]{1,0:T(8,128)S(1)}, f32[64,128]{1,0:T(8,128)S(1)}, u32[]{:S(2)}, u32[]{:S(2)}) collective-permute-start(f32[64,128]{1,0:T(8,128)S(1)} %get-tuple-element.26), channel_id=1, source_target_pairs={{0,2},{1,3},{2,0},{3,1},{4,6},{5,7},{6,4},{7,5},{8,13},{9,12},{10,... | collective-permute-start | bytes 98312 | tf_op jit(solution)/shard_map/ppermute | solution.py:26
  29.4 2.1 %collective-permute-start.9 = (f32[64,128]{1,0:T(8,128)S(1)}, f32[64,128]{1,0:T(8,128)S(1)}, u32[]{:S(2)}, u32[]{:S(2)}) collective-permute-start(f32[64,128]{1,0:T(8,128)S(1)} %get-tuple-element.25), channel_id=1, source_target_pairs={{0,3},{1,2},{2,1},{3,0},{4,7},{5,6},{6,5},{7,4},{8,14},{9,15},{10,... | collective-permute-start | bytes 98312 | tf_op jit(solution)/shard_map/ppermute | solution.py:26
  31.5 0.5 %collective-permute-done.8 = f32[64,128]{1,0:T(8,128)S(1)} collective-permute-done((f32[64,128]{1,0:T(8,128)S(1)}, f32[64,128]{1,0:T(8,128)S(1)}, u32[]{:S(2)}, u32[]{:S(2)}) %collective-permute-start.8) | collective-permute-done | bytes 32800 | tf_op jit(solution)/shard_map/ppermute | solution.py:26
  32.0 3.1 %collective-permute-done.9 = f32[64,128]{1,0:T(8,128)S(1)} collective-permute-done((f32[64,128]{1,0:T(8,128)S(1)}, f32[64,128]{1,0:T(8,128)S(1)}, u32[]{:S(2)}, u32[]{:S(2)}) %collective-permute-start.9) | collective-permute-done | bytes 32800 | tf_op jit(solution)/shard_map/ppermute | solution.py:26
  35.1 1.6 %collective-permute-start.11 = (f32[64,128]{1,0:T(8,128)S(1)}, f32[64,128]{1,0:T(8,128)S(1)}, u32[]{:S(2)}, u32[]{:S(2)}) collective-permute-start(f32[64,128]{1,0:T(8,128)S(1)} %add_add_fusion), channel_id=1, source_target_pairs={{0,16},{1,17},{2,18},{3,19},{4,20},{5,21},{6,22},{7,23},{8,24},{9,... | collective-permute-start | bytes 98312 | tf_op jit(solution)/shard_map/ppermute | solution.py:26
  36.7 2.6 %collective-permute-done.11 = f32[64,128]{1,0:T(8,128)S(1)} collective-permute-done((f32[64,128]{1,0:T(8,128)S(1)}, f32[64,128]{1,0:T(8,128)S(1)}, u32[]{:S(2)}, u32[]{:S(2)}) %collective-permute-start.11) | collective-permute-done | bytes 32800 | tf_op jit(solution)/shard_map/ppermute | solution.py:26
  39.3 1.2 %collective-permute-done.12 = f32[64,128]{1,0:T(8,128)S(1)} collective-permute-done((f32[64,128]{1,0:T(8,128)S(1)}, f32[64,128]{1,0:T(8,128)S(1)}, u32[]{:S(2)}, u32[]{:S(2)}) %collective-permute-start.12) | collective-permute-done | bytes 32800 | tf_op jit(solution)/shard_map/ppermute | solution.py:26
  40.5 0.6 %add.37 = f32[64,128]{1,0:T(8,128)} add(f32[64,128]{1,0:T(8,128)S(1)} %add.36, f32[64,128]{1,0:T(8,128)S(1)} %collective-permute-done.12) | non-fusion elementwise | flops 8192 | bytes 98304 | tf_op jit(solution)/shard_map/add | solution.py:205
  (18 shorter events, 0.1 us)
Async XLA Ops:
  0.0 13.9 %copy-start = (bf16[512,5,128]{2,0,1:T(8,128)(2,1)S(1)}, bf16[512,5,128]{2,0,1:T(8,128)(2,1)}, u32[]{:S(2)}) copy-start(bf16[512,5,128]{2,0,1:T(8,128)(2,1)} %param.4) | copy-start | bytes 1966084
  1.2 9.3 %collective-permute-start = (bf16[4,128,256]{2,1,0:T(8,128)(2,1)S(1)}, bf16[4,128,256]{2,1,0:T(8,128)(2,1)S(1)}, u32[]{:S(2)}, u32[]{:S(2)}) collective-permute-start(bf16[4,128,256]{2,1,0:T(8,128)(2,1)S(1)} %get-tuple-element.23), channel_id=1, source_target_pairs={{0,4},{1,5},{2,6},{3,7},{4,0},{5,1},{6,2},{7,3},{8,12},{9,13},{10,... | collective-permute-start | bytes 786440 | tf_op jit(solution)/shard_map/ppermute | solution.py:26
  4.3 9.6 %copy-start.1 = (s32[4,5]{1,0:T(4,128)S(1)}, s32[4,5]{1,0:T(4,128)}, u32[]{:S(2)}) copy-start(s32[4,5]{1,0:T(4,128)} %mask_ref.1) | copy-start | bytes 244
  4.3 19.5 %collective-permute-start.2 = (bf16[4,128,256]{2,1,0:T(8,128)(2,1)S(1)}, bf16[4,128,256]{2,1,0:T(8,128)(2,1)S(1)}, u32[]{:S(2)}, u32[]{:S(2)}) collective-permute-start(bf16[4,128,256]{2,1,0:T(8,128)(2,1)S(1)} %get-tuple-element.21), channel_id=1, source_target_pairs={{0,1},{1,2},{2,3},{3,0},{4,5},{5,6},{6,7},{7,4},{8,9},{9,10},{10,1... | collective-permute-start | bytes 786440 | tf_op jit(solution)/shard_map/ppermute | solution.py:26
  10.6 11.9 %collective-permute-start.1 = (bf16[4,128,256]{2,1,0:T(8,128)(2,1)S(1)}, bf16[4,128,256]{2,1,0:T(8,128)(2,1)S(1)}, u32[]{:S(2)}, u32[]{:S(2)}) collective-permute-start(bf16[4,128,256]{2,1,0:T(8,128)(2,1)S(1)} %get-tuple-element.13), channel_id=1, source_target_pairs={{0,4},{1,5},{2,6},{3,7},{4,0},{5,1},{6,2},{7,3},{8,12},{9,13},{10,... | collective-permute-start | bytes 786440 | tf_op jit(solution)/shard_map/ppermute | solution.py:26
  12.3 11.4 %collective-permute-start.3 = (bf16[4,128,256]{2,1,0:T(8,128)(2,1)S(1)}, bf16[4,128,256]{2,1,0:T(8,128)(2,1)S(1)}, u32[]{:S(2)}, u32[]{:S(2)}) collective-permute-start(bf16[4,128,256]{2,1,0:T(8,128)(2,1)S(1)} %collective-permute-done.refs_2_), channel_id=1, source_target_pairs={{0,1},{1,2},{2,3},{3,0},{4,5},{5,6},{6,7},{7,4},{8,9},{9,10},{10,1... | collective-permute-start | bytes 786440 | tf_op jit(solution)/shard_map/ppermute | solution.py:26
  13.9 8.6 %copy-start.2 = (bf16[8,128,512]{2,1,0:T(8,128)(2,1)S(1)}, bf16[8,128,512]{2,1,0:T(8,128)(2,1)}, u32[]{:S(2)}) copy-start(bf16[8,128,512]{2,1,0:T(8,128)(2,1)} %param.3) | copy-start | bytes 3145732
  14.7 7.8 %collective-permute-start.4 = (bf16[128,256]{1,0:T(8,128)(2,1)S(1)}, bf16[128,256]{1,0:T(8,128)(2,1)S(1)}, u32[]{:S(2)}, u32[]{:S(2)}) collective-permute-start(bf16[128,256]{1,0:T(8,128)(2,1)S(1)} %get-tuple-element.15), channel_id=1, source_target_pairs={{0,1},{1,2},{2,3},{3,0},{4,5},{5,6},{6,7},{7,4},{8,9},{9,10},{10,1... | collective-permute-start | bytes 196616 | tf_op jit(solution)/shard_map/ppermute | solution.py:26
  22.5 1.3 %collective-permute-start.5 = (bf16[128,256]{1,0:T(8,128)(2,1)S(1)}, bf16[128,256]{1,0:T(8,128)(2,1)S(1)}, u32[]{:S(2)}, u32[]{:S(2)}) collective-permute-start(bf16[128,256]{1,0:T(8,128)(2,1)S(1)} %collective-permute-done.4.refs_5_), channel_id=1, source_target_pairs={{0,8},{1,9},{2,10},{3,11},{4,12},{5,13},{6,14},{7,15},{8,0},{9,1},... | collective-permute-start | bytes 196616 | tf_op jit(solution)/shard_map/ppermute | solution.py:26
  24.8 1.5 %collective-permute-start.6 = (f32[4,64,128]{2,1,0:T(8,128)S(1)}, f32[4,64,128]{2,1,0:T(8,128)S(1)}, u32[]{:S(2)}, u32[]{:S(2)}) collective-permute-start(f32[4,64,128]{2,1,0:T(8,128)S(1)} %get-tuple-element.20), channel_id=1, source_target_pairs={{0,8},{1,9},{2,10},{3,11},{4,12},{5,13},{6,14},{7,15},{8,0},{9,1},... | collective-permute-start | bytes 393224 | tf_op jit(solution)/shard_map/ppermute | solution.py:26
  26.3 5.1 %collective-permute-start.10 = (f32[64,128]{1,0:T(8,128)S(1)}, f32[64,128]{1,0:T(8,128)S(1)}, u32[]{:S(2)}, u32[]{:S(2)}) collective-permute-start(f32[64,128]{1,0:T(8,128)S(1)} %get-tuple-element.27), channel_id=1, source_target_pairs={{8,15},{9,14},{10,13},{11,12},{12,11},{13,10},{14,9},{15,8},{24,31... | collective-permute-start | bytes 98312 | tf_op jit(solution)/shard_map/ppermute | solution.py:26
  27.0 4.5 %collective-permute-start.7 = (f32[64,128]{1,0:T(8,128)S(1)}, f32[64,128]{1,0:T(8,128)S(1)}, u32[]{:S(2)}, u32[]{:S(2)}) collective-permute-start(f32[64,128]{1,0:T(8,128)S(1)} %get-tuple-element.24), channel_id=1, source_target_pairs={{0,1},{1,0},{2,3},{3,2},{4,5},{5,4},{6,7},{7,6},{8,12},{9,13},{10,... | collective-permute-start | bytes 98312 | tf_op jit(solution)/shard_map/ppermute | solution.py:26
  27.1 4.9 %collective-permute-start.8 = (f32[64,128]{1,0:T(8,128)S(1)}, f32[64,128]{1,0:T(8,128)S(1)}, u32[]{:S(2)}, u32[]{:S(2)}) collective-permute-start(f32[64,128]{1,0:T(8,128)S(1)} %get-tuple-element.26), channel_id=1, source_target_pairs={{0,2},{1,3},{2,0},{3,1},{4,6},{5,7},{6,4},{7,5},{8,13},{9,12},{10,... | collective-permute-start | bytes 98312 | tf_op jit(solution)/shard_map/ppermute | solution.py:26
  29.4 5.7 %collective-permute-start.9 = (f32[64,128]{1,0:T(8,128)S(1)}, f32[64,128]{1,0:T(8,128)S(1)}, u32[]{:S(2)}, u32[]{:S(2)}) collective-permute-start(f32[64,128]{1,0:T(8,128)S(1)} %get-tuple-element.25), channel_id=1, source_target_pairs={{0,3},{1,2},{2,1},{3,0},{4,7},{5,6},{6,5},{7,4},{8,14},{9,15},{10,... | collective-permute-start | bytes 98312 | tf_op jit(solution)/shard_map/ppermute | solution.py:26
  35.1 4.2 %collective-permute-start.11 = (f32[64,128]{1,0:T(8,128)S(1)}, f32[64,128]{1,0:T(8,128)S(1)}, u32[]{:S(2)}, u32[]{:S(2)}) collective-permute-start(f32[64,128]{1,0:T(8,128)S(1)} %add_add_fusion), channel_id=1, source_target_pairs={{0,16},{1,17},{2,18},{3,19},{4,20},{5,21},{6,22},{7,23},{8,24},{9,... | collective-permute-start | bytes 98312 | tf_op jit(solution)/shard_map/ppermute | solution.py:26
  39.3 1.2 %collective-permute-start.12 = (f32[64,128]{1,0:T(8,128)S(1)}, f32[64,128]{1,0:T(8,128)S(1)}, u32[]{:S(2)}, u32[]{:S(2)}) collective-permute-start(f32[64,128]{1,0:T(8,128)S(1)} %add.36), channel_id=1, source_target_pairs={{0,8},{1,9},{2,10},{3,11},{4,12},{5,13},{6,14},{7,15},{8,0},{9,1},... | collective-permute-start | bytes 98312 | tf_op jit(solution)/shard_map/ppermute | solution.py:26

commit v3 on v2

--- a/solution.py
+++ b/solution.py
@@ -45,27 +45,44 @@
     return lax.dot_general(a, b, (((1,), (1,)), ((), ())), preferred_element_type=F32)
 
 
-def density_kernel(centre, mask_ref, dens_ref, local_ref, back_ref, edge_ref, whole_ref):
+def masked(mask_ref, dens_ref, l, c):
+    orb = dens_ref.shape[2]
+    block = dens_ref[c, l * orb : (l + 1) * orb, :]
+    return jnp.where(mask_ref[l, c] != 0, block, jnp.zeros_like(block))
+
+
+def beyond(centre):
+    return [(l, s) for l in range(centre) for s in range(l + 1)]
+
+
+def pack_kernel(centre, mask_ref, dens_ref, last_ref, out_ref):
+    band_count, cols, orb = dens_ref.shape
+    blocks = cols // orb
+    chunk, rows, unused = last_ref.shape
+    for p in range(chunk):
+        for j in range(centre):
+            at = (p * centre + j) * rows
+            out_ref[at : at + rows, :] = last_ref[p, :, j * orb : (j + 1) * orb]
+    at = chunk * centre * rows
+    for l, s in beyond(centre):
+        out_ref[at : at + orb, :] = masked(mask_ref, dens_ref, blocks - centre + l, s - l + 2 * centre)
+        at += orb
+
+
+def band_kernel(centre, mask_ref, dens_ref, local_ref, back_ref):
     band_count, cols, orb = dens_ref.shape
     blocks = cols // orb
     local_ref[...] = jnp.zeros_like(local_ref)
     back_ref[...] = jnp.zeros_like(back_ref)
-    whole_ref[...] = jnp.zeros_like(whole_ref)
     for l in range(blocks):
         for c in range(band_count):
-            block = dens_ref[c, l * orb : (l + 1) * orb, :]
-            block = jnp.where(mask_ref[l, c] != 0, block, jnp.zeros_like(block))
             s = l + c - centre
             if s < 0:
-                back_ref[l * orb : (l + 1) * orb, (s + centre) * orb : (s + centre + 1) * orb] = block
+                back_ref[l * orb : (l + 1) * orb, (s + centre) * orb : (s + centre + 1) * orb] = masked(
+                    mask_ref, dens_ref, l, c
+                )
             elif s < blocks:
-                local_ref[l * orb : (l + 1) * orb, s * orb : (s + 1) * orb] = block
-            else:
-                first = l - blocks + centre
-                whole_ref[first * orb : (first + 1) * orb, (s - blocks) * orb : (s - blocks + 1) * orb] = block
-    half = edge_ref.shape[0]
-    core = lax.rem(lax.axis_index("ri"), 2)
-    edge_ref[...] = whole_ref[pl.ds(pl.multiple_of(core * half, half), half), :]
+                local_ref[l * orb : (l + 1) * orb, s * orb : (s + 1) * orb] = masked(mask_ref, dens_ref, l, c)
 
 
 def inner_kernel(count, wide, *refs):
@@ -90,22 +107,29 @@
     total_ref[...] = total
 
 
-def outer_kernel(count, plan, sizes, *refs):
+def outer_kernel(count, centre, plan, sizes, *refs):
     own_ref = refs[0]
     rests = refs[1:count]
-    halos = refs[count : 2 * count]
-    back_ref, mine_ref, partner_ref, inner_ref, open_ref, keep_ref, give_ref, edge_ref, kx_ref = refs[2 * count :]
-    chunk, rows, wide = halos[0].shape
-    half = mine_ref.shape[0]
+    packed_ref = refs[count]
+    halos = refs[count + 1 : 2 * count]
+    back_ref, inner_ref, open_ref, keep_ref, give_ref, edge_ref, kx_ref = refs[2 * count :]
+    chunk, rows, unused = own_ref.shape
+    orb = packed_ref.shape[1]
+    wide = centre * orb
     core = lax.rem(lax.axis_index("ri"), 2)
     row = lax.axis_index("row")
     col = lax.axis_index("col")
-    edge_ref[pl.ds(pl.multiple_of(core * half, half), half), :] = mine_ref[...]
-    edge_ref[pl.ds(pl.multiple_of((1 - core) * half, half), half), :] = partner_ref[...]
+    edge_ref[...] = jnp.zeros_like(edge_ref)
+    at = chunk * centre * rows
+    for l, s in beyond(centre):
+        edge_ref[l * orb : (l + 1) * orb, s * orb : (s + 1) * orb] = packed_ref[at : at + orb, :]
+        at += orb
     total = inner_ref[...]
     for p in range(chunk):
         near = jnp.concatenate([own_ref[p, :, :wide]] + [ref[p, :, :wide] for ref in rests], axis=0)
-        halo = jnp.concatenate([ref[p] for ref in halos], axis=0)
+        starts = [(p * centre + j) * rows for j in range(centre)]
+        first = jnp.concatenate([packed_ref[at : at + rows, :] for at in starts], axis=1)
+        halo = jnp.concatenate([first] + [ref[p] for ref in halos], axis=0)
         mixed = (open_ref[p] + times(halo, edge_ref[...])).astype(BF16)
         behind = times(near, back_ref[...]).astype(BF16)
         total = total + times_turned(
@@ -142,31 +166,31 @@
         cut = lax.dynamic_slice(three_centre, (index * chunk, 0, lo), (chunk, rows, hi - lo))
         return cut
 
+    density = jnp.transpose(density_band, (1, 0, 2))
     edges = [move(pick(row ^ d, last, cols), sizes, lambda i, j, k, d=d: (i, j ^ d, k)) for d in range(1, n_row)]
-    halos = [move(pick(row, last, cols), sizes, forward)]
+    packed = pl.pallas_call(
+        functools.partial(pack_kernel, centre),
+        out_shape=jax.ShapeDtypeStruct((chunk * centre * rows + len(beyond(centre)) * orb, orb), BF16),
+        in_specs=[SMEM, VMEM, VMEM],
+        out_specs=VMEM,
+        compiler_params=PARAMS,
+        cost_estimate=pl.CostEstimate(flops=1, bytes_accessed=1, transcendentals=0),
+    )(band_mask, density, pick(row, last, cols))
+    packed = move(packed, sizes, forward)
+    local, back = pl.pallas_call(
+        functools.partial(band_kernel, centre),
+        out_shape=[jax.ShapeDtypeStruct((cols, cols), BF16), jax.ShapeDtypeStruct((wide, wide), BF16)],
+        in_specs=[SMEM, VMEM],
+        out_specs=[VMEM] * 2,
+        compiler_params=PARAMS,
+        cost_estimate=pl.CostEstimate(flops=1, bytes_accessed=1, transcendentals=0),
+    )(band_mask, density)
     mine = pick(row, 0, cols)
-
-    local, back, edge = pl.pallas_call(
-        functools.partial(density_kernel, centre),
-        out_shape=[
-            jax.ShapeDtypeStruct((cols, cols), BF16),
-            jax.ShapeDtypeStruct((wide, wide), BF16),
-            jax.ShapeDtypeStruct((wide // 2, wide), BF16),
-        ],
-        in_specs=[SMEM, VMEM],
-        out_specs=[VMEM] * 3,
-        scratch_shapes=[pltpu.VMEM((wide, wide), BF16)],
-        compiler_params=PARAMS,
-        cost_estimate=pl.CostEstimate(flops=10**10, bytes_accessed=1, transcendentals=0),
-    )(band_mask, jnp.transpose(density_band, (1, 0, 2)))
-    edge = move(edge, sizes, forward)
-    partner = move(edge, sizes, lambda i, j, k: (i ^ 1, j, k))
-
+    halos = [move(part, sizes, forward) for part in edges]
     rests = [
         move(after(pick(row ^ d, 0, last), edges[d - 1]), sizes, lambda i, j, k, d=d: (i, j ^ d, k))
         for d in range(1, n_row)
     ]
-    halos += [move(part, sizes, forward) for part in edges]
 
     whole = n_row * rows
     total, open_part = pl.pallas_call(
@@ -181,14 +205,14 @@
     half = n_row * n_col // 2
     out_rows = whole // n_col
     keep, give = pl.pallas_call(
-        functools.partial(outer_kernel, n_row, plan, sizes),
+        functools.partial(outer_kernel, n_row, centre, plan, sizes),
         out_shape=[jax.ShapeDtypeStruct((half, out_rows, rows), F32)] * 2,
-        in_specs=[VMEM] * (2 * n_row + 5),
+        in_specs=[VMEM] * (2 * n_row + 3),
         out_specs=[VMEM] * 2,
         scratch_shapes=[pltpu.VMEM((wide, wide), BF16), pltpu.VMEM((n_row, whole, rows), F32)],
         compiler_params=PARAMS,
         cost_estimate=pl.CostEstimate(flops=1, bytes_accessed=1, transcendentals=0),
-    )(mine, *rests, *halos, back, edge, partner, total, open_part)
+    )(mine, *rests, packed, *halos, back, total, open_part)
 
     got = move(give, sizes, lambda i, j, k: (i ^ 1, j, k))
     pieces = keep + got

time: 41.2 us -> 40.1 us (0.973)
  waiting for transfers between devices: 19.4 us -> 18.1 us
  Pallas kernels: 2.91 us -> 3.48 us
    ppermute x13 -> x11, waiting for transfers between devices: 19.4 us -> 18.1 us  [move(): return lax.ppermute(value, AXES, pairs)]
    pallas_call x2 -> x3, Pallas kernels: 1.81 us -> 2.38 us  [the longest x1 1.04 us: per_device(): pl.pallas_call(functools.partial(outer_kernel, n_row, centre, plan, sizes...]
    ppermute x13 -> x11, starting transfers between devices: 16.7 us -> 16.3 us  [move(): return lax.ppermute(value, AXES, pairs)]
  transfers between devices with their start and end apart: 13 -> 11, of which waited for: 8 -> 7; matrix products, arithmetic and copies ran while one was open for 0% -> 0% of each run, Pallas kernels for 5% -> 6%
where the time goes in v3:
time: 40.1 us; the launch traced here: 40 us
  waiting for transfers between devices  18.1 us (45%)
  starting transfers between devices  16.3 us (41%)
  Pallas kernels  3.48 us (9%)
  local copies, waits for them, and re-layouts  1.3 us (3%)
  other arithmetic  0.65 us (2%)
    ppermute x11, waiting for transfers between devices, move(): return lax.ppermute(value, AXES, pairs)  18.1 us
    ppermute x11, starting transfers between devices, move(): return lax.ppermute(value, AXES, pairs)  16.3 us
    dynamic_slice x2, local copies, waits for them, and re-layouts, pick(): lax.dynamic_slice(three_centre, (index * chunk, 0, lo), (chunk, rows, hi...  1.27 us
    pallas_call x1, Pallas kernels, per_device(): pl.pallas_call(functools.partial(inner_kernel, n_row, wide), out_shape=[j...  1.1 us
    pallas_call x1, Pallas kernels, per_device(): pl.pallas_call(functools.partial(outer_kernel, n_row, centre, plan, sizes...  1.04 us
  transfers between devices with their start and end apart: 11, of which 7 were waited for; matrix products, arithmetic and copies ran while one was open for 0% of the time, Pallas kernels for 6%

profile of v3, /device:TPU:0, one launch (start us, length us, event | category | flops | bytes accessed | tf_op | source)
XLA Modules:
  0.0 40.0 jit_solution(8690515924937509250)
XLA Ops:
  0.0 1.2 %constant_dynamic-slice_fusion = (bf16[4,128,256]{2,1,0:T(8,128)(2,1)S(1)}, bf16[4,128,256]{2,1,0:T(8,128)(2,1)S(1)}, bf16[4,128,256]{2,1,0:T(8,128)(2,1)S(1)}) fusion(bf16[8,128,512]{2,1,0:T(8,128)(2,1)} %param.3, s32[]{:T(128)S(6)} %select_n.17, s32[]{:T(128)S(6)} %select_n.18), kind=kLoop, calls=%fused_computation.5 | loop fusion | bytes 1572872 | tf_op jit(solution)/shard_map/dynamic_slice | solution.py:166
  1.3 3.0 %collective-permute-start = (bf16[4,128,256]{2,1,0:T(8,128)(2,1)S(1)}, bf16[4,128,256]{2,1,0:T(8,128)(2,1)S(1)}, u32[]{:S(2)}, u32[]{:S(2)}) collective-permute-start(bf16[4,128,256]{2,1,0:T(8,128)(2,1)S(1)} %get-tuple-element.21), channel_id=1, source_target_pairs={{0,4},{1,5},{2,6},{3,7},{4,0},{5,1},{6,2},{7,3},{8,12},{9,13},{10,... | collective-permute-start | bytes 786440 | tf_op jit(solution)/shard_map/ppermute | solution.py:26
  4.3 0.6 %shard_map.37 = bf16[1408,128]{1,0:T(8,128)(2,1)S(1)} custom-call(s32[4,5]{1,0:T(4,128)S(1)} %copy-done.1, bf16[5,512,128]{2,1,0:T(8,128)(2,1)S(1)} %bitcast.11, bf16[4,128,256]{2,1,0:T(8,128)(2,1)S(1)} %get-tuple-element.19.last_ref), custom_call_target="tpu_custom_call" | custom-call | flops 1 | bytes 1 | tf_op jit(solution)/shard_map/pallas_call | solution.py:171
  4.9 1.6 %collective-permute-start.2 = (bf16[1408,128]{1,0:T(8,128)(2,1)S(1)}, bf16[1408,128]{1,0:T(8,128)(2,1)S(1)}, u32[]{:S(2)}, u32[]{:S(2)}) collective-permute-start(bf16[1408,128]{1,0:T(8,128)(2,1)S(1)} %shard_map.37), channel_id=1, source_target_pairs={{0,1},{1,2},{2,3},{3,0},{4,5},{5,6},{6,7},{7,4},{8,9},{9,10},{10,1... | collective-permute-start | bytes 1081352 | tf_op jit(solution)/shard_map/ppermute | solution.py:26
  6.6 4.0 %collective-permute-done.refs_2_ = bf16[4,128,256]{2,1,0:T(8,128)(2,1)S(1)} collective-permute-done((bf16[4,128,256]{2,1,0:T(8,128)(2,1)S(1)}, bf16[4,128,256]{2,1,0:T(8,128)(2,1)S(1)}, u32[]{:S(2)}, u32[]{:S(2)}) %collective-permute-start) | collective-permute-done | bytes 262176 | tf_op jit(solution)/shard_map/ppermute | solution.py:26
  10.6 1.7 %collective-permute-start.1 = (bf16[4,128,256]{2,1,0:T(8,128)(2,1)S(1)}, bf16[4,128,256]{2,1,0:T(8,128)(2,1)S(1)}, u32[]{:S(2)}, u32[]{:S(2)}) collective-permute-start(bf16[4,128,256]{2,1,0:T(8,128)(2,1)S(1)} %get-tuple-element.12), channel_id=1, source_target_pairs={{0,4},{1,5},{2,6},{3,7},{4,0},{5,1},{6,2},{7,3},{8,12},{9,13},{10,... | collective-permute-start | bytes 786440 | tf_op jit(solution)/shard_map/ppermute | solution.py:26
  12.3 1.6 %collective-permute-start.3 = (bf16[4,128,256]{2,1,0:T(8,128)(2,1)S(1)}, bf16[4,128,256]{2,1,0:T(8,128)(2,1)S(1)}, u32[]{:S(2)}, u32[]{:S(2)}) collective-permute-start(bf16[4,128,256]{2,1,0:T(8,128)(2,1)S(1)} %collective-permute-done.refs_2_), channel_id=1, source_target_pairs={{0,1},{1,2},{2,3},{3,0},{4,5},{5,6},{6,7},{7,4},{8,9},{9,10},{10,1... | collective-permute-start | bytes 786440 | tf_op jit(solution)/shard_map/ppermute | solution.py:26
  13.9 0.7 %shard_map.38 = (bf16[512,512]{1,0:T(8,128)(2,1)S(1)}, bf16[256,256]{1,0:T(8,128)(2,1)S(1)}) custom-call(s32[4,5]{1,0:T(4,128)S(1)} %copy-done.1, bf16[5,512,128]{2,1,0:T(8,128)(2,1)S(1)} %bitcast.12), custom_call_target="tpu_custom_call" | custom-call | flops 1 | bytes 1 | tf_op jit(solution)/shard_map/pallas_call | solution.py:180
  14.7 3.4 %collective-permute-done.1.refs_1_ = bf16[4,128,256]{2,1,0:T(8,128)(2,1)S(1)} collective-permute-done((bf16[4,128,256]{2,1,0:T(8,128)(2,1)S(1)}, bf16[4,128,256]{2,1,0:T(8,128)(2,1)S(1)}, u32[]{:S(2)}, u32[]{:S(2)}) %collective-permute-start.1) | collective-permute-done | bytes 262176 | tf_op jit(solution)/shard_map/ppermute | solution.py:26
  18.1 1.1 %shard_map.39 = (f32[256,256]{1,0:T(8,128)S(1)}, f32[4,256,256]{2,1,0:T(8,128)S(1)}) custom-call(bf16[4,128,512]{2,1,0:T(8,128)(2,1)S(1)} %constant_dynamic-slice_fusion.3.refs_0_, bf16[4,128,256]{2,1,0:T(8,128)(2,1)S(1)} %collective-permute-done.1.refs_1_, bf16[4,128,256]{2,1,0:T(8,128)(2,1)S(1)} %collective-permute-done.refs_2_, ...), custom_call_target="tpu_custom_call" | custom-call | flops 1 | bytes 1 | tf_op jit(solution)/shard_map/pallas_call | solution.py:196
  19.2 3.1 %collective-permute-done.3.refs_3_ = bf16[4,128,256]{2,1,0:T(8,128)(2,1)S(1)} collective-permute-done((bf16[4,128,256]{2,1,0:T(8,128)(2,1)S(1)}, bf16[4,128,256]{2,1,0:T(8,128)(2,1)S(1)}, u32[]{:S(2)}, u32[]{:S(2)}) %collective-permute-start.3) | collective-permute-done | bytes 262176 | tf_op jit(solution)/shard_map/ppermute | solution.py:26
  22.3 1.0 %shard_map.40 = (f32[4,64,128]{2,1,0:T(8,128)S(1)}, f32[4,64,128]{2,1,0:T(8,128)S(1)}) custom-call(bf16[4,128,512]{2,1,0:T(8,128)(2,1)S(1)} %constant_dynamic-slice_fusion.3.refs_0_, bf16[4,128,256]{2,1,0:T(8,128)(2,1)S(1)} %collective-permute-done.1.refs_1_, bf16[1408,128]{1,0:T(8,128)(2,1)S(1)} %collective-permute-done.2.refs_2_, ...), custom_call_target="tpu_custom_call" | custom-call | flops 1 | bytes 1 | tf_op jit(solution)/shard_map/pallas_call | solution.py:207
  23.4 0.1 collective-permute-start.4
  23.5 1.3 %collective-permute-done.4 = f32[4,64,128]{2,1,0:T(8,128)S(1)} collective-permute-done((f32[4,64,128]{2,1,0:T(8,128)S(1)}, f32[4,64,128]{2,1,0:T(8,128)S(1)}, u32[]{:S(2)}, u32[]{:S(2)}) %collective-permute-start.4) | collective-permute-done | bytes 131104 | tf_op jit(solution)/shard_map/ppermute | solution.py:26
  24.8 0.1 collective-permute-start.5
  24.9 2.3 %collective-permute-start.6 = (f32[64,128]{1,0:T(8,128)S(1)}, f32[64,128]{1,0:T(8,128)S(1)}, u32[]{:S(2)}, u32[]{:S(2)}) collective-permute-start(f32[64,128]{1,0:T(8,128)S(1)} %get-tuple-element.24), channel_id=1, source_target_pairs={{0,2},{1,3},{2,0},{3,1},{4,6},{5,7},{6,4},{7,5},{8,13},{9,12},{10,... | collective-permute-start | bytes 98312 | tf_op jit(solution)/shard_map/ppermute | solution.py:26
  27.2 2.1 %collective-permute-start.7 = (f32[64,128]{1,0:T(8,128)S(1)}, f32[64,128]{1,0:T(8,128)S(1)}, u32[]{:S(2)}, u32[]{:S(2)}) collective-permute-start(f32[64,128]{1,0:T(8,128)S(1)} %get-tuple-element.23), channel_id=1, source_target_pairs={{0,3},{1,2},{2,1},{3,0},{4,7},{5,6},{6,5},{7,4},{8,14},{9,15},{10,... | collective-permute-start | bytes 98312 | tf_op jit(solution)/shard_map/ppermute | solution.py:26
  29.3 0.7 %collective-permute-start.8 = (f32[64,128]{1,0:T(8,128)S(1)}, f32[64,128]{1,0:T(8,128)S(1)}, u32[]{:S(2)}, u32[]{:S(2)}) collective-permute-start(f32[64,128]{1,0:T(8,128)S(1)} %get-tuple-element.25), channel_id=1, source_target_pairs={{8,15},{9,14},{10,13},{11,12},{12,11},{13,10},{14,9},{15,8},{24,31... | collective-permute-start | bytes 98312 | tf_op jit(solution)/shard_map/ppermute | solution.py:26
  30.0 2.9 %collective-permute-done.7 = f32[64,128]{1,0:T(8,128)S(1)} collective-permute-done((f32[64,128]{1,0:T(8,128)S(1)}, f32[64,128]{1,0:T(8,128)S(1)}, u32[]{:S(2)}, u32[]{:S(2)}) %collective-permute-start.7) | collective-permute-done | bytes 32800 | tf_op jit(solution)/shard_map/ppermute | solution.py:26
  32.9 1.6 %collective-permute-start.9 = (f32[64,128]{1,0:T(8,128)S(1)}, f32[64,128]{1,0:T(8,128)S(1)}, u32[]{:S(2)}, u32[]{:S(2)}) collective-permute-start(f32[64,128]{1,0:T(8,128)S(1)} %add_add_fusion), channel_id=1, source_target_pairs={{0,16},{1,17},{2,18},{3,19},{4,20},{5,21},{6,22},{7,23},{8,24},{9,... | collective-permute-start | bytes 98312 | tf_op jit(solution)/shard_map/ppermute | solution.py:26
  34.5 2.4 %collective-permute-done.9 = f32[64,128]{1,0:T(8,128)S(1)} collective-permute-done((f32[64,128]{1,0:T(8,128)S(1)}, f32[64,128]{1,0:T(8,128)S(1)}, u32[]{:S(2)}, u32[]{:S(2)}) %collective-permute-start.9) | collective-permute-done | bytes 32800 | tf_op jit(solution)/shard_map/ppermute | solution.py:26
  36.9 1.6 %collective-permute-start.10 = (f32[64,128]{1,0:T(8,128)S(1)}, f32[64,128]{1,0:T(8,128)S(1)}, u32[]{:S(2)}, u32[]{:S(2)}) collective-permute-start(f32[64,128]{1,0:T(8,128)S(1)} %add.36), channel_id=1, source_target_pairs={{0,8},{1,9},{2,10},{3,11},{4,12},{5,13},{6,14},{7,15},{8,0},{9,1},... | collective-permute-start | bytes 98312 | tf_op jit(solution)/shard_map/ppermute | solution.py:26
  38.5 0.9 %collective-permute-done.10 = f32[64,128]{1,0:T(8,128)S(1)} collective-permute-done((f32[64,128]{1,0:T(8,128)S(1)}, f32[64,128]{1,0:T(8,128)S(1)}, u32[]{:S(2)}, u32[]{:S(2)}) %collective-permute-start.10) | collective-permute-done | bytes 32800 | tf_op jit(solution)/shard_map/ppermute | solution.py:26
  39.4 0.6 %add.37 = f32[64,128]{1,0:T(8,128)} add(f32[64,128]{1,0:T(8,128)S(1)} %add.36, f32[64,128]{1,0:T(8,128)S(1)} %collective-permute-done.10) | non-fusion elementwise | flops 8192 | bytes 98304 | tf_op jit(solution)/shard_map/add | solution.py:229
  (15 shorter events, 0.1 us)
Async XLA Ops:
  0.0 4.3 %copy-start = (bf16[512,5,128]{2,0,1:T(8,128)(2,1)S(1)}, bf16[512,5,128]{2,0,1:T(8,128)(2,1)}, u32[]{:S(2)}) copy-start(bf16[512,5,128]{2,0,1:T(8,128)(2,1)} %param.4) | copy-start | bytes 1966084
  1.2 3.1 %copy-start.1 = (s32[4,5]{1,0:T(4,128)S(1)}, s32[4,5]{1,0:T(4,128)}, u32[]{:S(2)}) copy-start(s32[4,5]{1,0:T(4,128)} %mask_ref.3) | copy-start | bytes 244
  1.2 13.4 %copy-start.2 = (bf16[8,128,512]{2,1,0:T(8,128)(2,1)S(1)}, bf16[8,128,512]{2,1,0:T(8,128)(2,1)}, u32[]{:S(2)}) copy-start(bf16[8,128,512]{2,1,0:T(8,128)(2,1)} %param.3) | copy-start | bytes 3145732
  1.3 9.3 %collective-permute-start = (bf16[4,128,256]{2,1,0:T(8,128)(2,1)S(1)}, bf16[4,128,256]{2,1,0:T(8,128)(2,1)S(1)}, u32[]{:S(2)}, u32[]{:S(2)}) collective-permute-start(bf16[4,128,256]{2,1,0:T(8,128)(2,1)S(1)} %get-tuple-element.21), channel_id=1, source_target_pairs={{0,4},{1,5},{2,6},{3,7},{4,0},{5,1},{6,2},{7,3},{8,12},{9,13},{10,... | collective-permute-start | bytes 786440 | tf_op jit(solution)/shard_map/ppermute | solution.py:26
  4.9 14.3 %collective-permute-start.2 = (bf16[1408,128]{1,0:T(8,128)(2,1)S(1)}, bf16[1408,128]{1,0:T(8,128)(2,1)S(1)}, u32[]{:S(2)}, u32[]{:S(2)}) collective-permute-start(bf16[1408,128]{1,0:T(8,128)(2,1)S(1)} %shard_map.37), channel_id=1, source_target_pairs={{0,1},{1,2},{2,3},{3,0},{4,5},{5,6},{6,7},{7,4},{8,9},{9,10},{10,1... | collective-permute-start | bytes 1081352 | tf_op jit(solution)/shard_map/ppermute | solution.py:26
  10.6 7.5 %collective-permute-start.1 = (bf16[4,128,256]{2,1,0:T(8,128)(2,1)S(1)}, bf16[4,128,256]{2,1,0:T(8,128)(2,1)S(1)}, u32[]{:S(2)}, u32[]{:S(2)}) collective-permute-start(bf16[4,128,256]{2,1,0:T(8,128)(2,1)S(1)} %get-tuple-element.12), channel_id=1, source_target_pairs={{0,4},{1,5},{2,6},{3,7},{4,0},{5,1},{6,2},{7,3},{8,12},{9,13},{10,... | collective-permute-start | bytes 786440 | tf_op jit(solution)/shard_map/ppermute | solution.py:26
  12.3 10.0 %collective-permute-start.3 = (bf16[4,128,256]{2,1,0:T(8,128)(2,1)S(1)}, bf16[4,128,256]{2,1,0:T(8,128)(2,1)S(1)}, u32[]{:S(2)}, u32[]{:S(2)}) collective-permute-start(bf16[4,128,256]{2,1,0:T(8,128)(2,1)S(1)} %collective-permute-done.refs_2_), channel_id=1, source_target_pairs={{0,1},{1,2},{2,3},{3,0},{4,5},{5,6},{6,7},{7,4},{8,9},{9,10},{10,1... | collective-permute-start | bytes 786440 | tf_op jit(solution)/shard_map/ppermute | solution.py:26
  23.4 1.4 %collective-permute-start.4 = (f32[4,64,128]{2,1,0:T(8,128)S(1)}, f32[4,64,128]{2,1,0:T(8,128)S(1)}, u32[]{:S(2)}, u32[]{:S(2)}) collective-permute-start(f32[4,64,128]{2,1,0:T(8,128)S(1)} %get-tuple-element.18), channel_id=1, source_target_pairs={{0,8},{1,9},{2,10},{3,11},{4,12},{5,13},{6,14},{7,15},{8,0},{9,1},... | collective-permute-start | bytes 393224 | tf_op jit(solution)/shard_map/ppermute | solution.py:26
  24.8 5.1 %collective-permute-start.5 = (f32[64,128]{1,0:T(8,128)S(1)}, f32[64,128]{1,0:T(8,128)S(1)}, u32[]{:S(2)}, u32[]{:S(2)}) collective-permute-start(f32[64,128]{1,0:T(8,128)S(1)} %get-tuple-element.22), channel_id=1, source_target_pairs={{0,1},{1,0},{2,3},{3,2},{4,5},{5,4},{6,7},{7,6},{8,12},{9,13},{10,... | collective-permute-start | bytes 98312 | tf_op jit(solution)/shard_map/ppermute | solution.py:26
  24.9 5.1 %collective-permute-start.6 = (f32[64,128]{1,0:T(8,128)S(1)}, f32[64,128]{1,0:T(8,128)S(1)}, u32[]{:S(2)}, u32[]{:S(2)}) collective-permute-start(f32[64,128]{1,0:T(8,128)S(1)} %get-tuple-element.24), channel_id=1, source_target_pairs={{0,2},{1,3},{2,0},{3,1},{4,6},{5,7},{6,4},{7,5},{8,13},{9,12},{10,... | collective-permute-start | bytes 98312 | tf_op jit(solution)/shard_map/ppermute | solution.py:26
  27.2 5.7 %collective-permute-start.7 = (f32[64,128]{1,0:T(8,128)S(1)}, f32[64,128]{1,0:T(8,128)S(1)}, u32[]{:S(2)}, u32[]{:S(2)}) collective-permute-start(f32[64,128]{1,0:T(8,128)S(1)} %get-tuple-element.23), channel_id=1, source_target_pairs={{0,3},{1,2},{2,1},{3,0},{4,7},{5,6},{6,5},{7,4},{8,14},{9,15},{10,... | collective-permute-start | bytes 98312 | tf_op jit(solution)/shard_map/ppermute | solution.py:26
  29.3 3.6 %collective-permute-start.8 = (f32[64,128]{1,0:T(8,128)S(1)}, f32[64,128]{1,0:T(8,128)S(1)}, u32[]{:S(2)}, u32[]{:S(2)}) collective-permute-start(f32[64,128]{1,0:T(8,128)S(1)} %get-tuple-element.25), channel_id=1, source_target_pairs={{8,15},{9,14},{10,13},{11,12},{12,11},{13,10},{14,9},{15,8},{24,31... | collective-permute-start | bytes 98312 | tf_op jit(solution)/shard_map/ppermute | solution.py:26
  32.9 4.0 %collective-permute-start.9 = (f32[64,128]{1,0:T(8,128)S(1)}, f32[64,128]{1,0:T(8,128)S(1)}, u32[]{:S(2)}, u32[]{:S(2)}) collective-permute-start(f32[64,128]{1,0:T(8,128)S(1)} %add_add_fusion), channel_id=1, source_target_pairs={{0,16},{1,17},{2,18},{3,19},{4,20},{5,21},{6,22},{7,23},{8,24},{9,... | collective-permute-start | bytes 98312 | tf_op jit(solution)/shard_map/ppermute | solution.py:26
  36.9 2.4 %collective-permute-start.10 = (f32[64,128]{1,0:T(8,128)S(1)}, f32[64,128]{1,0:T(8,128)S(1)}, u32[]{:S(2)}, u32[]{:S(2)}) collective-permute-start(f32[64,128]{1,0:T(8,128)S(1)} %add.36), channel_id=1, source_target_pairs={{0,8},{1,9},{2,10},{3,11},{4,12},{5,13},{6,14},{7,15},{8,0},{9,1},... | collective-permute-start | bytes 98312 | tf_op jit(solution)/shard_map/ppermute | solution.py:26

commit v4 on v3

v4 whole, which is shorter than its diff:
```python
import functools

import jax
import jax.numpy as jnp
from jax import lax
from jax.experimental import pallas as pl
from jax.experimental.pallas import tpu as pltpu
from jax.sharding import PartitionSpec as P

AXES = ("ri", "row", "col")
F32 = jnp.float32
BF16 = jnp.bfloat16
VMEM = pl.BlockSpec(memory_space=pltpu.VMEM)
HBM = pl.BlockSpec(memory_space=pltpu.HBM)
SMEM = pl.BlockSpec(memory_space=pltpu.SMEM)
PARAMS = pltpu.CompilerParams(vmem_limit_bytes=32 * 1024 * 1024)


def move(value, sizes, target):
    pairs = []
    for i in range(sizes[0]):
        for j in range(sizes[1]):
            for k in range(sizes[2]):
                to = target(i, j, k)
                if to is not None:
                    pairs.append(((i * sizes[1] + j) * sizes[2] + k, (to[0] * sizes[1] + to[1]) * sizes[2] + to[2]))
    return lax.ppermute(value, AXES, pairs)


def owned(rows, cols):
    offsets = [(a, b) for a in range(rows) for b in range(cols)]
    half = len(offsets) // 2
    first = offsets[1:half] + offsets[:1]
    return first, offsets[half:]


def times(a, b):
    return jnp.dot(a, b, preferred_element_type=F32)


def times_turned(a, b):
    return lax.dot_general(a, b, (((1,), (1,)), ((), ())), preferred_element_type=F32)


def masked(mask_ref, dens_ref, l, c):
    orb = dens_ref.shape[2]
    block = dens_ref[c, l * orb : (l + 1) * orb, :]
    return jnp.where(mask_ref[l, c] != 0, block, jnp.zeros_like(block))


def beyond(centre):
    return [(l, s) for l in range(centre) for s in range(l + 1)]


def side_by_side(parts):
    return jnp.concatenate([parts[p] for p in range(parts.shape[0])], axis=1)


def cut(tensor_ref, chunk, index, lo, size, out_ref, sem):
    return pltpu.make_async_copy(tensor_ref.at[pl.ds(index * chunk, chunk), :, pl.ds(lo, size)], out_ref, sem)


def edge_kernel(tensor_ref, *refs):
    outs, sems = refs[:-1], refs[-1]
    chunk, rows, wide = outs[0].shape
    row = lax.axis_index("row")
    copies = [
        cut(tensor_ref, chunk, row ^ (d + 1), tensor_ref.shape[2] - wide, wide, out, sems.at[d])
        for d, out in enumerate(outs)
    ]
    for copy in copies:
        copy.start()
    for copy in copies:
        copy.wait()


def pack_kernel(centre, chunk, mask_ref, dens_ref, tensor_ref, out_ref, blocks_ref, sems):
    band_count, cols, orb = dens_ref.shape
    blocks = cols // orb
    rows = tensor_ref.shape[1]
    row = lax.axis_index("row")
    core = lax.rem(lax.axis_index("ri"), 2)
    copies = []
    for p in range(chunk):
        for j in range(centre):
            n = p * centre + j
            copies.append(
                pltpu.make_async_copy(
                    tensor_ref.at[row * chunk + p, :, pl.ds(cols - (centre - j) * orb, orb)],
                    out_ref.at[pl.ds(n * rows, rows), :],
                    sems.at[n],
                )
            )
    for copy in copies:
        copy.start()
    for n, (l, s) in enumerate(beyond(centre)):
        blocks_ref[n * orb : (n + 1) * orb, :] = masked(mask_ref, dens_ref, blocks - centre + l, s - l + 2 * centre)
    half = blocks_ref.shape[0] // 2
    out_ref[chunk * centre * rows :, :] = blocks_ref[pl.ds(pl.multiple_of(core * half, half), half), :]
    for copy in copies:
        copy.wait()


def band_kernel(centre, count, mask_ref, dens_ref, tensor_ref, *refs):
    mine_ref = refs[0]
    rests = refs[1:count]
    local_ref, back_ref, sems = refs[count:]
    band_count, cols, orb = dens_ref.shape
    chunk = mine_ref.shape[0]
    blocks = cols // orb
    row = lax.axis_index("row")
    copies = [cut(tensor_ref, chunk, row, 0, cols, mine_ref, sems.at[0])]
    for d, rest_ref in enumerate(rests):
        copies.append(cut(tensor_ref, chunk, row ^ (d + 1), 0, rest_ref.shape[2], rest_ref, sems.at[d + 1]))
    for copy in copies:
        copy.start()
    local_ref[...] = jnp.zeros_like(local_ref)
    back_ref[...] = jnp.zeros_like(back_ref)
    for l in range(blocks):
        for c in range(band_count):
            s = l + c - centre
            if s < 0:
                back_ref[l * orb : (l + 1) * orb, (s + centre) * orb : (s + centre + 1) * orb] = masked(
                    mask_ref, dens_ref, l, c
                )
            elif s < blocks:
                local_ref[l * orb : (l + 1) * orb, s * orb : (s + 1) * orb] = masked(mask_ref, dens_ref, l, c)
    for copy in copies:
        copy.wait()


def inner_kernel(count, centre, *refs):
    own_ref = refs[0]
    rests = refs[1:count]
    edges = refs[count : 2 * count - 1]
    packed_ref, partner_ref, local_ref, back_ref = refs[2 * count - 1 : 2 * count + 3]
    total_ref, near_ref, behind_ref, open_ref, cross_ref, blocks_ref = refs[2 * count + 3 :]
    chunk, rows, cols = own_ref.shape
    orb = packed_ref.shape[1]
    wide = centre * orb
    core = lax.rem(lax.axis_index("ri"), 2)

    half = partner_ref.shape[0]
    blocks_ref[pl.ds(pl.multiple_of(core * half, half), half), :] = packed_ref[chunk * centre * rows :, :]
    blocks_ref[pl.ds(pl.multiple_of((1 - core) * half, half), half), :] = partner_ref[...]
    cross_ref[...] = jnp.zeros_like(cross_ref)
    for n, (l, s) in enumerate(beyond(centre)):
        cross_ref[l * orb : (l + 1) * orb, s * orb : (s + 1) * orb] = blocks_ref[n * orb : (n + 1) * orb, :]

    def turned(columns):
        return side_by_side(columns.reshape(chunk, rows, columns.shape[1]))

    halo = jnp.concatenate(
        [
            jnp.concatenate([packed_ref[(p * centre + j) * rows :][:rows] for j in range(centre)], axis=1)
            for p in range(chunk)
        ],
        axis=0,
    )
    held = [own_ref[...].reshape(chunk * rows, cols)] + [
        jnp.concatenate([rest[...], edge[...]], axis=2).reshape(chunk * rows, cols) for rest, edge in zip(rests, edges)
    ]
    near, behind, later, later_mixed = [], [], [], []
    first = None
    for d, columns in enumerate(held):
        near.append(turned(columns[:, :wide]))
        behind.append(turned(times(columns[:, :wide], back_ref[...]).astype(BF16)))
        mixed = times(columns[:, : min(cols, 2 * wide)], local_ref[: min(cols, 2 * wide), :wide])
        if d == 0:
            first = turned((mixed + times(halo, cross_ref[...])).astype(BF16))
        else:
            open_ref[d - 1] = mixed
        part, part_mixed = [], []
        for lo in range(wide, cols, wide):
            l_lo, l_hi = lo - wide, min(cols, lo + 2 * wide)
            part.append(turned(columns[:, lo : lo + wide]))
            part_mixed.append(
                turned(times(columns[:, l_lo:l_hi], local_ref[l_lo:l_hi, lo : lo + wide]).astype(BF16))
            )
        later.append(jnp.concatenate(part, axis=1))
        later_mixed.append(jnp.concatenate(part_mixed, axis=1))
    near = jnp.concatenate(near, axis=0)
    behind = jnp.concatenate(behind, axis=0)
    near_ref[...] = near
    behind_ref[...] = behind
    total_ref[...] = times_turned(jnp.concatenate(later, axis=0), jnp.concatenate(later_mixed, axis=0))
    total_ref[:, :rows] += times_turned(near, first)
    total_ref[:rows, :] += times_turned(turned(halo), behind)


def outer_kernel(count, plan, sizes, *refs):
    halos = refs[: count - 1]
    inner_ref, near_ref, behind_ref, open_ref, cross_ref, keep_ref, give_ref, kx_ref = refs[count - 1 :]
    chunk, rows, wide = halos[0].shape
    core = lax.rem(lax.axis_index("ri"), 2)
    row = lax.axis_index("row")
    col = lax.axis_index("col")
    mixed = []
    for d, halo in enumerate(halos):
        part = open_ref[d] + times(halo[...].reshape(chunk * rows, wide), cross_ref[...])
        mixed.append(side_by_side(part.astype(BF16).reshape(chunk, rows, wide)))
    columns = times_turned(near_ref[...], jnp.concatenate(mixed, axis=0))
    lines = times_turned(jnp.concatenate([side_by_side(halo[...]) for halo in halos], axis=0), behind_ref[...])
    for d in range(count):
        at = slice(d * rows, (d + 1) * rows)
        kx_ref[d, :rows] = inner_ref[:rows, at]
        kx_ref[d, rows:] = inner_ref[rows:, at] + lines[:, at]
        if d > 0:
            kx_ref[d] += columns[:, (d - 1) * rows : d * rows]
    out_rows = count * rows // sizes[2]
    per_group = rows // out_rows
    for ref, side in ((give_ref, 1 - core), (keep_ref, core)):
        for k, (zero, one) in enumerate(zip(*plan)):
            dr = jnp.where(side == 0, zero[0], one[0])
            to_col = col ^ jnp.where(side == 0, zero[1], one[1])
            start = ((to_col // per_group) ^ row) * rows + (to_col % per_group) * out_rows
            ref[k] = kx_ref[dr, pl.ds(pl.multiple_of(start, out_rows), out_rows), :]


def kernel(body, outs, in_specs, scratch=()):
    return pl.pallas_call(
        body,
        out_shape=outs,
        in_specs=in_specs,
        out_specs=[VMEM] * len(outs),
        scratch_shapes=scratch,
        compiler_params=PARAMS,
        cost_estimate=pl.CostEstimate(flops=1, bytes_accessed=1, transcendentals=0),
    )


def per_device(sizes, three_centre, density_band, band_mask):
    n_ri, n_row, n_col = sizes
    funcs, rows, cols = three_centre.shape
    band_count, orb = density_band.shape[1:]
    centre = band_count // 2
    wide = centre * orb
    chunk = funcs // n_row
    core = lax.rem(lax.axis_index("ri"), 2)
    plan = owned(n_row, n_col)
    array = jax.ShapeDtypeStruct
    sems = pltpu.SemaphoreType.DMA

    def forward(i, j, k):
        return i, j, (k + 1) % n_col

    density = jnp.transpose(density_band, (1, 0, 2))
    edges = kernel(
        edge_kernel, [array((chunk, rows, wide), BF16)] * (n_row - 1), [HBM], [sems((n_row - 1,))]
    )(three_centre)
    edges = [move(edges[d - 1], sizes, lambda i, j, k, d=d: (i, j ^ d, k)) for d in range(1, n_row)]
    half = len(beyond(centre)) * orb // 2
    own_halo = chunk * centre * rows
    (packed,) = kernel(
        functools.partial(pack_kernel, centre, chunk),
        [array((own_halo + half, orb), BF16)],
        [SMEM, VMEM, HBM],
        [pltpu.VMEM((2 * half, orb), BF16), sems((chunk * centre,))],
    )(band_mask, density, three_centre)
    packed = move(packed, sizes, forward)
    partner = move(packed[own_halo:], sizes, lambda i, j, k: (i ^ 1, j, k))
    mine, *rests, local, back = kernel(
        functools.partial(band_kernel, centre, n_row),
        [array((chunk, rows, cols), BF16)]
        + [array((chunk, rows, cols - wide), BF16)] * (n_row - 1)
        + [array((cols, cols), BF16), array((wide, wide), BF16)],
        [SMEM, VMEM, HBM],
        [sems((n_row,))],
    )(band_mask, density, three_centre)
    halos = [move(part, sizes, forward) for part in edges]
    rests = [
        move(rests[d - 1], sizes, lambda i, j, k, d=d: (i, j ^ d, k)) for d in range(1, n_row)
    ]

    whole = n_row * rows
    handed = kernel(
        functools.partial(inner_kernel, n_row, centre),
        [
            array((whole, whole), F32),
            array((whole, chunk * wide), BF16),
            array((whole, chunk * wide), BF16),
            array((n_row - 1, chunk * rows, wide), F32),
            array((wide, wide), BF16),
        ],
        [VMEM] * (2 * n_row + 3),
        [pltpu.VMEM((2 * half, orb), BF16)],
    )(mine, *rests, *edges, packed, partner, local, back)

    half = n_row * n_col // 2
    keep, give = kernel(
        functools.partial(outer_kernel, n_row, plan, sizes),
        [array((half, whole // n_col, rows), F32)] * 2,
        [VMEM] * (n_row - 1 + 5),
        [pltpu.VMEM((n_row, whole, rows), F32)],
    )(*halos, *handed)

    got = move(give, sizes, lambda i, j, k: (i ^ 1, j, k))
    pieces = keep + got
    total = jnp.where(core == 0, pieces[half - 1], 0.0)
    for n, (zero, one) in enumerate(zip(*plan)):
        def target(i, j, k):
            dr, dc = one if i % 2 else zero
            return None if (dr, dc) == (0, 0) else (i, j ^ dr, k ^ dc)

        total = total + move(pieces[n], sizes, target)
    result = total
    for d in range(2, n_ri, 2):
        result = result + move(total, sizes, lambda i, j, k, d=d: (i ^ d, j, k))
    return result + move(result, sizes, lambda i, j, k: (i ^ 1, j, k))


def solution(mesh):
    sizes = tuple(mesh.shape[axis] for axis in AXES)
    placed = (P("ri", "row", "col"), P("col", None, None), P("col", None))
    return jax.shard_map(
        functools.partial(per_device, sizes), mesh=mesh, in_specs=placed, out_specs=P("col", "row"), check_vma=False
    )
```

time: 40.1 us -> 39.2 us (0.978)
  waiting for transfers between devices: 18.1 us -> 16.8 us
    ppermute x11 -> x12, waiting for transfers between devices: 18.1 us -> 16.8 us  [move(): return lax.ppermute(value, AXES, pairs)]
    dynamic_slice x2 -> x0, local copies, waits for them, and re-layouts: 1.27 us -> none  [pick(): lax.dynamic_slice(three_centre, (index * chunk, 0, lo), (chunk, rows, hi...]
    unnamed x6, local copies, waits for them, and re-layouts: 0.02 us -> 1.23 us
    ppermute x11 -> x12, starting transfers between devices: 16.3 us -> 16.5 us  [move(): return lax.ppermute(value, AXES, pairs)]
    pallas_call x4 -> x5, Pallas kernels: 3.48 us -> 3.66 us  [the longest x1 1.45 us: per_device(): kernel(functools.partial(inner_kernel, n_row, centre), [array((whole, who...]
  transfers between devices with their start and end apart: 11 -> 12, of which waited for: 7 -> 8; matrix products, arithmetic and copies ran while one was open for 0% -> 0% of each run, Pallas kernels for 6% -> 8%
where the time goes in v4:
time: 39.2 us; the launch traced here: 39 us
  waiting for transfers between devices  16.8 us (43%)
  starting transfers between devices  16.5 us (42%)
  Pallas kernels  3.66 us (9%)
  local copies, waits for them, and re-layouts  1.25 us (3%)
  other arithmetic  0.66 us (2%)
    ppermute x12, waiting for transfers between devices, move(): return lax.ppermute(value, AXES, pairs)  16.8 us
    ppermute x12, starting transfers between devices, move(): return lax.ppermute(value, AXES, pairs)  16.5 us
    pallas_call x1, Pallas kernels, per_device(): kernel(functools.partial(inner_kernel, n_row, centre), [array((whole, who...  1.45 us
    unnamed x6, local copies, waits for them, and re-layouts  1.23 us
    pallas_call x1, Pallas kernels, per_device(): kernel(functools.partial(band_kernel, centre, n_row), [array((chunk, rows...  0.8 us
  transfers between devices with their start and end apart: 12, of which 8 were waited for; matrix products, arithmetic and copies ran while one was open for 0% of the time, Pallas kernels for 8%

profile of v4, /device:TPU:0, one launch (start us, length us, event | category | flops | bytes accessed | tf_op | source)
XLA Modules:
  0.0 39.0 jit_solution(6279881701064740632)
XLA Ops:
  0.0 1.2 %copy-done = bf16[8,128,512]{2,1,0:T(8,128)(2,1)S(1)} copy-done((bf16[8,128,512]{2,1,0:T(8,128)(2,1)S(1)}, bf16[8,128,512]{2,1,0:T(8,128)(2,1)}, u32[]{:S(2)}) %copy-start) | copy-done | bytes 1048600
  1.3 3.0 %collective-permute-start = (bf16[4,128,256]{2,1,0:T(8,128)(2,1)S(1)}, bf16[4,128,256]{2,1,0:T(8,128)(2,1)S(1)}, u32[]{:S(2)}, u32[]{:S(2)}) collective-permute-start(bf16[4,128,256]{2,1,0:T(8,128)(2,1)S(1)} %shard_map.37), channel_id=1, source_target_pairs={{0,4},{1,5},{2,6},{3,7},{4,0},{5,1},{6,2},{7,3},{8,12},{9,13},{10,... | collective-permute-start | bytes 786440 | tf_op jit(solution)/shard_map/ppermute | solution.py:27
  4.3 0.7 %shard_map.39 = bf16[1216,128]{1,0:T(8,128)(2,1)S(1)} custom-call(s32[4,5]{1,0:T(4,128)S(1)} %copy-done.2, bf16[5,512,128]{2,1,0:T(8,128)(2,1)S(1)} %bitcast.11, bf16[8,128,512]{2,1,0:T(8,128)(2,1)S(1)} %copy-done), custom_call_target="tpu_custom_call" | custom-call | flops 1 | bytes 1 | tf_op jit(solution)/shard_map/pallas_call | solution.py:254
  5.1 1.6 %collective-permute-start.3 = (bf16[1216,128]{1,0:T(8,128)(2,1)S(1)}, bf16[1216,128]{1,0:T(8,128)(2,1)S(1)}, u32[]{:S(2)}, u32[]{:S(2)}) collective-permute-start(bf16[1216,128]{1,0:T(8,128)(2,1)S(1)} %shard_map.39), channel_id=1, source_target_pairs={{0,1},{1,2},{2,3},{3,0},{4,5},{5,6},{6,7},{7,4},{8,9},{9,10},{10,1... | collective-permute-start | bytes 933896 | tf_op jit(solution)/shard_map/ppermute | solution.py:27
  6.7 0.8 %shard_map.38 = (bf16[4,128,512]{2,1,0:T(8,128)(2,1)S(1)}, bf16[4,128,256]{2,1,0:T(8,128)(2,1)S(1)}, bf16[512,512]{1,0:T(8,128)(2,1)S(1)}, bf16[256,256]{1,0:T(8,128)(2,1)S(1)}) custom-call(s32[4,5]{1,0:T(4,128)S(1)} %copy-done.2, bf16[5,512,128]{2,1,0:T(8,128)(2,1)S(1)} %bitcast.12, bf16[8,128,512]{2,1,0:T(8,128)(2,1)S(1)} %copy-done), custom_call_target="tpu_custom_call" | custom-call | flops 1 | bytes 1 | tf_op jit(solution)/shard_map/pallas_call | solution.py:262
  7.5 1.0 %collective-permute-start.2 = (bf16[4,128,256]{2,1,0:T(8,128)(2,1)S(1)}, bf16[4,128,256]{2,1,0:T(8,128)(2,1)S(1)}, u32[]{:S(2)}, u32[]{:S(2)}) collective-permute-start(bf16[4,128,256]{2,1,0:T(8,128)(2,1)S(1)} %get-tuple-element.17), channel_id=1, source_target_pairs={{0,4},{1,5},{2,6},{3,7},{4,0},{5,1},{6,2},{7,3},{8,12},{9,13},{10,... | collective-permute-start | bytes 786440 | tf_op jit(solution)/shard_map/ppermute | solution.py:27
  8.5 2.9 %collective-permute-done.refs_2_ = bf16[4,128,256]{2,1,0:T(8,128)(2,1)S(1)} collective-permute-done((bf16[4,128,256]{2,1,0:T(8,128)(2,1)S(1)}, bf16[4,128,256]{2,1,0:T(8,128)(2,1)S(1)}, u32[]{:S(2)}, u32[]{:S(2)}) %collective-permute-start) | collective-permute-done | bytes 262176 | tf_op jit(solution)/shard_map/ppermute | solution.py:27
  11.4 2.1 %collective-permute-start.1 = (bf16[4,128,256]{2,1,0:T(8,128)(2,1)S(1)}, bf16[4,128,256]{2,1,0:T(8,128)(2,1)S(1)}, u32[]{:S(2)}, u32[]{:S(2)}) collective-permute-start(bf16[4,128,256]{2,1,0:T(8,128)(2,1)S(1)} %collective-permute-done.refs_2_), channel_id=1, source_target_pairs={{0,1},{1,2},{2,3},{3,0},{4,5},{5,6},{6,7},{7,4},{8,9},{9,10},{10,1... | collective-permute-start | bytes 786440 | tf_op jit(solution)/shard_map/ppermute | solution.py:27
  13.5 3.6 %collective-permute-done.3.refs_3_ = bf16[1216,128]{1,0:T(8,128)(2,1)S(1)} collective-permute-done((bf16[1216,128]{1,0:T(8,128)(2,1)S(1)}, bf16[1216,128]{1,0:T(8,128)(2,1)S(1)}, u32[]{:S(2)}, u32[]{:S(2)}) %collective-permute-start.3) | collective-permute-done | bytes 311328 | tf_op jit(solution)/shard_map/ppermute | solution.py:27
  17.2 1.2 %collective-permute-done.4.refs_4_ = bf16[192,128]{1,0:T(8,128)(2,1)S(1)} collective-permute-done((bf16[192,128]{1,0:T(8,128)(2,1)S(1)}, bf16[192,128]{1,0:T(8,128)(2,1)S(1)}, u32[]{:S(2)}, u32[]{:S(2)}) %collective-permute-start.4) | collective-permute-done | bytes 49184 | tf_op jit(solution)/shard_map/ppermute | solution.py:27
  18.4 1.5 %shard_map.40 = (f32[256,256]{1,0:T(8,128)S(1)}, bf16[256,1024]{1,0:T(8,128)(2,1)S(1)}, bf16[256,1024]{1,0:T(8,128)(2,1)S(1)}, f32[1,512,256]{2,1,0:T(8,128)S(1)}, bf16[256,256]{1,0:T(8,128)(2,1)S(1)}) custom-call(bf16[4,128,512]{2,1,0:T(8,128)(2,1)S(1)} %get-tuple-element.16.refs_0_, bf16[4,128,256]{2,1,0:T(8,128)(2,1)S(1)} %collective-permute-done.2.refs_1_, ...), custom_call_target="tpu_custom_call" | custom-call | flops 1 | bytes 1 | tf_op jit(solution)/shard_map/pallas_call | solution.py:276
  19.9 1.5 %collective-permute-done.1.refs_0_ = bf16[4,128,256]{2,1,0:T(8,128)(2,1)S(1)} collective-permute-done((bf16[4,128,256]{2,1,0:T(8,128)(2,1)S(1)}, bf16[4,128,256]{2,1,0:T(8,128)(2,1)S(1)}, u32[]{:S(2)}, u32[]{:S(2)}) %collective-permute-start.1) | collective-permute-done | bytes 262176 | tf_op jit(solution)/shard_map/ppermute | solution.py:27
  21.4 0.6 %shard_map.41 = (f32[4,64,128]{2,1,0:T(8,128)S(1)}, f32[4,64,128]{2,1,0:T(8,128)S(1)}) custom-call(bf16[4,128,256]{2,1,0:T(8,128)(2,1)S(1)} %collective-permute-done.1.refs_0_, f32[256,256]{1,0:T(8,128)S(1)} %get-tuple-element.20.refs_1_, bf16[256,1024]{1,0:T(8,128)(2,1)S(1)} %get-tuple-element.21.refs_2_, bf16[256,1024]{1,0:T(8,128)(2,1)S(1)} %get-tuple-element.22.refs_3_, ...), custom_call_target="tpu_custom_call" | custom-call | flops 1 | bytes 1 | tf_op jit(solution)/shard_map/pallas_call | solution.py:290
  22.0 0.1 collective-permute-start.5
  22.1 1.3 %collective-permute-done.5 = f32[4,64,128]{2,1,0:T(8,128)S(1)} collective-permute-done((f32[4,64,128]{2,1,0:T(8,128)S(1)}, f32[4,64,128]{2,1,0:T(8,128)S(1)}, u32[]{:S(2)}, u32[]{:S(2)}) %collective-permute-start.5) | collective-permute-done | bytes 131104 | tf_op jit(solution)/shard_map/ppermute | solution.py:27
  23.6 2.3 %collective-permute-start.7 = (f32[64,128]{1,0:T(8,128)S(1)}, f32[64,128]{1,0:T(8,128)S(1)}, u32[]{:S(2)}, u32[]{:S(2)}) collective-permute-start(f32[64,128]{1,0:T(8,128)S(1)} %get-tuple-element.29), channel_id=1, source_target_pairs={{0,2},{1,3},{2,0},{3,1},{4,6},{5,7},{6,4},{7,5},{8,13},{9,12},{10,... | collective-permute-start | bytes 98312 | tf_op jit(solution)/shard_map/ppermute | solution.py:27
  25.9 2.1 %collective-permute-start.8 = (f32[64,128]{1,0:T(8,128)S(1)}, f32[64,128]{1,0:T(8,128)S(1)}, u32[]{:S(2)}, u32[]{:S(2)}) collective-permute-start(f32[64,128]{1,0:T(8,128)S(1)} %get-tuple-element.28), channel_id=1, source_target_pairs={{0,3},{1,2},{2,1},{3,0},{4,7},{5,6},{6,5},{7,4},{8,14},{9,15},{10,... | collective-permute-start | bytes 98312 | tf_op jit(solution)/shard_map/ppermute | solution.py:27
  28.0 0.7 %collective-permute-start.9 = (f32[64,128]{1,0:T(8,128)S(1)}, f32[64,128]{1,0:T(8,128)S(1)}, u32[]{:S(2)}, u32[]{:S(2)}) collective-permute-start(f32[64,128]{1,0:T(8,128)S(1)} %get-tuple-element.30), channel_id=1, source_target_pairs={{8,15},{9,14},{10,13},{11,12},{12,11},{13,10},{14,9},{15,8},{24,31... | collective-permute-start | bytes 98312 | tf_op jit(solution)/shard_map/ppermute | solution.py:27
  28.6 2.9 %collective-permute-done.8 = f32[64,128]{1,0:T(8,128)S(1)} collective-permute-done((f32[64,128]{1,0:T(8,128)S(1)}, f32[64,128]{1,0:T(8,128)S(1)}, u32[]{:S(2)}, u32[]{:S(2)}) %collective-permute-start.8) | collective-permute-done | bytes 32800 | tf_op jit(solution)/shard_map/ppermute | solution.py:27
  31.6 1.6 %collective-permute-start.10 = (f32[64,128]{1,0:T(8,128)S(1)}, f32[64,128]{1,0:T(8,128)S(1)}, u32[]{:S(2)}, u32[]{:S(2)}) collective-permute-start(f32[64,128]{1,0:T(8,128)S(1)} %add_add_fusion), channel_id=1, source_target_pairs={{0,16},{1,17},{2,18},{3,19},{4,20},{5,21},{6,22},{7,23},{8,24},{9,... | collective-permute-start | bytes 98312 | tf_op jit(solution)/shard_map/ppermute | solution.py:27
  33.2 2.4 %collective-permute-done.10 = f32[64,128]{1,0:T(8,128)S(1)} collective-permute-done((f32[64,128]{1,0:T(8,128)S(1)}, f32[64,128]{1,0:T(8,128)S(1)}, u32[]{:S(2)}, u32[]{:S(2)}) %collective-permute-start.10) | collective-permute-done | bytes 32800 | tf_op jit(solution)/shard_map/ppermute | solution.py:27
  35.6 1.9 %collective-permute-start.11 = (f32[64,128]{1,0:T(8,128)S(1)}, f32[64,128]{1,0:T(8,128)S(1)}, u32[]{:S(2)}, u32[]{:S(2)}) collective-permute-start(f32[64,128]{1,0:T(8,128)S(1)} %add.26), channel_id=1, source_target_pairs={{0,8},{1,9},{2,10},{3,11},{4,12},{5,13},{6,14},{7,15},{8,0},{9,1},... | collective-permute-start | bytes 98312 | tf_op jit(solution)/shard_map/ppermute | solution.py:27
  37.5 0.9 %collective-permute-done.11 = f32[64,128]{1,0:T(8,128)S(1)} collective-permute-done((f32[64,128]{1,0:T(8,128)S(1)}, f32[64,128]{1,0:T(8,128)S(1)}, u32[]{:S(2)}, u32[]{:S(2)}) %collective-permute-start.11) | collective-permute-done | bytes 32800 | tf_op jit(solution)/shard_map/ppermute | solution.py:27
  38.4 0.6 %add.27 = f32[64,128]{1,0:T(8,128)} add(f32[64,128]{1,0:T(8,128)S(1)} %add.26, f32[64,128]{1,0:T(8,128)S(1)} %collective-permute-done.11) | non-fusion elementwise | flops 8192 | bytes 98304 | tf_op jit(solution)/shard_map/add | solution.py:309
  (17 shorter events, 0.2 us)
Async XLA Ops:
  0.0 1.2 %copy-start = (bf16[8,128,512]{2,1,0:T(8,128)(2,1)S(1)}, bf16[8,128,512]{2,1,0:T(8,128)(2,1)}, u32[]{:S(2)}) copy-start(bf16[8,128,512]{2,1,0:T(8,128)(2,1)} %tensor_ref.5) | copy-start | bytes 3145732
  1.2 3.1 %copy-start.1 = (bf16[512,5,128]{2,0,1:T(8,128)(2,1)S(1)}, bf16[512,5,128]{2,0,1:T(8,128)(2,1)}, u32[]{:S(2)}) copy-start(bf16[512,5,128]{2,0,1:T(8,128)(2,1)} %param.4) | copy-start | bytes 1966084
  1.2 3.1 %copy-start.2 = (s32[4,5]{1,0:T(4,128)S(1)}, s32[4,5]{1,0:T(4,128)}, u32[]{:S(2)}) copy-start(s32[4,5]{1,0:T(4,128)} %mask_ref.3) | copy-start | bytes 244
  1.3 10.2 %collective-permute-start = (bf16[4,128,256]{2,1,0:T(8,128)(2,1)S(1)}, bf16[4,128,256]{2,1,0:T(8,128)(2,1)S(1)}, u32[]{:S(2)}, u32[]{:S(2)}) collective-permute-start(bf16[4,128,256]{2,1,0:T(8,128)(2,1)S(1)} %shard_map.37), channel_id=1, source_target_pairs={{0,4},{1,5},{2,6},{3,7},{4,0},{5,1},{6,2},{7,3},{8,12},{9,13},{10,... | collective-permute-start | bytes 786440 | tf_op jit(solution)/shard_map/ppermute | solution.py:27
  5.1 12.1 %collective-permute-start.3 = (bf16[1216,128]{1,0:T(8,128)(2,1)S(1)}, bf16[1216,128]{1,0:T(8,128)(2,1)S(1)}, u32[]{:S(2)}, u32[]{:S(2)}) collective-permute-start(bf16[1216,128]{1,0:T(8,128)(2,1)S(1)} %shard_map.39), channel_id=1, source_target_pairs={{0,1},{1,2},{2,3},{3,0},{4,5},{5,6},{6,7},{7,4},{8,9},{9,10},{10,1... | collective-permute-start | bytes 933896 | tf_op jit(solution)/shard_map/ppermute | solution.py:27
  7.5 9.7 %collective-permute-start.2 = (bf16[4,128,256]{2,1,0:T(8,128)(2,1)S(1)}, bf16[4,128,256]{2,1,0:T(8,128)(2,1)S(1)}, u32[]{:S(2)}, u32[]{:S(2)}) collective-permute-start(bf16[4,128,256]{2,1,0:T(8,128)(2,1)S(1)} %get-tuple-element.17), channel_id=1, source_target_pairs={{0,4},{1,5},{2,6},{3,7},{4,0},{5,1},{6,2},{7,3},{8,12},{9,13},{10,... | collective-permute-start | bytes 786440 | tf_op jit(solution)/shard_map/ppermute | solution.py:27
  11.4 10.0 %collective-permute-start.1 = (bf16[4,128,256]{2,1,0:T(8,128)(2,1)S(1)}, bf16[4,128,256]{2,1,0:T(8,128)(2,1)S(1)}, u32[]{:S(2)}, u32[]{:S(2)}) collective-permute-start(bf16[4,128,256]{2,1,0:T(8,128)(2,1)S(1)} %collective-permute-done.refs_2_), channel_id=1, source_target_pairs={{0,1},{1,2},{2,3},{3,0},{4,5},{5,6},{6,7},{7,4},{8,9},{9,10},{10,1... | collective-permute-start | bytes 786440 | tf_op jit(solution)/shard_map/ppermute | solution.py:27
  17.2 1.2 %collective-permute-start.4 = (bf16[192,128]{1,0:T(8,128)(2,1)S(1)}, bf16[192,128]{1,0:T(8,128)(2,1)S(1)}, u32[]{:S(2)}, u32[]{:S(2)}) collective-permute-start(bf16[192,128]{1,0:T(8,128)(2,1)S(1)} %slice.21), channel_id=1, source_target_pairs={{0,8},{1,9},{2,10},{3,11},{4,12},{5,13},{6,14},{7,15},{8,0},{9,1},... | collective-permute-start | bytes 147464 | tf_op jit(solution)/shard_map/ppermute | solution.py:27
  22.0 1.4 %collective-permute-start.5 = (f32[4,64,128]{2,1,0:T(8,128)S(1)}, f32[4,64,128]{2,1,0:T(8,128)S(1)}, u32[]{:S(2)}, u32[]{:S(2)}) collective-permute-start(f32[4,64,128]{2,1,0:T(8,128)S(1)} %get-tuple-element.26), channel_id=1, source_target_pairs={{0,8},{1,9},{2,10},{3,11},{4,12},{5,13},{6,14},{7,15},{8,0},{9,1},... | collective-permute-start | bytes 393224 | tf_op jit(solution)/shard_map/ppermute | solution.py:27
  23.5 5.1 %collective-permute-start.6 = (f32[64,128]{1,0:T(8,128)S(1)}, f32[64,128]{1,0:T(8,128)S(1)}, u32[]{:S(2)}, u32[]{:S(2)}) collective-permute-start(f32[64,128]{1,0:T(8,128)S(1)} %get-tuple-element.27), channel_id=1, source_target_pairs={{0,1},{1,0},{2,3},{3,2},{4,5},{5,4},{6,7},{7,6},{8,12},{9,13},{10,... | collective-permute-start | bytes 98312 | tf_op jit(solution)/shard_map/ppermute | solution.py:27
  23.6 5.1 %collective-permute-start.7 = (f32[64,128]{1,0:T(8,128)S(1)}, f32[64,128]{1,0:T(8,128)S(1)}, u32[]{:S(2)}, u32[]{:S(2)}) collective-permute-start(f32[64,128]{1,0:T(8,128)S(1)} %get-tuple-element.29), channel_id=1, source_target_pairs={{0,2},{1,3},{2,0},{3,1},{4,6},{5,7},{6,4},{7,5},{8,13},{9,12},{10,... | collective-permute-start | bytes 98312 | tf_op jit(solution)/shard_map/ppermute | solution.py:27
  25.9 5.7 %collective-permute-start.8 = (f32[64,128]{1,0:T(8,128)S(1)}, f32[64,128]{1,0:T(8,128)S(1)}, u32[]{:S(2)}, u32[]{:S(2)}) collective-permute-start(f32[64,128]{1,0:T(8,128)S(1)} %get-tuple-element.28), channel_id=1, source_target_pairs={{0,3},{1,2},{2,1},{3,0},{4,7},{5,6},{6,5},{7,4},{8,14},{9,15},{10,... | collective-permute-start | bytes 98312 | tf_op jit(solution)/shard_map/ppermute | solution.py:27
  28.0 3.6 %collective-permute-start.9 = (f32[64,128]{1,0:T(8,128)S(1)}, f32[64,128]{1,0:T(8,128)S(1)}, u32[]{:S(2)}, u32[]{:S(2)}) collective-permute-start(f32[64,128]{1,0:T(8,128)S(1)} %get-tuple-element.30), channel_id=1, source_target_pairs={{8,15},{9,14},{10,13},{11,12},{12,11},{13,10},{14,9},{15,8},{24,31... | collective-permute-start | bytes 98312 | tf_op jit(solution)/shard_map/ppermute | solution.py:27
  31.6 4.0 %collective-permute-start.10 = (f32[64,128]{1,0:T(8,128)S(1)}, f32[64,128]{1,0:T(8,128)S(1)}, u32[]{:S(2)}, u32[]{:S(2)}) collective-permute-start(f32[64,128]{1,0:T(8,128)S(1)} %add_add_fusion), channel_id=1, source_target_pairs={{0,16},{1,17},{2,18},{3,19},{4,20},{5,21},{6,22},{7,23},{8,24},{9,... | collective-permute-start | bytes 98312 | tf_op jit(solution)/shard_map/ppermute | solution.py:27
  35.6 2.8 %collective-permute-start.11 = (f32[64,128]{1,0:T(8,128)S(1)}, f32[64,128]{1,0:T(8,128)S(1)}, u32[]{:S(2)}, u32[]{:S(2)}) collective-permute-start(f32[64,128]{1,0:T(8,128)S(1)} %add.26), channel_id=1, source_target_pairs={{0,8},{1,9},{2,10},{3,11},{4,12},{5,13},{6,14},{7,15},{8,0},{9,1},... | collective-permute-start | bytes 98312 | tf_op jit(solution)/shard_map/ppermute | solution.py:27

commit v5 on v4

v5 whole, which is shorter than its diff:
```python
import functools

import jax
import jax.numpy as jnp
from jax import lax
from jax.experimental import pallas as pl
from jax.experimental.pallas import tpu as pltpu
from jax.sharding import PartitionSpec as P

AXES = ("ri", "row", "col")
F32 = jnp.float32
BF16 = jnp.bfloat16
VMEM = pl.BlockSpec(memory_space=pltpu.VMEM)
HBM = pl.BlockSpec(memory_space=pltpu.HBM)
SMEM = pl.BlockSpec(memory_space=pltpu.SMEM)
PARAMS = pltpu.CompilerParams(vmem_limit_bytes=32 * 1024 * 1024)


def move(value, sizes, target):
    pairs = []
    for i in range(sizes[0]):
        for j in range(sizes[1]):
            for k in range(sizes[2]):
                to = target(i, j, k)
                if to is not None:
                    pairs.append(((i * sizes[1] + j) * sizes[2] + k, (to[0] * sizes[1] + to[1]) * sizes[2] + to[2]))
    return lax.ppermute(value, AXES, pairs)


def after(value, *earlier):
    return lax.optimization_barrier((value,) + earlier)[0]


def owned(rows, cols):
    offsets = [(a, b) for a in range(rows) for b in range(cols)]
    half = len(offsets) // 2
    first = offsets[1:half] + offsets[:1]
    return first, offsets[half:]


def times(a, b):
    return jnp.dot(a, b, preferred_element_type=F32)


def times_turned(a, b):
    return lax.dot_general(a, b, (((1,), (1,)), ((), ())), preferred_element_type=F32)


def masked(mask_ref, dens_ref, l, c):
    orb = dens_ref.shape[2]
    block = dens_ref[c, l * orb : (l + 1) * orb, :]
    return jnp.where(mask_ref[l, c] != 0, block, jnp.zeros_like(block))


def beyond(centre):
    return [(l, s) for l in range(centre) for s in range(l + 1)]


def side_by_side(parts):
    return jnp.concatenate([parts[p] for p in range(parts.shape[0])], axis=1)


def cut(tensor_ref, chunk, index, lo, size, out_ref, sem):
    return pltpu.make_async_copy(tensor_ref.at[pl.ds(index * chunk, chunk), :, pl.ds(lo, size)], out_ref, sem)


def cut_kernel(count, tensor_ref, *refs):
    lasts, mine_ref, rests, sems = refs[:count], refs[count], refs[count + 1 : -1], refs[-1]
    chunk, rows, wide = lasts[0].shape
    cols = tensor_ref.shape[2]
    row = lax.axis_index("row")
    copies = [cut(tensor_ref, chunk, row, 0, cols, mine_ref, sems.at[0])]
    for d, out in enumerate(lasts):
        copies.append(cut(tensor_ref, chunk, row ^ d, cols - wide, wide, out, sems.at[1 + d]))
    for d, out in enumerate(rests):
        copies.append(cut(tensor_ref, chunk, row ^ (d + 1), 0, cols - wide, out, sems.at[1 + count + d]))
    for copy in copies:
        copy.start()
    for copy in copies:
        copy.wait()


def blocks_kernel(centre, mask_ref, dens_ref, out_ref, blocks_ref):
    band_count, cols, orb = dens_ref.shape
    core = lax.rem(lax.axis_index("ri"), 2)
    for n, (l, s) in enumerate(beyond(centre)):
        blocks_ref[n * orb : (n + 1) * orb, :] = masked(
            mask_ref, dens_ref, cols // orb - centre + l, s - l + 2 * centre
        )
    half = out_ref.shape[0]
    out_ref[...] = blocks_ref[pl.ds(pl.multiple_of(core * half, half), half), :]


def band_kernel(centre, mask_ref, dens_ref, local_ref, back_ref):
    band_count, cols, orb = dens_ref.shape
    blocks = cols // orb
    local_ref[...] = jnp.zeros_like(local_ref)
    back_ref[...] = jnp.zeros_like(back_ref)
    for l in range(blocks):
        for c in range(band_count):
            s = l + c - centre
            if s < 0:
                back_ref[l * orb : (l + 1) * orb, (s + centre) * orb : (s + centre + 1) * orb] = masked(
                    mask_ref, dens_ref, l, c
                )
            elif s < blocks:
                local_ref[l * orb : (l + 1) * orb, s * orb : (s + 1) * orb] = masked(mask_ref, dens_ref, l, c)


def turned(columns, chunk):
    return side_by_side(columns.reshape(chunk, columns.shape[0] // chunk, columns.shape[1]))


def own_kernel(count, *refs):
    own_ref = refs[0]
    edges = refs[1:count]
    local_ref, back_ref, total_ref, near_ref, behind_ref, open_ref, later_ref, part_ref = refs[count:]
    chunk, rows, cols = own_ref.shape
    wide = back_ref.shape[0]
    own = own_ref[...].reshape(chunk * rows, cols)
    near_ref[...] = turned(own[:, :wide], chunk)
    behind_ref[...] = turned(times(own[:, :wide], back_ref[...]).astype(BF16), chunk)
    open_ref[...] = times(own, local_ref[:, :wide])
    mixed = turned(times(own, local_ref[:, wide:]).astype(BF16), chunk)
    later = [turned(own[:, wide:], chunk)]
    for d, edge in enumerate(edges):
        columns = edge[...].reshape(chunk * rows, cols - wide)
        part_ref[d] = times(columns, local_ref[wide:, :])
        later.append(turned(columns, chunk))
    later = jnp.concatenate(later, axis=0)
    later_ref[...] = later
    total_ref[...] = times_turned(later, mixed)


def inner_kernel(count, centre, *refs):
    rests = refs[: count - 1]
    halo_ref, mine_ref, partner_ref, local_ref, back_ref = refs[count - 1 : count + 4]
    own_total_ref, own_near_ref, own_behind_ref, own_open_ref, later_ref, part_ref = refs[count + 4 : count + 10]
    total_ref, near_ref, behind_ref, open_ref, cross_ref, blocks_ref = refs[count + 10 :]
    chunk, rows, wide = halo_ref.shape
    orb = mine_ref.shape[1]
    core = lax.rem(lax.axis_index("ri"), 2)

    half = partner_ref.shape[0]
    blocks_ref[pl.ds(pl.multiple_of(core * half, half), half), :] = mine_ref[...]
    blocks_ref[pl.ds(pl.multiple_of((1 - core) * half, half), half), :] = partner_ref[...]
    cross_ref[...] = jnp.zeros_like(cross_ref)
    for n, (l, s) in enumerate(beyond(centre)):
        cross_ref[l * orb : (l + 1) * orb, s * orb : (s + 1) * orb] = blocks_ref[n * orb : (n + 1) * orb, :]

    halo = halo_ref[...].reshape(chunk * rows, wide)
    first = turned((own_open_ref[...] + times(halo, cross_ref[...])).astype(BF16), chunk)
    near, behind, mixed = [own_near_ref[...]], [own_behind_ref[...]], []
    for d, rest in enumerate(rests):
        columns = rest[...].reshape(chunk * rows, wide)
        near.append(turned(columns, chunk))
        behind.append(turned(times(columns, back_ref[...]).astype(BF16), chunk))
        whole = part_ref[d] + times(columns, local_ref[:wide, :])
        open_ref[d] = whole[:, :wide]
        mixed.append(turned(whole[:, wide:].astype(BF16), chunk))
    near = jnp.concatenate(near, axis=0)
    behind = jnp.concatenate(behind, axis=0)
    near_ref[...] = near
    behind_ref[...] = behind
    total_ref[:, :rows] = own_total_ref[...] + times_turned(near, first)
    total_ref[:, rows:] = times_turned(later_ref[...], jnp.concatenate(mixed, axis=0))
    total_ref[:rows, :] += times_turned(turned(halo, chunk), behind)


def outer_kernel(count, plan, sizes, *refs):
    halos = refs[: count - 1]
    inner_ref, near_ref, behind_ref, open_ref, cross_ref, keep_ref, give_ref, kx_ref = refs[count - 1 :]
    chunk, rows, wide = halos[0].shape
    core = lax.rem(lax.axis_index("ri"), 2)
    row = lax.axis_index("row")
    col = lax.axis_index("col")
    mixed = []
    for d, halo in enumerate(halos):
        part = open_ref[d] + times(halo[...].reshape(chunk * rows, wide), cross_ref[...])
        mixed.append(side_by_side(part.astype(BF16).reshape(chunk, rows, wide)))
    columns = times_turned(near_ref[...], jnp.concatenate(mixed, axis=0))
    lines = times_turned(jnp.concatenate([side_by_side(halo[...]) for halo in halos], axis=0), behind_ref[...])
    for d in range(count):
        at = slice(d * rows, (d + 1) * rows)
        kx_ref[d, :rows] = inner_ref[:rows, at]
        kx_ref[d, rows:] = inner_ref[rows:, at] + lines[:, at]
        if d > 0:
            kx_ref[d] += columns[:, (d - 1) * rows : d * rows]
    out_rows = count * rows // sizes[2]
    per_group = rows // out_rows
    for ref, side in ((give_ref, 1 - core), (keep_ref, core)):
        for k, (zero, one) in enumerate(zip(*plan)):
            dr = jnp.where(side == 0, zero[0], one[0])
            to_col = col ^ jnp.where(side == 0, zero[1], one[1])
            start = ((to_col // per_group) ^ row) * rows + (to_col % per_group) * out_rows
            ref[k] = kx_ref[dr, pl.ds(pl.multiple_of(start, out_rows), out_rows), :]


def kernel(body, outs, in_specs, scratch=()):
    return pl.pallas_call(
        body,
        out_shape=outs,
        in_specs=in_specs,
        out_specs=[VMEM] * len(outs),
        scratch_shapes=scratch,
        compiler_params=PARAMS,
        cost_estimate=pl.CostEstimate(flops=1, bytes_accessed=1, transcendentals=0),
    )


def per_device(sizes, three_centre, density_band, band_mask):
    n_ri, n_row, n_col = sizes
    funcs, rows, cols = three_centre.shape
    band_count, orb = density_band.shape[1:]
    centre = band_count // 2
    wide = centre * orb
    chunk = funcs // n_row
    core = lax.rem(lax.axis_index("ri"), 2)
    plan = owned(n_row, n_col)
    array = jax.ShapeDtypeStruct
    sems = pltpu.SemaphoreType.DMA

    def forward(i, j, k):
        return i, j, (k + 1) % n_col

    density = jnp.transpose(density_band, (1, 0, 2))
    cuts = kernel(
        functools.partial(cut_kernel, n_row),
        [array((chunk, rows, wide), BF16)] * n_row
        + [array((chunk, rows, cols), BF16)]
        + [array((chunk, rows, cols - wide), BF16)] * (n_row - 1),
        [HBM],
        [sems((2 * n_row,))],
    )(three_centre)
    halo, edges, mine, rests = cuts[0], cuts[1:n_row], cuts[n_row], cuts[n_row + 1 :]
    halo = move(halo, sizes, forward)
    edges = [move(edges[d - 1], sizes, lambda i, j, k, d=d: (i, j ^ d, k)) for d in range(1, n_row)]
    half = len(beyond(centre)) * orb // 2
    (blocks,) = kernel(
        functools.partial(blocks_kernel, centre),
        [array((half, orb), BF16)],
        [SMEM, VMEM],
        [pltpu.VMEM((2 * half, orb), BF16)],
    )(band_mask, density)
    blocks = move(blocks, sizes, forward)
    partner = move(blocks, sizes, lambda i, j, k: (i ^ 1, j, k))
    local, back = kernel(
        functools.partial(band_kernel, centre),
        [array((cols, cols), BF16), array((wide, wide), BF16)],
        [SMEM, VMEM],
    )(band_mask, density)
    halos = [move(after(part, blocks), sizes, forward) for part in edges]
    rests = [
        move(after(rests[d - 1], edges[d - 1]), sizes, lambda i, j, k, d=d: (i, j ^ d, k))
        for d in range(1, n_row)
    ]

    whole = n_row * rows
    side = chunk * wide
    first_terms = kernel(
        functools.partial(own_kernel, n_row),
        [
            array((whole, rows), F32),
            array((rows, side), BF16),
            array((rows, side), BF16),
            array((chunk * rows, wide), F32),
            array((whole, chunk * (cols - wide)), BF16),
            array((n_row - 1, chunk * rows, cols), F32),
        ],
        [VMEM] * (n_row + 2),
    )(mine, *edges, local, back)
    handed = kernel(
        functools.partial(inner_kernel, n_row, centre),
        [
            array((whole, whole), F32),
            array((whole, side), BF16),
            array((whole, side), BF16),
            array((n_row - 1, chunk * rows, wide), F32),
            array((wide, wide), BF16),
        ],
        [VMEM] * (n_row + 10),
        [pltpu.VMEM((2 * half, orb), BF16)],
    )(*rests, halo, blocks, partner, local, back, *first_terms)

    half = n_row * n_col // 2
    keep, give = kernel(
        functools.partial(outer_kernel, n_row, plan, sizes),
        [array((half, whole // n_col, rows), F32)] * 2,
        [VMEM] * (n_row - 1 + 5),
        [pltpu.VMEM((n_row, whole, rows), F32)],
    )(*halos, *handed)

    got = move(give, sizes, lambda i, j, k: (i ^ 1, j, k))
    pieces = keep + got
    total = jnp.where(core == 0, pieces[half - 1], 0.0)
    for n, (zero, one) in enumerate(zip(*plan)):
        def target(i, j, k):
            dr, dc = one if i % 2 else zero
            return None if (dr, dc) == (0, 0) else (i, j ^ dr, k ^ dc)

        total = total + move(pieces[n], sizes, target)
    result = total
    for d in range(2, n_ri, 2):
        result = result + move(total, sizes, lambda i, j, k, d=d: (i ^ d, j, k))
    return result + move(result, sizes, lambda i, j, k: (i ^ 1, j, k))


def solution(mesh):
    sizes = tuple(mesh.shape[axis] for axis in AXES)
    placed = (P("ri", "row", "col"), P("col", None, None), P("col", None))
    return jax.shard_map(
        functools.partial(per_device, sizes), mesh=mesh, in_specs=placed, out_specs=P("col", "row"), check_vma=False
    )
```

time: 39.2 us -> 38.7 us (0.987)
  waiting for transfers between devices: 16.8 us -> 16.2 us
    pallas_call x3 -> x4, Pallas kernels: 1.57 us -> 2.37 us  [the longest x1 0.93 us: per_device(): kernel(functools.partial(own_kernel, n_row), [array((whole, rows), F32),...]
    ppermute x12 -> x13, waiting for transfers between devices: 16.8 us -> 16.2 us  [move(): return lax.ppermute(value, AXES, pairs)]
    pallas_call x1, Pallas kernels: 1.45 us -> 0.88 us  [per_device(): kernel(functools.partial(inner_kernel, n_row, centre), [array((whole, who...]
    ppermute x12 -> x13, starting transfers between devices: 16.5 us -> 16.3 us  [move(): return lax.ppermute(value, AXES, pairs)]
  transfers between devices with their start and end apart: 12 -> 13, of which waited for: 8 -> 9; matrix products, arithmetic and copies ran while one was open for 0% -> 0% of each run, Pallas kernels for 8% -> 8%
where the time goes in v5:
time: 38.7 us; the launch traced here: 38.5 us
  starting transfers between devices  16.3 us (42%)
  waiting for transfers between devices  16.2 us (42%)
  Pallas kernels  3.88 us (10%)
  local copies, waits for them, and re-layouts  1.31 us (3%)
  other arithmetic  0.66 us (2%)
    ppermute x13, starting transfers between devices, move(): return lax.ppermute(value, AXES, pairs)  16.3 us
    ppermute x13, waiting for transfers between devices, move(): return lax.ppermute(value, AXES, pairs)  16.2 us
    unnamed x6, local copies, waits for them, and re-layouts  1.3 us
    pallas_call x1, Pallas kernels, per_device(): kernel(functools.partial(own_kernel, n_row), [array((whole, rows), F32),...  0.93 us
    pallas_call x1, Pallas kernels, per_device(): kernel(functools.partial(inner_kernel, n_row, centre), [array((whole, who...  0.88 us
  transfers between devices with their start and end apart: 13, of which 9 were waited for; matrix products, arithmetic and copies ran while one was open for 0% of the time, Pallas kernels for 8%

profile of v5, /device:TPU:0, one launch (start us, length us, event | category | flops | bytes accessed | tf_op | source)
XLA Modules:
  0.0 38.5 jit_solution(11129338511869031240)
XLA Ops:
  0.0 1.3 %copy-done.1 = bf16[8,128,512]{2,1,0:T(8,128)(2,1)S(1)} copy-done((bf16[8,128,512]{2,1,0:T(8,128)(2,1)S(1)}, bf16[8,128,512]{2,1,0:T(8,128)(2,1)}, u32[]{:S(2)}) %copy-start.1) | copy-done | bytes 1048600
  1.4 3.0 %collective-permute-start = (bf16[4,128,256]{2,1,0:T(8,128)(2,1)S(1)}, bf16[4,128,256]{2,1,0:T(8,128)(2,1)S(1)}, u32[]{:S(2)}, u32[]{:S(2)}) collective-permute-start(bf16[4,128,256]{2,1,0:T(8,128)(2,1)S(1)} %get-tuple-element.26), channel_id=1, source_target_pairs={{0,4},{1,5},{2,6},{3,7},{4,0},{5,1},{6,2},{7,3},{8,12},{9,13},{10,... | collective-permute-start | bytes 786440 | tf_op jit(solution)/shard_map/ppermute | solution.py:27
  4.5 0.6 %shard_map.38 = bf16[192,128]{1,0:T(8,128)(2,1)S(1)} custom-call(s32[4,5]{1,0:T(4,128)S(1)} %copy-done.2, bf16[5,512,128]{2,1,0:T(8,128)(2,1)S(1)} %bitcast.11), custom_call_target="tpu_custom_call" | custom-call | flops 1 | bytes 1 | tf_op jit(solution)/shard_map/pallas_call | solution.py:239
  5.1 1.6 %collective-permute-start.1 = (bf16[192,128]{1,0:T(8,128)(2,1)S(1)}, bf16[192,128]{1,0:T(8,128)(2,1)S(1)}, u32[]{:S(2)}, u32[]{:S(2)}) collective-permute-start(bf16[192,128]{1,0:T(8,128)(2,1)S(1)} %shard_map.38), channel_id=1, source_target_pairs={{0,1},{1,2},{2,3},{3,0},{4,5},{5,6},{6,7},{7,4},{8,9},{9,10},{10,1... | collective-permute-start | bytes 147464 | tf_op jit(solution)/shard_map/ppermute | solution.py:27
  6.7 1.6 %collective-permute-start.4 = (bf16[4,128,256]{2,1,0:T(8,128)(2,1)S(1)}, bf16[4,128,256]{2,1,0:T(8,128)(2,1)S(1)}, u32[]{:S(2)}, u32[]{:S(2)}) collective-permute-start(bf16[4,128,256]{2,1,0:T(8,128)(2,1)S(1)} %get-tuple-element.30), channel_id=1, source_target_pairs={{0,1},{1,2},{2,3},{3,0},{4,5},{5,6},{6,7},{7,4},{8,9},{9,10},{10,1... | collective-permute-start | bytes 786440 | tf_op jit(solution)/shard_map/ppermute | solution.py:27
  8.3 2.5 %collective-permute-done.refs_1_ = bf16[4,128,256]{2,1,0:T(8,128)(2,1)S(1)} collective-permute-done((bf16[4,128,256]{2,1,0:T(8,128)(2,1)S(1)}, bf16[4,128,256]{2,1,0:T(8,128)(2,1)S(1)}, u32[]{:S(2)}, u32[]{:S(2)}) %collective-permute-start) | collective-permute-done | bytes 262176 | tf_op jit(solution)/shard_map/ppermute | solution.py:27
  10.8 1.7 %collective-permute-start.3 = (bf16[4,128,256]{2,1,0:T(8,128)(2,1)S(1)}, bf16[4,128,256]{2,1,0:T(8,128)(2,1)S(1)}, u32[]{:S(2)}, u32[]{:S(2)}) collective-permute-start(bf16[4,128,256]{2,1,0:T(8,128)(2,1)S(1)} %get-tuple-element.29), channel_id=1, source_target_pairs={{0,4},{1,5},{2,6},{3,7},{4,0},{5,1},{6,2},{7,3},{8,12},{9,13},{10,... | collective-permute-start | bytes 786440 | tf_op jit(solution)/shard_map/ppermute | solution.py:27
  12.5 1.6 %collective-permute-start.2 = (bf16[4,128,256]{2,1,0:T(8,128)(2,1)S(1)}, bf16[4,128,256]{2,1,0:T(8,128)(2,1)S(1)}, u32[]{:S(2)}, u32[]{:S(2)}) collective-permute-start(bf16[4,128,256]{2,1,0:T(8,128)(2,1)S(1)} %collective-permute-done.refs_1_), channel_id=1, source_target_pairs={{0,1},{1,2},{2,3},{3,0},{4,5},{5,6},{6,7},{7,4},{8,9},{9,10},{10,1... | collective-permute-start | bytes 786440 | tf_op jit(solution)/shard_map/ppermute | solution.py:27
  14.1 0.7 %shard_map.39 = (bf16[512,512]{1,0:T(8,128)(2,1)S(1)}, bf16[256,256]{1,0:T(8,128)(2,1)S(1)}) custom-call(s32[4,5]{1,0:T(4,128)S(1)} %copy-done.2, bf16[5,512,128]{2,1,0:T(8,128)(2,1)S(1)} %bitcast.12), custom_call_target="tpu_custom_call" | custom-call | flops 1 | bytes 1 | tf_op jit(solution)/shard_map/pallas_call | solution.py:247
  14.8 0.9 %shard_map.40 = (f32[256,128]{1,0:T(8,128)S(1)}, bf16[128,1024]{1,0:T(8,128)(2,1)S(1)}, bf16[128,1024]{1,0:T(8,128)(2,1)S(1)}, f32[512,256]{1,0:T(8,128)S(1)}, b...) custom-call(bf16[4,128,512]{2,1,0:T(8,128)(2,1)S(1)} %get-tuple-element.33.refs_0_, ...), custom_call_target="tpu_custom_call" | custom-call | flops 1 | bytes 1 | tf_op jit(solution)/shard_map/pallas_call | solution.py:260
  15.8 1.5 %collective-permute-done.4.refs_1_ = bf16[4,128,256]{2,1,0:T(8,128)(2,1)S(1)} collective-permute-done((bf16[4,128,256]{2,1,0:T(8,128)(2,1)S(1)}, bf16[4,128,256]{2,1,0:T(8,128)(2,1)S(1)}, u32[]{:S(2)}, u32[]{:S(2)}) %collective-permute-start.4) | collective-permute-done | bytes 262176 | tf_op jit(solution)/shard_map/ppermute | solution.py:27
  17.3 1.0 %collective-permute-done.3.refs_0_ = bf16[4,128,256]{2,1,0:T(8,128)(2,1)S(1)} collective-permute-done((bf16[4,128,256]{2,1,0:T(8,128)(2,1)S(1)}, bf16[4,128,256]{2,1,0:T(8,128)(2,1)S(1)}, u32[]{:S(2)}, u32[]{:S(2)}) %collective-permute-start.3) | collective-permute-done | bytes 262176 | tf_op jit(solution)/shard_map/ppermute | solution.py:27
  18.3 0.9 %shard_map.41 = (f32[256,256]{1,0:T(8,128)S(1)}, bf16[256,1024]{1,0:T(8,128)(2,1)S(1)}, bf16[256,1024]{1,0:T(8,128)(2,1)S(1)}, f32[1,512,256]{2,1,0:T(8,128)S(1)}, bf16[256,256]{1,0:T(8,128)(2,1)S(1)}) custom-call(bf16[4,128,256]{2,1,0:T(8,128)(2,1)S(1)} %collective-permute-done.3.refs_0_, bf16[4,128,256]{2,1,0:T(8,128)(2,1)S(1)} %collective-permute-done.4.refs_1_, ...), custom_call_target="tpu_custom_call" | custom-call | flops 1 | bytes 1 | tf_op jit(solution)/shard_map/pallas_call | solution.py:272
  19.2 3.0 %collective-permute-done.2.refs_0_ = bf16[4,128,256]{2,1,0:T(8,128)(2,1)S(1)} collective-permute-done((bf16[4,128,256]{2,1,0:T(8,128)(2,1)S(1)}, bf16[4,128,256]{2,1,0:T(8,128)(2,1)S(1)}, u32[]{:S(2)}, u32[]{:S(2)}) %collective-permute-start.2) | collective-permute-done | bytes 262176 | tf_op jit(solution)/shard_map/ppermute | solution.py:27
  22.1 0.6 %shard_map.42 = (f32[4,64,128]{2,1,0:T(8,128)S(1)}, f32[4,64,128]{2,1,0:T(8,128)S(1)}) custom-call(bf16[4,128,256]{2,1,0:T(8,128)(2,1)S(1)} %collective-permute-done.2.refs_0_, f32[256,256]{1,0:T(8,128)S(1)} %get-tuple-element.40.refs_1_, bf16[256,1024]{1,0:T(8,128)(2,1)S(1)} %get-tuple-element.41.refs_2_, bf16[256,1024]{1,0:T(8,128)(2,1)S(1)} %get-tuple-element.42.refs_3_, ...), custom_call_target="tpu_custom_call" | custom-call | flops 1 | bytes 1 | tf_op jit(solution)/shard_map/pallas_call | solution.py:286
  22.9 1.3 %collective-permute-done.6 = f32[4,64,128]{2,1,0:T(8,128)S(1)} collective-permute-done((f32[4,64,128]{2,1,0:T(8,128)S(1)}, f32[4,64,128]{2,1,0:T(8,128)S(1)}, u32[]{:S(2)}, u32[]{:S(2)}) %collective-permute-start.6) | collective-permute-done | bytes 131104 | tf_op jit(solution)/shard_map/ppermute | solution.py:27
  24.2 0.7 %collective-permute-start.10 = (f32[64,128]{1,0:T(8,128)S(1)}, f32[64,128]{1,0:T(8,128)S(1)}, u32[]{:S(2)}, u32[]{:S(2)}) collective-permute-start(f32[64,128]{1,0:T(8,128)S(1)} %get-tuple-element.50), channel_id=1, source_target_pairs={{8,15},{9,14},{10,13},{11,12},{12,11},{13,10},{14,9},{15,8},{24,31... | collective-permute-start | bytes 98312 | tf_op jit(solution)/shard_map/ppermute | solution.py:27
  25.0 1.6 %collective-permute-start.8 = (f32[64,128]{1,0:T(8,128)S(1)}, f32[64,128]{1,0:T(8,128)S(1)}, u32[]{:S(2)}, u32[]{:S(2)}) collective-permute-start(f32[64,128]{1,0:T(8,128)S(1)} %get-tuple-element.49), channel_id=1, source_target_pairs={{0,2},{1,3},{2,0},{3,1},{4,6},{5,7},{6,4},{7,5},{8,13},{9,12},{10,... | collective-permute-start | bytes 98312 | tf_op jit(solution)/shard_map/ppermute | solution.py:27
  26.6 2.8 %collective-permute-start.9 = (f32[64,128]{1,0:T(8,128)S(1)}, f32[64,128]{1,0:T(8,128)S(1)}, u32[]{:S(2)}, u32[]{:S(2)}) collective-permute-start(f32[64,128]{1,0:T(8,128)S(1)} %get-tuple-element.48), channel_id=1, source_target_pairs={{0,3},{1,2},{2,1},{3,0},{4,7},{5,6},{6,5},{7,4},{8,14},{9,15},{10,... | collective-permute-start | bytes 98312 | tf_op jit(solution)/shard_map/ppermute | solution.py:27
  29.9 2.8 %collective-permute-done.9 = f32[64,128]{1,0:T(8,128)S(1)} collective-permute-done((f32[64,128]{1,0:T(8,128)S(1)}, f32[64,128]{1,0:T(8,128)S(1)}, u32[]{:S(2)}, u32[]{:S(2)}) %collective-permute-start.9) | collective-permute-done | bytes 32800 | tf_op jit(solution)/shard_map/ppermute | solution.py:27
  32.7 1.6 %collective-permute-start.11 = (f32[64,128]{1,0:T(8,128)S(1)}, f32[64,128]{1,0:T(8,128)S(1)}, u32[]{:S(2)}, u32[]{:S(2)}) collective-permute-start(f32[64,128]{1,0:T(8,128)S(1)} %add_add_fusion), channel_id=1, source_target_pairs={{0,16},{1,17},{2,18},{3,19},{4,20},{5,21},{6,22},{7,23},{8,24},{9,... | collective-permute-start | bytes 98312 | tf_op jit(solution)/shard_map/ppermute | solution.py:27
  34.2 2.5 %collective-permute-done.11 = f32[64,128]{1,0:T(8,128)S(1)} collective-permute-done((f32[64,128]{1,0:T(8,128)S(1)}, f32[64,128]{1,0:T(8,128)S(1)}, u32[]{:S(2)}, u32[]{:S(2)}) %collective-permute-start.11) | collective-permute-done | bytes 32800 | tf_op jit(solution)/shard_map/ppermute | solution.py:27
  36.7 1.2 %collective-permute-done.12 = f32[64,128]{1,0:T(8,128)S(1)} collective-permute-done((f32[64,128]{1,0:T(8,128)S(1)}, f32[64,128]{1,0:T(8,128)S(1)}, u32[]{:S(2)}, u32[]{:S(2)}) %collective-permute-start.12) | collective-permute-done | bytes 32800 | tf_op jit(solution)/shard_map/ppermute | solution.py:27
  37.9 0.6 %add.27 = f32[64,128]{1,0:T(8,128)} add(f32[64,128]{1,0:T(8,128)S(1)} %add.26, f32[64,128]{1,0:T(8,128)S(1)} %collective-permute-done.12) | non-fusion elementwise | flops 8192 | bytes 98304 | tf_op jit(solution)/shard_map/add | solution.py:305
  (19 shorter events, 0.8 us)
Async XLA Ops:
  0.0 4.5 %copy-start = (bf16[512,5,128]{2,0,1:T(8,128)(2,1)S(1)}, bf16[512,5,128]{2,0,1:T(8,128)(2,1)}, u32[]{:S(2)}) copy-start(bf16[512,5,128]{2,0,1:T(8,128)(2,1)} %param.4) | copy-start | bytes 1966084
  0.0 1.3 %copy-start.1 = (bf16[8,128,512]{2,1,0:T(8,128)(2,1)S(1)}, bf16[8,128,512]{2,1,0:T(8,128)(2,1)}, u32[]{:S(2)}) copy-start(bf16[8,128,512]{2,1,0:T(8,128)(2,1)} %tensor_ref.1) | copy-start | bytes 3145732
  1.4 3.0 %copy-start.2 = (s32[4,5]{1,0:T(4,128)S(1)}, s32[4,5]{1,0:T(4,128)}, u32[]{:S(2)}) copy-start(s32[4,5]{1,0:T(4,128)} %mask_ref.3) | copy-start | bytes 244
  1.4 9.3 %collective-permute-start = (bf16[4,128,256]{2,1,0:T(8,128)(2,1)S(1)}, bf16[4,128,256]{2,1,0:T(8,128)(2,1)S(1)}, u32[]{:S(2)}, u32[]{:S(2)}) collective-permute-start(bf16[4,128,256]{2,1,0:T(8,128)(2,1)S(1)} %get-tuple-element.26), channel_id=1, source_target_pairs={{0,4},{1,5},{2,6},{3,7},{4,0},{5,1},{6,2},{7,3},{8,12},{9,13},{10,... | collective-permute-start | bytes 786440 | tf_op jit(solution)/shard_map/ppermute | solution.py:27
  5.1 7.4 %collective-permute-start.1 = (bf16[192,128]{1,0:T(8,128)(2,1)S(1)}, bf16[192,128]{1,0:T(8,128)(2,1)S(1)}, u32[]{:S(2)}, u32[]{:S(2)}) collective-permute-start(bf16[192,128]{1,0:T(8,128)(2,1)S(1)} %shard_map.38), channel_id=1, source_target_pairs={{0,1},{1,2},{2,3},{3,0},{4,5},{5,6},{6,7},{7,4},{8,9},{9,10},{10,1... | collective-permute-start | bytes 147464 | tf_op jit(solution)/shard_map/ppermute | solution.py:27
  6.7 10.6 %collective-permute-start.4 = (bf16[4,128,256]{2,1,0:T(8,128)(2,1)S(1)}, bf16[4,128,256]{2,1,0:T(8,128)(2,1)S(1)}, u32[]{:S(2)}, u32[]{:S(2)}) collective-permute-start(bf16[4,128,256]{2,1,0:T(8,128)(2,1)S(1)} %get-tuple-element.30), channel_id=1, source_target_pairs={{0,1},{1,2},{2,3},{3,0},{4,5},{5,6},{6,7},{7,4},{8,9},{9,10},{10,1... | collective-permute-start | bytes 786440 | tf_op jit(solution)/shard_map/ppermute | solution.py:27
  10.8 7.5 %collective-permute-start.3 = (bf16[4,128,256]{2,1,0:T(8,128)(2,1)S(1)}, bf16[4,128,256]{2,1,0:T(8,128)(2,1)S(1)}, u32[]{:S(2)}, u32[]{:S(2)}) collective-permute-start(bf16[4,128,256]{2,1,0:T(8,128)(2,1)S(1)} %get-tuple-element.29), channel_id=1, source_target_pairs={{0,4},{1,5},{2,6},{3,7},{4,0},{5,1},{6,2},{7,3},{8,12},{9,13},{10,... | collective-permute-start | bytes 786440 | tf_op jit(solution)/shard_map/ppermute | solution.py:27
  12.5 9.6 %collective-permute-start.2 = (bf16[4,128,256]{2,1,0:T(8,128)(2,1)S(1)}, bf16[4,128,256]{2,1,0:T(8,128)(2,1)S(1)}, u32[]{:S(2)}, u32[]{:S(2)}) collective-permute-start(bf16[4,128,256]{2,1,0:T(8,128)(2,1)S(1)} %collective-permute-done.refs_1_), channel_id=1, source_target_pairs={{0,1},{1,2},{2,3},{3,0},{4,5},{5,6},{6,7},{7,4},{8,9},{9,10},{10,1... | collective-permute-start | bytes 786440 | tf_op jit(solution)/shard_map/ppermute | solution.py:27
  14.1 1.7 %collective-permute-start.5 = (bf16[192,128]{1,0:T(8,128)(2,1)S(1)}, bf16[192,128]{1,0:T(8,128)(2,1)S(1)}, u32[]{:S(2)}, u32[]{:S(2)}) collective-permute-start(bf16[192,128]{1,0:T(8,128)(2,1)S(1)} %collective-permute-done.1.refs_2_), channel_id=1, source_target_pairs={{0,8},{1,9},{2,10},{3,11},{4,12},{5,13},{6,14},{7,15},{8,0},{9,1},... | collective-permute-start | bytes 147464 | tf_op jit(solution)/shard_map/ppermute | solution.py:27
  22.8 1.4 %collective-permute-start.6 = (f32[4,64,128]{2,1,0:T(8,128)S(1)}, f32[4,64,128]{2,1,0:T(8,128)S(1)}, u32[]{:S(2)}, u32[]{:S(2)}) collective-permute-start(f32[4,64,128]{2,1,0:T(8,128)S(1)} %get-tuple-element.46), channel_id=1, source_target_pairs={{0,8},{1,9},{2,10},{3,11},{4,12},{5,13},{6,14},{7,15},{8,0},{9,1},... | collective-permute-start | bytes 393224 | tf_op jit(solution)/shard_map/ppermute | solution.py:27
  24.2 5.1 %collective-permute-start.10 = (f32[64,128]{1,0:T(8,128)S(1)}, f32[64,128]{1,0:T(8,128)S(1)}, u32[]{:S(2)}, u32[]{:S(2)}) collective-permute-start(f32[64,128]{1,0:T(8,128)S(1)} %get-tuple-element.50), channel_id=1, source_target_pairs={{8,15},{9,14},{10,13},{11,12},{12,11},{13,10},{14,9},{15,8},{24,31... | collective-permute-start | bytes 98312 | tf_op jit(solution)/shard_map/ppermute | solution.py:27
  24.9 4.5 %collective-permute-start.7 = (f32[64,128]{1,0:T(8,128)S(1)}, f32[64,128]{1,0:T(8,128)S(1)}, u32[]{:S(2)}, u32[]{:S(2)}) collective-permute-start(f32[64,128]{1,0:T(8,128)S(1)} %get-tuple-element.47), channel_id=1, source_target_pairs={{0,1},{1,0},{2,3},{3,2},{4,5},{5,4},{6,7},{7,6},{8,12},{9,13},{10,... | collective-permute-start | bytes 98312 | tf_op jit(solution)/shard_map/ppermute | solution.py:27
  25.0 4.9 %collective-permute-start.8 = (f32[64,128]{1,0:T(8,128)S(1)}, f32[64,128]{1,0:T(8,128)S(1)}, u32[]{:S(2)}, u32[]{:S(2)}) collective-permute-start(f32[64,128]{1,0:T(8,128)S(1)} %get-tuple-element.49), channel_id=1, source_target_pairs={{0,2},{1,3},{2,0},{3,1},{4,6},{5,7},{6,4},{7,5},{8,13},{9,12},{10,... | collective-permute-start | bytes 98312 | tf_op jit(solution)/shard_map/ppermute | solution.py:27
  26.6 6.1 %collective-permute-start.9 = (f32[64,128]{1,0:T(8,128)S(1)}, f32[64,128]{1,0:T(8,128)S(1)}, u32[]{:S(2)}, u32[]{:S(2)}) collective-permute-start(f32[64,128]{1,0:T(8,128)S(1)} %get-tuple-element.48), channel_id=1, source_target_pairs={{0,3},{1,2},{2,1},{3,0},{4,7},{5,6},{6,5},{7,4},{8,14},{9,15},{10,... | collective-permute-start | bytes 98312 | tf_op jit(solution)/shard_map/ppermute | solution.py:27
  32.7 4.0 %collective-permute-start.11 = (f32[64,128]{1,0:T(8,128)S(1)}, f32[64,128]{1,0:T(8,128)S(1)}, u32[]{:S(2)}, u32[]{:S(2)}) collective-permute-start(f32[64,128]{1,0:T(8,128)S(1)} %add_add_fusion), channel_id=1, source_target_pairs={{0,16},{1,17},{2,18},{3,19},{4,20},{5,21},{6,22},{7,23},{8,24},{9,... | collective-permute-start | bytes 98312 | tf_op jit(solution)/shard_map/ppermute | solution.py:27
  36.7 1.2 %collective-permute-start.12 = (f32[64,128]{1,0:T(8,128)S(1)}, f32[64,128]{1,0:T(8,128)S(1)}, u32[]{:S(2)}, u32[]{:S(2)}) collective-permute-start(f32[64,128]{1,0:T(8,128)S(1)} %add.26), channel_id=1, source_target_pairs={{0,8},{1,9},{2,10},{3,11},{4,12},{5,13},{6,14},{7,15},{8,0},{9,1},... | collective-permute-start | bytes 98312 | tf_op jit(solution)/shard_map/ppermute | solution.py:27

commit v6 on v5

--- a/solution.py
+++ b/solution.py
@@ -32,10 +32,16 @@
 
 
 def owned(rows, cols):
-    offsets = [(a, b) for a in range(rows) for b in range(cols)]
-    half = len(offsets) // 2
-    first = offsets[1:half] + offsets[:1]
-    return first, offsets[half:]
+    sides = ([], [])
+    for a in range(rows):
+        for b in range(cols):
+            sides[b if b < 2 else (a + b + 1) % 2].append((a, b))
+    plan = []
+    for side in sides:
+        side = sorted(side, key=lambda at: (at[0] + at[1], at[0]))
+        far = min(side, key=lambda at: (-at[0] - at[1], at[0]))
+        plan.append([far] + [at for at in side if at != far])
+    return plan
 
 
 def times(a, b):
@@ -292,7 +298,7 @@
 
     got = move(give, sizes, lambda i, j, k: (i ^ 1, j, k))
     pieces = keep + got
-    total = jnp.where(core == 0, pieces[half - 1], 0.0)
+    total = jnp.where(core == 0, pieces[plan[0].index((0, 0))], 0.0)
     for n, (zero, one) in enumerate(zip(*plan)):
         def target(i, j, k):
             dr, dc = one if i % 2 else zero

time: 38.7 us -> 37.2 us (0.961)
  waiting for transfers between devices: 16.2 us -> 15.2 us
  starting transfers between devices: 16.3 us -> 15.9 us
    ppermute x13, waiting for transfers between devices: 16.2 us -> 15.2 us  [move(): return lax.ppermute(value, AXES, pairs)]
    ppermute x13, starting transfers between devices: 16.3 us -> 15.9 us  [move(): return lax.ppermute(value, AXES, pairs)]
  transfers between devices with their start and end apart: 13 -> 13, of which waited for: 9 -> 10; matrix products, arithmetic and copies ran while one was open for 0% -> 0% of each run, Pallas kernels for 8% -> 8%
where the time goes in v6:
time: 37.2 us; the launch traced here: 37.1 us
  starting transfers between devices  15.9 us (43%)
  waiting for transfers between devices  15.2 us (41%)
  Pallas kernels  3.89 us (10%)
  local copies, waits for them, and re-layouts  1.31 us (4%)
  other arithmetic  0.66 us (2%)
    ppermute x13, starting transfers between devices, move(): return lax.ppermute(value, AXES, pairs)  15.9 us
    ppermute x13, waiting for transfers between devices, move(): return lax.ppermute(value, AXES, pairs)  15.2 us
    unnamed x6, local copies, waits for them, and re-layouts  1.3 us
    pallas_call x1, Pallas kernels, per_device(): kernel(functools.partial(own_kernel, n_row), [array((whole, rows), F32),...  0.93 us
    pallas_call x1, Pallas kernels, per_device(): kernel(functools.partial(inner_kernel, n_row, centre), [array((whole, who...  0.88 us
  transfers between devices with their start and end apart: 13, of which 10 were waited for; matrix products, arithmetic and copies ran while one was open for 0% of the time, Pallas kernels for 8%

profile of v6, /device:TPU:0, one launch (start us, length us, event | category | flops | bytes accessed | tf_op | source)
XLA Modules:
  0.0 37.1 jit_solution(4220993285166407709)
XLA Ops:
  0.0 1.3 %copy-done.1 = bf16[8,128,512]{2,1,0:T(8,128)(2,1)S(1)} copy-done((bf16[8,128,512]{2,1,0:T(8,128)(2,1)S(1)}, bf16[8,128,512]{2,1,0:T(8,128)(2,1)}, u32[]{:S(2)}) %copy-start.1) | copy-done | bytes 1048600
  1.4 3.0 %collective-permute-start = (bf16[4,128,256]{2,1,0:T(8,128)(2,1)S(1)}, bf16[4,128,256]{2,1,0:T(8,128)(2,1)S(1)}, u32[]{:S(2)}, u32[]{:S(2)}) collective-permute-start(bf16[4,128,256]{2,1,0:T(8,128)(2,1)S(1)} %get-tuple-element.26), channel_id=1, source_target_pairs={{0,4},{1,5},{2,6},{3,7},{4,0},{5,1},{6,2},{7,3},{8,12},{9,13},{10,... | collective-permute-start | bytes 786440 | tf_op jit(solution)/shard_map/ppermute | solution.py:27
  5.1 1.6 %collective-permute-start.1 = (bf16[192,128]{1,0:T(8,128)(2,1)S(1)}, bf16[192,128]{1,0:T(8,128)(2,1)S(1)}, u32[]{:S(2)}, u32[]{:S(2)}) collective-permute-start(bf16[192,128]{1,0:T(8,128)(2,1)S(1)} %shard_map.38), channel_id=1, source_target_pairs={{0,1},{1,2},{2,3},{3,0},{4,5},{5,6},{6,7},{7,4},{8,9},{9,10},{10,1... | collective-permute-start | bytes 147464 | tf_op jit(solution)/shard_map/ppermute | solution.py:27
  6.7 1.6 %collective-permute-start.4 = (bf16[4,128,256]{2,1,0:T(8,128)(2,1)S(1)}, bf16[4,128,256]{2,1,0:T(8,128)(2,1)S(1)}, u32[]{:S(2)}, u32[]{:S(2)}) collective-permute-start(bf16[4,128,256]{2,1,0:T(8,128)(2,1)S(1)} %get-tuple-element.30), channel_id=1, source_target_pairs={{0,1},{1,2},{2,3},{3,0},{4,5},{5,6},{6,7},{7,4},{8,9},{9,10},{10,1... | collective-permute-start | bytes 786440 | tf_op jit(solution)/shard_map/ppermute | solution.py:27
  8.3 2.5 %collective-permute-done.refs_1_ = bf16[4,128,256]{2,1,0:T(8,128)(2,1)S(1)} collective-permute-done((bf16[4,128,256]{2,1,0:T(8,128)(2,1)S(1)}, bf16[4,128,256]{2,1,0:T(8,128)(2,1)S(1)}, u32[]{:S(2)}, u32[]{:S(2)}) %collective-permute-start) | collective-permute-done | bytes 262176 | tf_op jit(solution)/shard_map/ppermute | solution.py:27
  10.8 1.7 %collective-permute-start.3 = (bf16[4,128,256]{2,1,0:T(8,128)(2,1)S(1)}, bf16[4,128,256]{2,1,0:T(8,128)(2,1)S(1)}, u32[]{:S(2)}, u32[]{:S(2)}) collective-permute-start(bf16[4,128,256]{2,1,0:T(8,128)(2,1)S(1)} %get-tuple-element.29), channel_id=1, source_target_pairs={{0,4},{1,5},{2,6},{3,7},{4,0},{5,1},{6,2},{7,3},{8,12},{9,13},{10,... | collective-permute-start | bytes 786440 | tf_op jit(solution)/shard_map/ppermute | solution.py:27
  12.5 1.6 %collective-permute-start.2 = (bf16[4,128,256]{2,1,0:T(8,128)(2,1)S(1)}, bf16[4,128,256]{2,1,0:T(8,128)(2,1)S(1)}, u32[]{:S(2)}, u32[]{:S(2)}) collective-permute-start(bf16[4,128,256]{2,1,0:T(8,128)(2,1)S(1)} %collective-permute-done.refs_1_), channel_id=1, source_target_pairs={{0,1},{1,2},{2,3},{3,0},{4,5},{5,6},{6,7},{7,4},{8,9},{9,10},{10,1... | collective-permute-start | bytes 786440 | tf_op jit(solution)/shard_map/ppermute | solution.py:27
  14.1 0.7 %shard_map.39 = (bf16[512,512]{1,0:T(8,128)(2,1)S(1)}, bf16[256,256]{1,0:T(8,128)(2,1)S(1)}) custom-call(s32[4,5]{1,0:T(4,128)S(1)} %copy-done.2, bf16[5,512,128]{2,1,0:T(8,128)(2,1)S(1)} %bitcast.12), custom_call_target="tpu_custom_call" | custom-call | flops 1 | bytes 1 | tf_op jit(solution)/shard_map/pallas_call | solution.py:253
  14.8 0.9 %shard_map.40 = (f32[256,128]{1,0:T(8,128)S(1)}, bf16[128,1024]{1,0:T(8,128)(2,1)S(1)}, bf16[128,1024]{1,0:T(8,128)(2,1)S(1)}, f32[512,256]{1,0:T(8,128)S(1)}, b...) custom-call(bf16[4,128,512]{2,1,0:T(8,128)(2,1)S(1)} %get-tuple-element.33.refs_0_, ...), custom_call_target="tpu_custom_call" | custom-call | flops 1 | bytes 1 | tf_op jit(solution)/shard_map/pallas_call | solution.py:266
  15.8 1.5 %collective-permute-done.4.refs_1_ = bf16[4,128,256]{2,1,0:T(8,128)(2,1)S(1)} collective-permute-done((bf16[4,128,256]{2,1,0:T(8,128)(2,1)S(1)}, bf16[4,128,256]{2,1,0:T(8,128)(2,1)S(1)}, u32[]{:S(2)}, u32[]{:S(2)}) %collective-permute-start.4) | collective-permute-done | bytes 262176 | tf_op jit(solution)/shard_map/ppermute | solution.py:27
  17.3 1.0 %collective-permute-done.3.refs_0_ = bf16[4,128,256]{2,1,0:T(8,128)(2,1)S(1)} collective-permute-done((bf16[4,128,256]{2,1,0:T(8,128)(2,1)S(1)}, bf16[4,128,256]{2,1,0:T(8,128)(2,1)S(1)}, u32[]{:S(2)}, u32[]{:S(2)}) %collective-permute-start.3) | collective-permute-done | bytes 262176 | tf_op jit(solution)/shard_map/ppermute | solution.py:27
  18.3 0.9 %shard_map.41 = (f32[256,256]{1,0:T(8,128)S(1)}, bf16[256,1024]{1,0:T(8,128)(2,1)S(1)}, bf16[256,1024]{1,0:T(8,128)(2,1)S(1)}, f32[1,512,256]{2,1,0:T(8,128)S(1)}, bf16[256,256]{1,0:T(8,128)(2,1)S(1)}) custom-call(bf16[4,128,256]{2,1,0:T(8,128)(2,1)S(1)} %collective-permute-done.3.refs_0_, bf16[4,128,256]{2,1,0:T(8,128)(2,1)S(1)} %collective-permute-done.4.refs_1_, ...), custom_call_target="tpu_custom_call" | custom-call | flops 1 | bytes 1 | tf_op jit(solution)/shard_map/pallas_call | solution.py:278
  19.2 3.0 %collective-permute-done.2.refs_0_ = bf16[4,128,256]{2,1,0:T(8,128)(2,1)S(1)} collective-permute-done((bf16[4,128,256]{2,1,0:T(8,128)(2,1)S(1)}, bf16[4,128,256]{2,1,0:T(8,128)(2,1)S(1)}, u32[]{:S(2)}, u32[]{:S(2)}) %collective-permute-start.2) | collective-permute-done | bytes 262176 | tf_op jit(solution)/shard_map/ppermute | solution.py:27
  22.1 0.6 %shard_map.42 = (f32[4,64,128]{2,1,0:T(8,128)S(1)}, f32[4,64,128]{2,1,0:T(8,128)S(1)}) custom-call(bf16[4,128,256]{2,1,0:T(8,128)(2,1)S(1)} %collective-permute-done.2.refs_0_, f32[256,256]{1,0:T(8,128)S(1)} %get-tuple-element.40.refs_1_, bf16[256,1024]{1,0:T(8,128)(2,1)S(1)} %get-tuple-element.41.refs_2_, bf16[256,1024]{1,0:T(8,128)(2,1)S(1)} %get-tuple-element.42.refs_3_, ...), custom_call_target="tpu_custom_call" | custom-call | flops 1 | bytes 1 | tf_op jit(solution)/shard_map/pallas_call | solution.py:292
  22.9 1.3 %collective-permute-done.6 = f32[4,64,128]{2,1,0:T(8,128)S(1)} collective-permute-done((f32[4,64,128]{2,1,0:T(8,128)S(1)}, f32[4,64,128]{2,1,0:T(8,128)S(1)}, u32[]{:S(2)}, u32[]{:S(2)}) %collective-permute-start.6) | collective-permute-done | bytes 131104 | tf_op jit(solution)/shard_map/ppermute | solution.py:27
  24.2 1.0 %collective-permute-start.10 = (f32[64,128]{1,0:T(8,128)S(1)}, f32[64,128]{1,0:T(8,128)S(1)}, u32[]{:S(2)}, u32[]{:S(2)}) collective-permute-start(f32[64,128]{1,0:T(8,128)S(1)} %get-tuple-element.48), channel_id=1, source_target_pairs={{0,6},{1,7},{2,4},{3,5},{4,2},{5,3},{6,0},{7,1},{8,13},{9,12},{10,... | collective-permute-start | bytes 98312 | tf_op jit(solution)/shard_map/ppermute | solution.py:27
  25.3 1.3 %collective-permute-start.7 = (f32[64,128]{1,0:T(8,128)S(1)}, f32[64,128]{1,0:T(8,128)S(1)}, u32[]{:S(2)}, u32[]{:S(2)}) collective-permute-start(f32[64,128]{1,0:T(8,128)S(1)} %get-tuple-element.47), channel_id=1, source_target_pairs={{0,3},{1,2},{2,1},{3,0},{4,7},{5,6},{6,5},{7,4},{8,15},{9,14},{10,... | collective-permute-start | bytes 98312 | tf_op jit(solution)/shard_map/ppermute | solution.py:27
  26.6 0.7 %collective-permute-start.8 = (f32[64,128]{1,0:T(8,128)S(1)}, f32[64,128]{1,0:T(8,128)S(1)}, u32[]{:S(2)}, u32[]{:S(2)}) collective-permute-start(f32[64,128]{1,0:T(8,128)S(1)} %get-tuple-element.50), channel_id=1, source_target_pairs={{8,9},{9,8},{10,11},{11,10},{12,13},{13,12},{14,15},{15,14},{24,25... | collective-permute-start | bytes 98312 | tf_op jit(solution)/shard_map/ppermute | solution.py:27
  27.3 1.4 %collective-permute-start.9 = (f32[64,128]{1,0:T(8,128)S(1)}, f32[64,128]{1,0:T(8,128)S(1)}, u32[]{:S(2)}, u32[]{:S(2)}) collective-permute-start(f32[64,128]{1,0:T(8,128)S(1)} %get-tuple-element.49), channel_id=1, source_target_pairs={{0,4},{1,5},{2,6},{3,7},{4,0},{5,1},{6,2},{7,3},{8,10},{9,11},{10,... | collective-permute-start | bytes 98312 | tf_op jit(solution)/shard_map/ppermute | solution.py:27
  28.6 1.7 %collective-permute-done.10 = f32[64,128]{1,0:T(8,128)S(1)} collective-permute-done((f32[64,128]{1,0:T(8,128)S(1)}, f32[64,128]{1,0:T(8,128)S(1)}, u32[]{:S(2)}, u32[]{:S(2)}) %collective-permute-start.10) | collective-permute-done | bytes 32800 | tf_op jit(solution)/shard_map/ppermute | solution.py:27
  31.3 1.6 %collective-permute-start.11 = (f32[64,128]{1,0:T(8,128)S(1)}, f32[64,128]{1,0:T(8,128)S(1)}, u32[]{:S(2)}, u32[]{:S(2)}) collective-permute-start(f32[64,128]{1,0:T(8,128)S(1)} %add_add_fusion), channel_id=1, source_target_pairs={{0,16},{1,17},{2,18},{3,19},{4,20},{5,21},{6,22},{7,23},{8,24},{9,... | collective-permute-start | bytes 98312 | tf_op jit(solution)/shard_map/ppermute | solution.py:27
  32.8 2.4 %collective-permute-done.11 = f32[64,128]{1,0:T(8,128)S(1)} collective-permute-done((f32[64,128]{1,0:T(8,128)S(1)}, f32[64,128]{1,0:T(8,128)S(1)}, u32[]{:S(2)}, u32[]{:S(2)}) %collective-permute-start.11) | collective-permute-done | bytes 32800 | tf_op jit(solution)/shard_map/ppermute | solution.py:27
  35.5 0.9 %collective-permute-done.12 = f32[64,128]{1,0:T(8,128)S(1)} collective-permute-done((f32[64,128]{1,0:T(8,128)S(1)}, f32[64,128]{1,0:T(8,128)S(1)}, u32[]{:S(2)}, u32[]{:S(2)}) %collective-permute-start.12) | collective-permute-done | bytes 32800 | tf_op jit(solution)/shard_map/ppermute | solution.py:27
  36.5 0.6 %add.27 = f32[64,128]{1,0:T(8,128)} add(f32[64,128]{1,0:T(8,128)S(1)} %add.26, f32[64,128]{1,0:T(8,128)S(1)} %collective-permute-done.12) | non-fusion elementwise | flops 8192 | bytes 98304 | tf_op jit(solution)/shard_map/add | solution.py:311
  (19 shorter events, 2.0 us)
Async XLA Ops:
  0.0 4.5 %copy-start = (bf16[512,5,128]{2,0,1:T(8,128)(2,1)S(1)}, bf16[512,5,128]{2,0,1:T(8,128)(2,1)}, u32[]{:S(2)}) copy-start(bf16[512,5,128]{2,0,1:T(8,128)(2,1)} %param.4) | copy-start | bytes 1966084
  0.0 1.3 %copy-start.1 = (bf16[8,128,512]{2,1,0:T(8,128)(2,1)S(1)}, bf16[8,128,512]{2,1,0:T(8,128)(2,1)}, u32[]{:S(2)}) copy-start(bf16[8,128,512]{2,1,0:T(8,128)(2,1)} %tensor_ref.1) | copy-start | bytes 3145732
  1.4 3.0 %copy-start.2 = (s32[4,5]{1,0:T(4,128)S(1)}, s32[4,5]{1,0:T(4,128)}, u32[]{:S(2)}) copy-start(s32[4,5]{1,0:T(4,128)} %mask_ref.3) | copy-start | bytes 244
  1.4 9.3 %collective-permute-start = (bf16[4,128,256]{2,1,0:T(8,128)(2,1)S(1)}, bf16[4,128,256]{2,1,0:T(8,128)(2,1)S(1)}, u32[]{:S(2)}, u32[]{:S(2)}) collective-permute-start(bf16[4,128,256]{2,1,0:T(8,128)(2,1)S(1)} %get-tuple-element.26), channel_id=1, source_target_pairs={{0,4},{1,5},{2,6},{3,7},{4,0},{5,1},{6,2},{7,3},{8,12},{9,13},{10,... | collective-permute-start | bytes 786440 | tf_op jit(solution)/shard_map/ppermute | solution.py:27
  5.1 7.4 %collective-permute-start.1 = (bf16[192,128]{1,0:T(8,128)(2,1)S(1)}, bf16[192,128]{1,0:T(8,128)(2,1)S(1)}, u32[]{:S(2)}, u32[]{:S(2)}) collective-permute-start(bf16[192,128]{1,0:T(8,128)(2,1)S(1)} %shard_map.38), channel_id=1, source_target_pairs={{0,1},{1,2},{2,3},{3,0},{4,5},{5,6},{6,7},{7,4},{8,9},{9,10},{10,1... | collective-permute-start | bytes 147464 | tf_op jit(solution)/shard_map/ppermute | solution.py:27
  6.7 10.6 %collective-permute-start.4 = (bf16[4,128,256]{2,1,0:T(8,128)(2,1)S(1)}, bf16[4,128,256]{2,1,0:T(8,128)(2,1)S(1)}, u32[]{:S(2)}, u32[]{:S(2)}) collective-permute-start(bf16[4,128,256]{2,1,0:T(8,128)(2,1)S(1)} %get-tuple-element.30), channel_id=1, source_target_pairs={{0,1},{1,2},{2,3},{3,0},{4,5},{5,6},{6,7},{7,4},{8,9},{9,10},{10,1... | collective-permute-start | bytes 786440 | tf_op jit(solution)/shard_map/ppermute | solution.py:27
  10.8 7.5 %collective-permute-start.3 = (bf16[4,128,256]{2,1,0:T(8,128)(2,1)S(1)}, bf16[4,128,256]{2,1,0:T(8,128)(2,1)S(1)}, u32[]{:S(2)}, u32[]{:S(2)}) collective-permute-start(bf16[4,128,256]{2,1,0:T(8,128)(2,1)S(1)} %get-tuple-element.29), channel_id=1, source_target_pairs={{0,4},{1,5},{2,6},{3,7},{4,0},{5,1},{6,2},{7,3},{8,12},{9,13},{10,... | collective-permute-start | bytes 786440 | tf_op jit(solution)/shard_map/ppermute | solution.py:27
  12.5 9.6 %collective-permute-start.2 = (bf16[4,128,256]{2,1,0:T(8,128)(2,1)S(1)}, bf16[4,128,256]{2,1,0:T(8,128)(2,1)S(1)}, u32[]{:S(2)}, u32[]{:S(2)}) collective-permute-start(bf16[4,128,256]{2,1,0:T(8,128)(2,1)S(1)} %collective-permute-done.refs_1_), channel_id=1, source_target_pairs={{0,1},{1,2},{2,3},{3,0},{4,5},{5,6},{6,7},{7,4},{8,9},{9,10},{10,1... | collective-permute-start | bytes 786440 | tf_op jit(solution)/shard_map/ppermute | solution.py:27
  14.1 1.7 %collective-permute-start.5 = (bf16[192,128]{1,0:T(8,128)(2,1)S(1)}, bf16[192,128]{1,0:T(8,128)(2,1)S(1)}, u32[]{:S(2)}, u32[]{:S(2)}) collective-permute-start(bf16[192,128]{1,0:T(8,128)(2,1)S(1)} %collective-permute-done.1.refs_2_), channel_id=1, source_target_pairs={{0,8},{1,9},{2,10},{3,11},{4,12},{5,13},{6,14},{7,15},{8,0},{9,1},... | collective-permute-start | bytes 147464 | tf_op jit(solution)/shard_map/ppermute | solution.py:27
  22.8 1.4 %collective-permute-start.6 = (f32[4,64,128]{2,1,0:T(8,128)S(1)}, f32[4,64,128]{2,1,0:T(8,128)S(1)}, u32[]{:S(2)}, u32[]{:S(2)}) collective-permute-start(f32[4,64,128]{2,1,0:T(8,128)S(1)} %get-tuple-element.46), channel_id=1, source_target_pairs={{0,8},{1,9},{2,10},{3,11},{4,12},{5,13},{6,14},{7,15},{8,0},{9,1},... | collective-permute-start | bytes 393224 | tf_op jit(solution)/shard_map/ppermute | solution.py:27
  24.2 6.1 %collective-permute-start.10 = (f32[64,128]{1,0:T(8,128)S(1)}, f32[64,128]{1,0:T(8,128)S(1)}, u32[]{:S(2)}, u32[]{:S(2)}) collective-permute-start(f32[64,128]{1,0:T(8,128)S(1)} %get-tuple-element.48), channel_id=1, source_target_pairs={{0,6},{1,7},{2,4},{3,5},{4,2},{5,3},{6,0},{7,1},{8,13},{9,12},{10,... | collective-permute-start | bytes 98312 | tf_op jit(solution)/shard_map/ppermute | solution.py:27
  25.3 5.7 %collective-permute-start.7 = (f32[64,128]{1,0:T(8,128)S(1)}, f32[64,128]{1,0:T(8,128)S(1)}, u32[]{:S(2)}, u32[]{:S(2)}) collective-permute-start(f32[64,128]{1,0:T(8,128)S(1)} %get-tuple-element.47), channel_id=1, source_target_pairs={{0,3},{1,2},{2,1},{3,0},{4,7},{5,6},{6,5},{7,4},{8,15},{9,14},{10,... | collective-permute-start | bytes 98312 | tf_op jit(solution)/shard_map/ppermute | solution.py:27
  26.6 4.4 %collective-permute-start.8 = (f32[64,128]{1,0:T(8,128)S(1)}, f32[64,128]{1,0:T(8,128)S(1)}, u32[]{:S(2)}, u32[]{:S(2)}) collective-permute-start(f32[64,128]{1,0:T(8,128)S(1)} %get-tuple-element.50), channel_id=1, source_target_pairs={{8,9},{9,8},{10,11},{11,10},{12,13},{13,12},{14,15},{15,14},{24,25... | collective-permute-start | bytes 98312 | tf_op jit(solution)/shard_map/ppermute | solution.py:27
  27.3 4.0 %collective-permute-start.9 = (f32[64,128]{1,0:T(8,128)S(1)}, f32[64,128]{1,0:T(8,128)S(1)}, u32[]{:S(2)}, u32[]{:S(2)}) collective-permute-start(f32[64,128]{1,0:T(8,128)S(1)} %get-tuple-element.49), channel_id=1, source_target_pairs={{0,4},{1,5},{2,6},{3,7},{4,0},{5,1},{6,2},{7,3},{8,10},{9,11},{10,... | collective-permute-start | bytes 98312 | tf_op jit(solution)/shard_map/ppermute | solution.py:27
  31.3 4.0 %collective-permute-start.11 = (f32[64,128]{1,0:T(8,128)S(1)}, f32[64,128]{1,0:T(8,128)S(1)}, u32[]{:S(2)}, u32[]{:S(2)}) collective-permute-start(f32[64,128]{1,0:T(8,128)S(1)} %add_add_fusion), channel_id=1, source_target_pairs={{0,16},{1,17},{2,18},{3,19},{4,20},{5,21},{6,22},{7,23},{8,24},{9,... | collective-permute-start | bytes 98312 | tf_op jit(solution)/shard_map/ppermute | solution.py:27
  35.2 1.2 %collective-permute-start.12 = (f32[64,128]{1,0:T(8,128)S(1)}, f32[64,128]{1,0:T(8,128)S(1)}, u32[]{:S(2)}, u32[]{:S(2)}) collective-permute-start(f32[64,128]{1,0:T(8,128)S(1)} %add.26), channel_id=1, source_target_pairs={{0,8},{1,9},{2,10},{3,11},{4,12},{5,13},{6,14},{7,15},{8,0},{9,1},... | collective-permute-start | bytes 98312 | tf_op jit(solution)/shard_map/ppermute | solution.py:27

commit v7 on v6

--- a/solution.py
+++ b/solution.py
@@ -54,8 +54,8 @@
 
 def masked(mask_ref, dens_ref, l, c):
     orb = dens_ref.shape[2]
-    block = dens_ref[c, l * orb : (l + 1) * orb, :]
-    return jnp.where(mask_ref[l, c] != 0, block, jnp.zeros_like(block))
+    kept = mask_ref[l : l + 1, c : c + 1].astype(F32)
+    return (dens_ref[c, l * orb : (l + 1) * orb, :].astype(F32) * kept).astype(BF16)
 
 
 def beyond(centre):
@@ -117,25 +117,29 @@
     return side_by_side(columns.reshape(chunk, columns.shape[0] // chunk, columns.shape[1]))
 
 
-def own_kernel(count, *refs):
-    own_ref = refs[0]
-    edges = refs[1:count]
-    local_ref, back_ref, total_ref, near_ref, behind_ref, open_ref, later_ref, part_ref = refs[count:]
+def own_kernel(own_ref, local_ref, back_ref, near_ref, behind_ref, open_ref, later_ref, mixed_ref):
     chunk, rows, cols = own_ref.shape
     wide = back_ref.shape[0]
     own = own_ref[...].reshape(chunk * rows, cols)
     near_ref[...] = turned(own[:, :wide], chunk)
     behind_ref[...] = turned(times(own[:, :wide], back_ref[...]).astype(BF16), chunk)
     open_ref[...] = times(own, local_ref[:, :wide])
-    mixed = turned(times(own, local_ref[:, wide:]).astype(BF16), chunk)
-    later = [turned(own[:, wide:], chunk)]
+    mixed_ref[...] = turned(times(own, local_ref[:, wide:]).astype(BF16), chunk)
+    later_ref[...] = turned(own[:, wide:], chunk)
+
+
+def edge_kernel(count, *refs):
+    edges = refs[: count - 1]
+    local_ref, own_later_ref, mixed_ref, total_ref, later_ref, part_ref = refs[count - 1 :]
+    chunk, rows, wide = edges[0].shape
+    later = [own_later_ref[...]]
     for d, edge in enumerate(edges):
-        columns = edge[...].reshape(chunk * rows, cols - wide)
-        part_ref[d] = times(columns, local_ref[wide:, :])
+        columns = edge[...].reshape(chunk * rows, wide)
+        part_ref[d] = times(columns, local_ref[local_ref.shape[0] - wide :, :])
         later.append(turned(columns, chunk))
     later = jnp.concatenate(later, axis=0)
     later_ref[...] = later
-    total_ref[...] = times_turned(later, mixed)
+    total_ref[...] = times_turned(later, mixed_ref[...])
 
 
 def inner_kernel(count, centre, *refs):
@@ -245,7 +249,7 @@
     (blocks,) = kernel(
         functools.partial(blocks_kernel, centre),
         [array((half, orb), BF16)],
-        [SMEM, VMEM],
+        [VMEM, VMEM],
         [pltpu.VMEM((2 * half, orb), BF16)],
     )(band_mask, density)
     blocks = move(blocks, sizes, forward)
@@ -253,28 +257,37 @@
     local, back = kernel(
         functools.partial(band_kernel, centre),
         [array((cols, cols), BF16), array((wide, wide), BF16)],
-        [SMEM, VMEM],
-    )(band_mask, density)
-    halos = [move(after(part, blocks), sizes, forward) for part in edges]
-    rests = [
-        move(after(rests[d - 1], edges[d - 1]), sizes, lambda i, j, k, d=d: (i, j ^ d, k))
-        for d in range(1, n_row)
-    ]
-
+        [VMEM, VMEM],
+    )(band_mask, after(density, blocks))
     whole = n_row * rows
     side = chunk * wide
-    first_terms = kernel(
-        functools.partial(own_kernel, n_row),
+    *own, own_later, mixed = kernel(
+        own_kernel,
         [
-            array((whole, rows), F32),
             array((rows, side), BF16),
             array((rows, side), BF16),
             array((chunk * rows, wide), F32),
+            array((rows, chunk * (cols - wide)), BF16),
+            array((rows, chunk * (cols - wide)), BF16),
+        ],
+        [VMEM] * 3,
+    )(mine, local, back)
+    halos = [move(after(part, blocks), sizes, forward) for part in edges]
+    rests = [
+        move(after(rests[d - 1], mixed), sizes, lambda i, j, k, d=d: (i, j ^ d, k))
+        for d in range(1, n_row)
+    ]
+
+    total, later, part = kernel(
+        functools.partial(edge_kernel, n_row),
+        [
+            array((whole, rows), F32),
             array((whole, chunk * (cols - wide)), BF16),
             array((n_row - 1, chunk * rows, cols), F32),
         ],
         [VMEM] * (n_row + 2),
-    )(mine, *edges, local, back)
+    )(*edges, local, own_later, mixed)
+    first_terms = [total, *own, later, part]
     handed = kernel(
         functools.partial(inner_kernel, n_row, centre),
         [

time: 37.2 us -> 36.7 us (0.987)
  waiting for transfers between devices: 15.2 us -> 18.2 us
  starting transfers between devices: 15.9 us -> 13.4 us
  Pallas kernels: 3.89 us -> 2.92 us
    ppermute x13, waiting for transfers between devices: 15.2 us -> 18.2 us  [move(): return lax.ppermute(value, AXES, pairs)]
    ppermute x13, starting transfers between devices: 15.9 us -> 13.4 us  [move(): return lax.ppermute(value, AXES, pairs)]
    pallas_call x1, Pallas kernels: 0.72 us -> 0.21 us  [per_device(): kernel(functools.partial(band_kernel, centre), [array((cols, cols), BF16)...]
    pallas_call x1, Pallas kernels: 0.6 us -> 0.12 us  [per_device(): kernel(functools.partial(blocks_kernel, centre), [array((half, orb), BF16...]
    pallas_call x1 -> x2, Pallas kernels: 0.93 us -> 0.94 us  [the longest x1 0.51 us: per_device(): kernel(own_kernel, [array((rows, side), BF16), array((rows, side), BF16),...]
  transfers between devices with their start and end apart: 13 -> 13, of which waited for: 10 -> 11; matrix products, arithmetic and copies ran while one was open for 0% -> 0% of each run, Pallas kernels for 8% -> 6%
where the time goes in v7:
time: 36.7 us; the launch traced here: 36.6 us
  waiting for transfers between devices  18.2 us (50%)
  starting transfers between devices  13.4 us (37%)
  Pallas kernels  2.92 us (8%)
  local copies, waits for them, and re-layouts  1.31 us (4%)
  other arithmetic  0.65 us (2%)
    ppermute x13, waiting for transfers between devices, move(): return lax.ppermute(value, AXES, pairs)  18.2 us
    ppermute x13, starting transfers between devices, move(): return lax.ppermute(value, AXES, pairs)  13.4 us
    unnamed x6, local copies, waits for them, and re-layouts  1.3 us
    pallas_call x1, Pallas kernels, per_device(): kernel(functools.partial(inner_kernel, n_row, centre), [array((whole, who...  0.88 us
  transfers between devices with their start and end apart: 13, of which 11 were waited for; matrix products, arithmetic and copies ran while one was open for 0% of the time, Pallas kernels for 6%

profile of v7, /device:TPU:0, one launch (start us, length us, event | category | flops | bytes accessed | tf_op | source)
XLA Modules:
  0.0 36.6 jit_solution(222430672331198282)
XLA Ops:
  0.0 1.3 %copy-done.1 = bf16[8,128,512]{2,1,0:T(8,128)(2,1)S(1)} copy-done((bf16[8,128,512]{2,1,0:T(8,128)(2,1)S(1)}, bf16[8,128,512]{2,1,0:T(8,128)(2,1)}, u32[]{:S(2)}) %copy-start.1) | copy-done | bytes 1048600
  1.4 3.0 %collective-permute-start = (bf16[4,128,256]{2,1,0:T(8,128)(2,1)S(1)}, bf16[4,128,256]{2,1,0:T(8,128)(2,1)S(1)}, u32[]{:S(2)}, u32[]{:S(2)}) collective-permute-start(bf16[4,128,256]{2,1,0:T(8,128)(2,1)S(1)} %get-tuple-element.29), channel_id=1, source_target_pairs={{0,4},{1,5},{2,6},{3,7},{4,0},{5,1},{6,2},{7,3},{8,12},{9,13},{10,... | collective-permute-start | bytes 786440 | tf_op jit(solution)/shard_map/ppermute | solution.py:27
  4.6 1.6 %collective-permute-start.1 = (bf16[192,128]{1,0:T(8,128)(2,1)S(1)}, bf16[192,128]{1,0:T(8,128)(2,1)S(1)}, u32[]{:S(2)}, u32[]{:S(2)}) collective-permute-start(bf16[192,128]{1,0:T(8,128)(2,1)S(1)} %shard_map.38), channel_id=1, source_target_pairs={{0,1},{1,2},{2,3},{3,0},{4,5},{5,6},{6,7},{7,4},{8,9},{9,10},{10,1... | collective-permute-start | bytes 147464 | tf_op jit(solution)/shard_map/ppermute | solution.py:27
  6.2 1.6 %collective-permute-start.4 = (bf16[4,128,256]{2,1,0:T(8,128)(2,1)S(1)}, bf16[4,128,256]{2,1,0:T(8,128)(2,1)S(1)}, u32[]{:S(2)}, u32[]{:S(2)}) collective-permute-start(bf16[4,128,256]{2,1,0:T(8,128)(2,1)S(1)} %get-tuple-element.38), channel_id=1, source_target_pairs={{0,1},{1,2},{2,3},{3,0},{4,5},{5,6},{6,7},{7,4},{8,9},{9,10},{10,1... | collective-permute-start | bytes 786440 | tf_op jit(solution)/shard_map/ppermute | solution.py:27
  7.8 3.3 %collective-permute-done.1.refs_2_ = bf16[192,128]{1,0:T(8,128)(2,1)S(1)} collective-permute-done((bf16[192,128]{1,0:T(8,128)(2,1)S(1)}, bf16[192,128]{1,0:T(8,128)(2,1)S(1)}, u32[]{:S(2)}, u32[]{:S(2)}) %collective-permute-start.1) | collective-permute-done | bytes 49184 | tf_op jit(solution)/shard_map/ppermute | solution.py:27
  11.3 0.5 %shard_map.40 = (bf16[128,1024]{1,0:T(8,128)(2,1)S(1)}, bf16[128,1024]{1,0:T(8,128)(2,1)S(1)}, f32[512,256]{1,0:T(8,128)S(1)}, bf16[128,1024]{1,0:T(8,128)(2,1)S(1)}, bf16[128,1024]{1,0:T(8,128)(2,1)S(1)}) custom-call(bf16[4,128,512]{2,1,0:T(8,128)(2,1)S(1)} %get-tuple-element.32.own_ref, bf16[512,512]{1,0:T(8,128)(2,1)S(1)} %get-tuple-element.34.local_ref.refs_1_.refs_4_, ...), custom_call_target="tpu_custom_call" | custom-call | flops 1 | bytes 1 | tf_op jit(solution)/shard_map/pallas_call | solution.py:264
  11.8 0.5 %collective-permute-start.3 = (bf16[4,128,256]{2,1,0:T(8,128)(2,1)S(1)}, bf16[4,128,256]{2,1,0:T(8,128)(2,1)S(1)}, u32[]{:S(2)}, u32[]{:S(2)}) collective-permute-start(bf16[4,128,256]{2,1,0:T(8,128)(2,1)S(1)} %get-tuple-element.37), channel_id=1, source_target_pairs={{0,4},{1,5},{2,6},{3,7},{4,0},{5,1},{6,2},{7,3},{8,12},{9,13},{10,... | collective-permute-start | bytes 786440 | tf_op jit(solution)/shard_map/ppermute | solution.py:27
  13.1 0.8 %collective-permute-done.5.refs_3_ = bf16[192,128]{1,0:T(8,128)(2,1)S(1)} collective-permute-done((bf16[192,128]{1,0:T(8,128)(2,1)S(1)}, bf16[192,128]{1,0:T(8,128)(2,1)S(1)}, u32[]{:S(2)}, u32[]{:S(2)}) %collective-permute-start.5) | collective-permute-done | bytes 49184 | tf_op jit(solution)/shard_map/ppermute | solution.py:27
  13.9 3.3 %collective-permute-done.4.refs_1_ = bf16[4,128,256]{2,1,0:T(8,128)(2,1)S(1)} collective-permute-done((bf16[4,128,256]{2,1,0:T(8,128)(2,1)S(1)}, bf16[4,128,256]{2,1,0:T(8,128)(2,1)S(1)}, u32[]{:S(2)}, u32[]{:S(2)}) %collective-permute-start.4) | collective-permute-done | bytes 262176 | tf_op jit(solution)/shard_map/ppermute | solution.py:27
  17.2 1.0 %collective-permute-done.3.refs_0_ = bf16[4,128,256]{2,1,0:T(8,128)(2,1)S(1)} collective-permute-done((bf16[4,128,256]{2,1,0:T(8,128)(2,1)S(1)}, bf16[4,128,256]{2,1,0:T(8,128)(2,1)S(1)}, u32[]{:S(2)}, u32[]{:S(2)}) %collective-permute-start.3) | collective-permute-done | bytes 262176 | tf_op jit(solution)/shard_map/ppermute | solution.py:27
  18.2 0.9 %shard_map.42 = (f32[256,256]{1,0:T(8,128)S(1)}, bf16[256,1024]{1,0:T(8,128)(2,1)S(1)}, bf16[256,1024]{1,0:T(8,128)(2,1)S(1)}, f32[1,512,256]{2,1,0:T(8,128)S(1)}, bf16[256,256]{1,0:T(8,128)(2,1)S(1)}) custom-call(bf16[4,128,256]{2,1,0:T(8,128)(2,1)S(1)} %collective-permute-done.3.refs_0_, bf16[4,128,256]{2,1,0:T(8,128)(2,1)S(1)} %collective-permute-done.4.refs_1_, ...), custom_call_target="tpu_custom_call" | custom-call | flops 1 | bytes 1 | tf_op jit(solution)/shard_map/pallas_call | solution.py:291
  19.1 2.5 %collective-permute-done.2.refs_0_ = bf16[4,128,256]{2,1,0:T(8,128)(2,1)S(1)} collective-permute-done((bf16[4,128,256]{2,1,0:T(8,128)(2,1)S(1)}, bf16[4,128,256]{2,1,0:T(8,128)(2,1)S(1)}, u32[]{:S(2)}, u32[]{:S(2)}) %collective-permute-start.2) | collective-permute-done | bytes 262176 | tf_op jit(solution)/shard_map/ppermute | solution.py:27
  21.7 0.6 %shard_map.43 = (f32[4,64,128]{2,1,0:T(8,128)S(1)}, f32[4,64,128]{2,1,0:T(8,128)S(1)}) custom-call(bf16[4,128,256]{2,1,0:T(8,128)(2,1)S(1)} %collective-permute-done.2.refs_0_, f32[256,256]{1,0:T(8,128)S(1)} %get-tuple-element.46.refs_1_, bf16[256,1024]{1,0:T(8,128)(2,1)S(1)} %get-tuple-element.47.refs_2_, bf16[256,1024]{1,0:T(8,128)(2,1)S(1)} %get-tuple-element.48.refs_3_, ...), custom_call_target="tpu_custom_call" | custom-call | flops 1 | bytes 1 | tf_op jit(solution)/shard_map/pallas_call | solution.py:305
  22.4 1.3 %collective-permute-done.6 = f32[4,64,128]{2,1,0:T(8,128)S(1)} collective-permute-done((f32[4,64,128]{2,1,0:T(8,128)S(1)}, f32[4,64,128]{2,1,0:T(8,128)S(1)}, u32[]{:S(2)}, u32[]{:S(2)}) %collective-permute-start.6) | collective-permute-done | bytes 131104 | tf_op jit(solution)/shard_map/ppermute | solution.py:27
  23.8 1.0 %collective-permute-start.10 = (f32[64,128]{1,0:T(8,128)S(1)}, f32[64,128]{1,0:T(8,128)S(1)}, u32[]{:S(2)}, u32[]{:S(2)}) collective-permute-start(f32[64,128]{1,0:T(8,128)S(1)} %get-tuple-element.54), channel_id=1, source_target_pairs={{0,6},{1,7},{2,4},{3,5},{4,2},{5,3},{6,0},{7,1},{8,13},{9,12},{10,... | collective-permute-start | bytes 98312 | tf_op jit(solution)/shard_map/ppermute | solution.py:27
  24.8 1.3 %collective-permute-start.7 = (f32[64,128]{1,0:T(8,128)S(1)}, f32[64,128]{1,0:T(8,128)S(1)}, u32[]{:S(2)}, u32[]{:S(2)}) collective-permute-start(f32[64,128]{1,0:T(8,128)S(1)} %get-tuple-element.53), channel_id=1, source_target_pairs={{0,3},{1,2},{2,1},{3,0},{4,7},{5,6},{6,5},{7,4},{8,15},{9,14},{10,... | collective-permute-start | bytes 98312 | tf_op jit(solution)/shard_map/ppermute | solution.py:27
  26.1 0.7 %collective-permute-start.8 = (f32[64,128]{1,0:T(8,128)S(1)}, f32[64,128]{1,0:T(8,128)S(1)}, u32[]{:S(2)}, u32[]{:S(2)}) collective-permute-start(f32[64,128]{1,0:T(8,128)S(1)} %get-tuple-element.56), channel_id=1, source_target_pairs={{8,9},{9,8},{10,11},{11,10},{12,13},{13,12},{14,15},{15,14},{24,25... | collective-permute-start | bytes 98312 | tf_op jit(solution)/shard_map/ppermute | solution.py:27
  26.8 1.4 %collective-permute-start.9 = (f32[64,128]{1,0:T(8,128)S(1)}, f32[64,128]{1,0:T(8,128)S(1)}, u32[]{:S(2)}, u32[]{:S(2)}) collective-permute-start(f32[64,128]{1,0:T(8,128)S(1)} %get-tuple-element.55), channel_id=1, source_target_pairs={{0,4},{1,5},{2,6},{3,7},{4,0},{5,1},{6,2},{7,3},{8,10},{9,11},{10,... | collective-permute-start | bytes 98312 | tf_op jit(solution)/shard_map/ppermute | solution.py:27
  28.2 1.7 %collective-permute-done.10 = f32[64,128]{1,0:T(8,128)S(1)} collective-permute-done((f32[64,128]{1,0:T(8,128)S(1)}, f32[64,128]{1,0:T(8,128)S(1)}, u32[]{:S(2)}, u32[]{:S(2)}) %collective-permute-start.10) | collective-permute-done | bytes 32800 | tf_op jit(solution)/shard_map/ppermute | solution.py:27
  29.9 0.6 %collective-permute-done.7 = f32[64,128]{1,0:T(8,128)S(1)} collective-permute-done((f32[64,128]{1,0:T(8,128)S(1)}, f32[64,128]{1,0:T(8,128)S(1)}, u32[]{:S(2)}, u32[]{:S(2)}) %collective-permute-start.7) | collective-permute-done | bytes 32800 | tf_op jit(solution)/shard_map/ppermute | solution.py:27
  30.8 1.6 %collective-permute-start.11 = (f32[64,128]{1,0:T(8,128)S(1)}, f32[64,128]{1,0:T(8,128)S(1)}, u32[]{:S(2)}, u32[]{:S(2)}) collective-permute-start(f32[64,128]{1,0:T(8,128)S(1)} %add_add_fusion), channel_id=1, source_target_pairs={{0,16},{1,17},{2,18},{3,19},{4,20},{5,21},{6,22},{7,23},{8,24},{9,... | collective-permute-start | bytes 98312 | tf_op jit(solution)/shard_map/ppermute | solution.py:27
  32.3 2.4 %collective-permute-done.11 = f32[64,128]{1,0:T(8,128)S(1)} collective-permute-done((f32[64,128]{1,0:T(8,128)S(1)}, f32[64,128]{1,0:T(8,128)S(1)}, u32[]{:S(2)}, u32[]{:S(2)}) %collective-permute-start.11) | collective-permute-done | bytes 32800 | tf_op jit(solution)/shard_map/ppermute | solution.py:27
  35.1 0.9 %collective-permute-done.12 = f32[64,128]{1,0:T(8,128)S(1)} collective-permute-done((f32[64,128]{1,0:T(8,128)S(1)}, f32[64,128]{1,0:T(8,128)S(1)}, u32[]{:S(2)}, u32[]{:S(2)}) %collective-permute-start.12) | collective-permute-done | bytes 32800 | tf_op jit(solution)/shard_map/ppermute | solution.py:27
  36.0 0.6 %add.27 = f32[64,128]{1,0:T(8,128)} add(f32[64,128]{1,0:T(8,128)S(1)} %add.26, f32[64,128]{1,0:T(8,128)S(1)} %collective-permute-done.12) | non-fusion elementwise | flops 8192 | bytes 98304 | tf_op jit(solution)/shard_map/add | solution.py:324
  (20 shorter events, 2.0 us)
Async XLA Ops:
  0.0 4.5 %copy-start = (bf16[512,5,128]{2,0,1:T(8,128)(2,1)S(1)}, bf16[512,5,128]{2,0,1:T(8,128)(2,1)}, u32[]{:S(2)}) copy-start(bf16[512,5,128]{2,0,1:T(8,128)(2,1)} %param.4) | copy-start | bytes 1966084
  0.0 1.3 %copy-start.1 = (bf16[8,128,512]{2,1,0:T(8,128)(2,1)S(1)}, bf16[8,128,512]{2,1,0:T(8,128)(2,1)}, u32[]{:S(2)}) copy-start(bf16[8,128,512]{2,1,0:T(8,128)(2,1)} %tensor_ref.1) | copy-start | bytes 3145732
  1.4 3.0 %copy-start.2 = (s32[4,5]{1,0:T(4,128)S(1)}, s32[4,5]{1,0:T(4,128)}, u32[]{:S(2)}) copy-start(s32[4,5]{1,0:T(4,128)} %mask_ref.3) | copy-start | bytes 244
  1.4 10.9 %collective-permute-start = (bf16[4,128,256]{2,1,0:T(8,128)(2,1)S(1)}, bf16[4,128,256]{2,1,0:T(8,128)(2,1)S(1)}, u32[]{:S(2)}, u32[]{:S(2)}) collective-permute-start(bf16[4,128,256]{2,1,0:T(8,128)(2,1)S(1)} %get-tuple-element.29), channel_id=1, source_target_pairs={{0,4},{1,5},{2,6},{3,7},{4,0},{5,1},{6,2},{7,3},{8,12},{9,13},{10,... | collective-permute-start | bytes 786440 | tf_op jit(solution)/shard_map/ppermute | solution.py:27
  4.6 6.5 %collective-permute-start.1 = (bf16[192,128]{1,0:T(8,128)(2,1)S(1)}, bf16[192,128]{1,0:T(8,128)(2,1)S(1)}, u32[]{:S(2)}, u32[]{:S(2)}) collective-permute-start(bf16[192,128]{1,0:T(8,128)(2,1)S(1)} %shard_map.38), channel_id=1, source_target_pairs={{0,1},{1,2},{2,3},{3,0},{4,5},{5,6},{6,7},{7,4},{8,9},{9,10},{10,1... | collective-permute-start | bytes 147464 | tf_op jit(solution)/shard_map/ppermute | solution.py:27
  6.2 11.0 %collective-permute-start.4 = (bf16[4,128,256]{2,1,0:T(8,128)(2,1)S(1)}, bf16[4,128,256]{2,1,0:T(8,128)(2,1)S(1)}, u32[]{:S(2)}, u32[]{:S(2)}) collective-permute-start(bf16[4,128,256]{2,1,0:T(8,128)(2,1)S(1)} %get-tuple-element.38), channel_id=1, source_target_pairs={{0,1},{1,2},{2,3},{3,0},{4,5},{5,6},{6,7},{7,4},{8,9},{9,10},{10,1... | collective-permute-start | bytes 786440 | tf_op jit(solution)/shard_map/ppermute | solution.py:27
  11.8 6.4 %collective-permute-start.3 = (bf16[4,128,256]{2,1,0:T(8,128)(2,1)S(1)}, bf16[4,128,256]{2,1,0:T(8,128)(2,1)S(1)}, u32[]{:S(2)}, u32[]{:S(2)}) collective-permute-start(bf16[4,128,256]{2,1,0:T(8,128)(2,1)S(1)} %get-tuple-element.37), channel_id=1, source_target_pairs={{0,4},{1,5},{2,6},{3,7},{4,0},{5,1},{6,2},{7,3},{8,12},{9,13},{10,... | collective-permute-start | bytes 786440 | tf_op jit(solution)/shard_map/ppermute | solution.py:27
  12.3 9.4 %collective-permute-start.2 = (bf16[4,128,256]{2,1,0:T(8,128)(2,1)S(1)}, bf16[4,128,256]{2,1,0:T(8,128)(2,1)S(1)}, u32[]{:S(2)}, u32[]{:S(2)}) collective-permute-start(bf16[4,128,256]{2,1,0:T(8,128)(2,1)S(1)} %collective-permute-done.refs_0_), channel_id=1, source_target_pairs={{0,1},{1,2},{2,3},{3,0},{4,5},{5,6},{6,7},{7,4},{8,9},{9,10},{10,1... | collective-permute-start | bytes 786440 | tf_op jit(solution)/shard_map/ppermute | solution.py:27
  12.7 1.2 %collective-permute-start.5 = (bf16[192,128]{1,0:T(8,128)(2,1)S(1)}, bf16[192,128]{1,0:T(8,128)(2,1)S(1)}, u32[]{:S(2)}, u32[]{:S(2)}) collective-permute-start(bf16[192,128]{1,0:T(8,128)(2,1)S(1)} %collective-permute-done.1.refs_2_), channel_id=1, source_target_pairs={{0,8},{1,9},{2,10},{3,11},{4,12},{5,13},{6,14},{7,15},{8,0},{9,1},... | collective-permute-start | bytes 147464 | tf_op jit(solution)/shard_map/ppermute | solution.py:27
  22.3 1.4 %collective-permute-start.6 = (f32[4,64,128]{2,1,0:T(8,128)S(1)}, f32[4,64,128]{2,1,0:T(8,128)S(1)}, u32[]{:S(2)}, u32[]{:S(2)}) collective-permute-start(f32[4,64,128]{2,1,0:T(8,128)S(1)} %get-tuple-element.52), channel_id=1, source_target_pairs={{0,8},{1,9},{2,10},{3,11},{4,12},{5,13},{6,14},{7,15},{8,0},{9,1},... | collective-permute-start | bytes 393224 | tf_op jit(solution)/shard_map/ppermute | solution.py:27
  23.8 6.1 %collective-permute-start.10 = (f32[64,128]{1,0:T(8,128)S(1)}, f32[64,128]{1,0:T(8,128)S(1)}, u32[]{:S(2)}, u32[]{:S(2)}) collective-permute-start(f32[64,128]{1,0:T(8,128)S(1)} %get-tuple-element.54), channel_id=1, source_target_pairs={{0,6},{1,7},{2,4},{3,5},{4,2},{5,3},{6,0},{7,1},{8,13},{9,12},{10,... | collective-permute-start | bytes 98312 | tf_op jit(solution)/shard_map/ppermute | solution.py:27
  24.8 5.7 %collective-permute-start.7 = (f32[64,128]{1,0:T(8,128)S(1)}, f32[64,128]{1,0:T(8,128)S(1)}, u32[]{:S(2)}, u32[]{:S(2)}) collective-permute-start(f32[64,128]{1,0:T(8,128)S(1)} %get-tuple-element.53), channel_id=1, source_target_pairs={{0,3},{1,2},{2,1},{3,0},{4,7},{5,6},{6,5},{7,4},{8,15},{9,14},{10,... | collective-permute-start | bytes 98312 | tf_op jit(solution)/shard_map/ppermute | solution.py:27
  26.1 4.4 %collective-permute-start.8 = (f32[64,128]{1,0:T(8,128)S(1)}, f32[64,128]{1,0:T(8,128)S(1)}, u32[]{:S(2)}, u32[]{:S(2)}) collective-permute-start(f32[64,128]{1,0:T(8,128)S(1)} %get-tuple-element.56), channel_id=1, source_target_pairs={{8,9},{9,8},{10,11},{11,10},{12,13},{13,12},{14,15},{15,14},{24,25... | collective-permute-start | bytes 98312 | tf_op jit(solution)/shard_map/ppermute | solution.py:27
  26.8 4.0 %collective-permute-start.9 = (f32[64,128]{1,0:T(8,128)S(1)}, f32[64,128]{1,0:T(8,128)S(1)}, u32[]{:S(2)}, u32[]{:S(2)}) collective-permute-start(f32[64,128]{1,0:T(8,128)S(1)} %get-tuple-element.55), channel_id=1, source_target_pairs={{0,4},{1,5},{2,6},{3,7},{4,0},{5,1},{6,2},{7,3},{8,10},{9,11},{10,... | collective-permute-start | bytes 98312 | tf_op jit(solution)/shard_map/ppermute | solution.py:27
  30.8 4.0 %collective-permute-start.11 = (f32[64,128]{1,0:T(8,128)S(1)}, f32[64,128]{1,0:T(8,128)S(1)}, u32[]{:S(2)}, u32[]{:S(2)}) collective-permute-start(f32[64,128]{1,0:T(8,128)S(1)} %add_add_fusion), channel_id=1, source_target_pairs={{0,16},{1,17},{2,18},{3,19},{4,20},{5,21},{6,22},{7,23},{8,24},{9,... | collective-permute-start | bytes 98312 | tf_op jit(solution)/shard_map/ppermute | solution.py:27
  34.8 1.2 %collective-permute-start.12 = (f32[64,128]{1,0:T(8,128)S(1)}, f32[64,128]{1,0:T(8,128)S(1)}, u32[]{:S(2)}, u32[]{:S(2)}) collective-permute-start(f32[64,128]{1,0:T(8,128)S(1)} %add.26), channel_id=1, source_target_pairs={{0,8},{1,9},{2,10},{3,11},{4,12},{5,13},{6,14},{7,15},{8,0},{9,1},... | collective-permute-start | bytes 98312 | tf_op jit(solution)/shard_map/ppermute | solution.py:27

commit v8 on v7

--- a/solution.py
+++ b/solution.py
@@ -170,8 +170,8 @@
         mixed.append(turned(whole[:, wide:].astype(BF16), chunk))
     near = jnp.concatenate(near, axis=0)
     behind = jnp.concatenate(behind, axis=0)
-    near_ref[...] = near
-    behind_ref[...] = behind
+    near_ref[...] = near.T
+    behind_ref[...] = behind.T
     total_ref[:, :rows] = own_total_ref[...] + times_turned(near, first)
     total_ref[:, rows:] = times_turned(later_ref[...], jnp.concatenate(mixed, axis=0))
     total_ref[:rows, :] += times_turned(turned(halo, chunk), behind)
@@ -188,8 +188,8 @@
     for d, halo in enumerate(halos):
         part = open_ref[d] + times(halo[...].reshape(chunk * rows, wide), cross_ref[...])
         mixed.append(side_by_side(part.astype(BF16).reshape(chunk, rows, wide)))
-    columns = times_turned(near_ref[...], jnp.concatenate(mixed, axis=0))
-    lines = times_turned(jnp.concatenate([side_by_side(halo[...]) for halo in halos], axis=0), behind_ref[...])
+    columns = times(jnp.concatenate(mixed, axis=0), near_ref[...]).T
+    lines = times(jnp.concatenate([side_by_side(halo[...]) for halo in halos], axis=0), behind_ref[...])
     for d in range(count):
         at = slice(d * rows, (d + 1) * rows)
         kx_ref[d, :rows] = inner_ref[:rows, at]
@@ -292,8 +292,8 @@
         functools.partial(inner_kernel, n_row, centre),
         [
             array((whole, whole), F32),
-            array((whole, side), BF16),
-            array((whole, side), BF16),
+            array((side, whole), BF16),
+            array((side, whole), BF16),
             array((n_row - 1, chunk * rows, wide), F32),
             array((wide, wide), BF16),
         ],

time: 36.7 us -> 36.6 us (level)
  no operation moved by 1% of the time
where the time goes in v8:
time: 36.6 us; the launch traced here: 36.5 us
  waiting for transfers between devices  18.2 us (50%)
  starting transfers between devices  13.4 us (37%)
  Pallas kernels  2.81 us (8%)
  local copies, waits for them, and re-layouts  1.31 us (4%)
  other arithmetic  0.65 us (2%)
    ppermute x13, waiting for transfers between devices, move(): return lax.ppermute(value, AXES, pairs)  18.2 us
    ppermute x13, starting transfers between devices, move(): return lax.ppermute(value, AXES, pairs)  13.4 us
    unnamed x6, local copies, waits for them, and re-layouts  1.3 us
    pallas_call x1, Pallas kernels, per_device(): kernel(functools.partial(inner_kernel, n_row, centre), [array((whole, who...  0.9 us
  transfers between devices with their start and end apart: 13, of which 11 were waited for; matrix products, arithmetic and copies ran while one was open for 0% of the time, Pallas kernels for 6%

profile of v8, /device:TPU:0, one launch (start us, length us, event | category | flops | bytes accessed | tf_op | source)
XLA Modules:
  0.0 36.5 jit_solution(17228661131951700395)
XLA Ops:
  0.0 1.3 %copy-done.1 = bf16[8,128,512]{2,1,0:T(8,128)(2,1)S(1)} copy-done((bf16[8,128,512]{2,1,0:T(8,128)(2,1)S(1)}, bf16[8,128,512]{2,1,0:T(8,128)(2,1)}, u32[]{:S(2)}) %copy-start.1) | copy-done | bytes 1048600
  1.4 3.0 %collective-permute-start = (bf16[4,128,256]{2,1,0:T(8,128)(2,1)S(1)}, bf16[4,128,256]{2,1,0:T(8,128)(2,1)S(1)}, u32[]{:S(2)}, u32[]{:S(2)}) collective-permute-start(bf16[4,128,256]{2,1,0:T(8,128)(2,1)S(1)} %get-tuple-element.29), channel_id=1, source_target_pairs={{0,4},{1,5},{2,6},{3,7},{4,0},{5,1},{6,2},{7,3},{8,12},{9,13},{10,... | collective-permute-start | bytes 786440 | tf_op jit(solution)/shard_map/ppermute | solution.py:27
  4.6 1.6 %collective-permute-start.1 = (bf16[192,128]{1,0:T(8,128)(2,1)S(1)}, bf16[192,128]{1,0:T(8,128)(2,1)S(1)}, u32[]{:S(2)}, u32[]{:S(2)}) collective-permute-start(bf16[192,128]{1,0:T(8,128)(2,1)S(1)} %shard_map.38), channel_id=1, source_target_pairs={{0,1},{1,2},{2,3},{3,0},{4,5},{5,6},{6,7},{7,4},{8,9},{9,10},{10,1... | collective-permute-start | bytes 147464 | tf_op jit(solution)/shard_map/ppermute | solution.py:27
  6.2 1.6 %collective-permute-start.4 = (bf16[4,128,256]{2,1,0:T(8,128)(2,1)S(1)}, bf16[4,128,256]{2,1,0:T(8,128)(2,1)S(1)}, u32[]{:S(2)}, u32[]{:S(2)}) collective-permute-start(bf16[4,128,256]{2,1,0:T(8,128)(2,1)S(1)} %get-tuple-element.38), channel_id=1, source_target_pairs={{0,1},{1,2},{2,3},{3,0},{4,5},{5,6},{6,7},{7,4},{8,9},{9,10},{10,1... | collective-permute-start | bytes 786440 | tf_op jit(solution)/shard_map/ppermute | solution.py:27
  7.8 3.3 %collective-permute-done.1.refs_2_ = bf16[192,128]{1,0:T(8,128)(2,1)S(1)} collective-permute-done((bf16[192,128]{1,0:T(8,128)(2,1)S(1)}, bf16[192,128]{1,0:T(8,128)(2,1)S(1)}, u32[]{:S(2)}, u32[]{:S(2)}) %collective-permute-start.1) | collective-permute-done | bytes 49184 | tf_op jit(solution)/shard_map/ppermute | solution.py:27
  11.3 0.5 %shard_map.40 = (bf16[128,1024]{1,0:T(8,128)(2,1)S(1)}, bf16[128,1024]{1,0:T(8,128)(2,1)S(1)}, f32[512,256]{1,0:T(8,128)S(1)}, bf16[128,1024]{1,0:T(8,128)(2,1)S(1)}, bf16[128,1024]{1,0:T(8,128)(2,1)S(1)}) custom-call(bf16[4,128,512]{2,1,0:T(8,128)(2,1)S(1)} %get-tuple-element.32.own_ref, bf16[512,512]{1,0:T(8,128)(2,1)S(1)} %get-tuple-element.34.local_ref.refs_1_.refs_4_, ...), custom_call_target="tpu_custom_call" | custom-call | flops 1 | bytes 1 | tf_op jit(solution)/shard_map/pallas_call | solution.py:264
  11.8 0.5 %collective-permute-start.3 = (bf16[4,128,256]{2,1,0:T(8,128)(2,1)S(1)}, bf16[4,128,256]{2,1,0:T(8,128)(2,1)S(1)}, u32[]{:S(2)}, u32[]{:S(2)}) collective-permute-start(bf16[4,128,256]{2,1,0:T(8,128)(2,1)S(1)} %get-tuple-element.37), channel_id=1, source_target_pairs={{0,4},{1,5},{2,6},{3,7},{4,0},{5,1},{6,2},{7,3},{8,12},{9,13},{10,... | collective-permute-start | bytes 786440 | tf_op jit(solution)/shard_map/ppermute | solution.py:27
  13.1 0.8 %collective-permute-done.5.refs_3_ = bf16[192,128]{1,0:T(8,128)(2,1)S(1)} collective-permute-done((bf16[192,128]{1,0:T(8,128)(2,1)S(1)}, bf16[192,128]{1,0:T(8,128)(2,1)S(1)}, u32[]{:S(2)}, u32[]{:S(2)}) %collective-permute-start.5) | collective-permute-done | bytes 49184 | tf_op jit(solution)/shard_map/ppermute | solution.py:27
  13.9 3.3 %collective-permute-done.4.refs_1_ = bf16[4,128,256]{2,1,0:T(8,128)(2,1)S(1)} collective-permute-done((bf16[4,128,256]{2,1,0:T(8,128)(2,1)S(1)}, bf16[4,128,256]{2,1,0:T(8,128)(2,1)S(1)}, u32[]{:S(2)}, u32[]{:S(2)}) %collective-permute-start.4) | collective-permute-done | bytes 262176 | tf_op jit(solution)/shard_map/ppermute | solution.py:27
  17.2 1.0 %collective-permute-done.3.refs_0_ = bf16[4,128,256]{2,1,0:T(8,128)(2,1)S(1)} collective-permute-done((bf16[4,128,256]{2,1,0:T(8,128)(2,1)S(1)}, bf16[4,128,256]{2,1,0:T(8,128)(2,1)S(1)}, u32[]{:S(2)}, u32[]{:S(2)}) %collective-permute-start.3) | collective-permute-done | bytes 262176 | tf_op jit(solution)/shard_map/ppermute | solution.py:27
  18.2 0.9 %shard_map.42 = (f32[256,256]{1,0:T(8,128)S(1)}, bf16[1024,256]{1,0:T(8,128)(2,1)S(1)}, bf16[1024,256]{1,0:T(8,128)(2,1)S(1)}, f32[1,512,256]{2,1,0:T(8,128)S(1)}, bf16[256,256]{1,0:T(8,128)(2,1)S(1)}) custom-call(bf16[4,128,256]{2,1,0:T(8,128)(2,1)S(1)} %collective-permute-done.3.refs_0_, bf16[4,128,256]{2,1,0:T(8,128)(2,1)S(1)} %collective-permute-done.4.refs_1_, ...), custom_call_target="tpu_custom_call" | custom-call | flops 1 | bytes 1 | tf_op jit(solution)/shard_map/pallas_call | solution.py:291
  19.2 2.5 %collective-permute-done.2.refs_0_ = bf16[4,128,256]{2,1,0:T(8,128)(2,1)S(1)} collective-permute-done((bf16[4,128,256]{2,1,0:T(8,128)(2,1)S(1)}, bf16[4,128,256]{2,1,0:T(8,128)(2,1)S(1)}, u32[]{:S(2)}, u32[]{:S(2)}) %collective-permute-start.2) | collective-permute-done | bytes 262176 | tf_op jit(solution)/shard_map/ppermute | solution.py:27
  21.7 0.5 %shard_map.43 = (f32[4,64,128]{2,1,0:T(8,128)S(1)}, f32[4,64,128]{2,1,0:T(8,128)S(1)}) custom-call(bf16[4,128,256]{2,1,0:T(8,128)(2,1)S(1)} %collective-permute-done.2.refs_0_, f32[256,256]{1,0:T(8,128)S(1)} %get-tuple-element.46.refs_1_, bf16[1024,256]{1,0:T(8,128)(2,1)S(1)} %get-tuple-element.47.refs_2_, bf16[1024,256]{1,0:T(8,128)(2,1)S(1)} %get-tuple-element.48.refs_3_, ...), custom_call_target="tpu_custom_call" | custom-call | flops 1 | bytes 1 | tf_op jit(solution)/shard_map/pallas_call | solution.py:305
  22.3 1.3 %collective-permute-done.6 = f32[4,64,128]{2,1,0:T(8,128)S(1)} collective-permute-done((f32[4,64,128]{2,1,0:T(8,128)S(1)}, f32[4,64,128]{2,1,0:T(8,128)S(1)}, u32[]{:S(2)}, u32[]{:S(2)}) %collective-permute-start.6) | collective-permute-done | bytes 131104 | tf_op jit(solution)/shard_map/ppermute | solution.py:27
  23.6 1.0 %collective-permute-start.10 = (f32[64,128]{1,0:T(8,128)S(1)}, f32[64,128]{1,0:T(8,128)S(1)}, u32[]{:S(2)}, u32[]{:S(2)}) collective-permute-start(f32[64,128]{1,0:T(8,128)S(1)} %get-tuple-element.54), channel_id=1, source_target_pairs={{0,6},{1,7},{2,4},{3,5},{4,2},{5,3},{6,0},{7,1},{8,13},{9,12},{10,... | collective-permute-start | bytes 98312 | tf_op jit(solution)/shard_map/ppermute | solution.py:27
  24.7 1.3 %collective-permute-start.7 = (f32[64,128]{1,0:T(8,128)S(1)}, f32[64,128]{1,0:T(8,128)S(1)}, u32[]{:S(2)}, u32[]{:S(2)}) collective-permute-start(f32[64,128]{1,0:T(8,128)S(1)} %get-tuple-element.53), channel_id=1, source_target_pairs={{0,3},{1,2},{2,1},{3,0},{4,7},{5,6},{6,5},{7,4},{8,15},{9,14},{10,... | collective-permute-start | bytes 98312 | tf_op jit(solution)/shard_map/ppermute | solution.py:27
  26.0 0.7 %collective-permute-start.8 = (f32[64,128]{1,0:T(8,128)S(1)}, f32[64,128]{1,0:T(8,128)S(1)}, u32[]{:S(2)}, u32[]{:S(2)}) collective-permute-start(f32[64,128]{1,0:T(8,128)S(1)} %get-tuple-element.56), channel_id=1, source_target_pairs={{8,9},{9,8},{10,11},{11,10},{12,13},{13,12},{14,15},{15,14},{24,25... | collective-permute-start | bytes 98312 | tf_op jit(solution)/shard_map/ppermute | solution.py:27
  26.7 1.4 %collective-permute-start.9 = (f32[64,128]{1,0:T(8,128)S(1)}, f32[64,128]{1,0:T(8,128)S(1)}, u32[]{:S(2)}, u32[]{:S(2)}) collective-permute-start(f32[64,128]{1,0:T(8,128)S(1)} %get-tuple-element.55), channel_id=1, source_target_pairs={{0,4},{1,5},{2,6},{3,7},{4,0},{5,1},{6,2},{7,3},{8,10},{9,11},{10,... | collective-permute-start | bytes 98312 | tf_op jit(solution)/shard_map/ppermute | solution.py:27
  28.0 1.7 %collective-permute-done.10 = f32[64,128]{1,0:T(8,128)S(1)} collective-permute-done((f32[64,128]{1,0:T(8,128)S(1)}, f32[64,128]{1,0:T(8,128)S(1)}, u32[]{:S(2)}, u32[]{:S(2)}) %collective-permute-start.10) | collective-permute-done | bytes 32800 | tf_op jit(solution)/shard_map/ppermute | solution.py:27
  29.8 0.6 %collective-permute-done.7 = f32[64,128]{1,0:T(8,128)S(1)} collective-permute-done((f32[64,128]{1,0:T(8,128)S(1)}, f32[64,128]{1,0:T(8,128)S(1)}, u32[]{:S(2)}, u32[]{:S(2)}) %collective-permute-start.7) | collective-permute-done | bytes 32800 | tf_op jit(solution)/shard_map/ppermute | solution.py:27
  30.7 1.6 %collective-permute-start.11 = (f32[64,128]{1,0:T(8,128)S(1)}, f32[64,128]{1,0:T(8,128)S(1)}, u32[]{:S(2)}, u32[]{:S(2)}) collective-permute-start(f32[64,128]{1,0:T(8,128)S(1)} %add_add_fusion), channel_id=1, source_target_pairs={{0,16},{1,17},{2,18},{3,19},{4,20},{5,21},{6,22},{7,23},{8,24},{9,... | collective-permute-start | bytes 98312 | tf_op jit(solution)/shard_map/ppermute | solution.py:27
  32.2 2.4 %collective-permute-done.11 = f32[64,128]{1,0:T(8,128)S(1)} collective-permute-done((f32[64,128]{1,0:T(8,128)S(1)}, f32[64,128]{1,0:T(8,128)S(1)}, u32[]{:S(2)}, u32[]{:S(2)}) %collective-permute-start.11) | collective-permute-done | bytes 32800 | tf_op jit(solution)/shard_map/ppermute | solution.py:27
  34.9 0.9 %collective-permute-done.12 = f32[64,128]{1,0:T(8,128)S(1)} collective-permute-done((f32[64,128]{1,0:T(8,128)S(1)}, f32[64,128]{1,0:T(8,128)S(1)}, u32[]{:S(2)}, u32[]{:S(2)}) %collective-permute-start.12) | collective-permute-done | bytes 32800 | tf_op jit(solution)/shard_map/ppermute | solution.py:27
  35.8 0.6 %add.27 = f32[64,128]{1,0:T(8,128)} add(f32[64,128]{1,0:T(8,128)S(1)} %add.26, f32[64,128]{1,0:T(8,128)S(1)} %collective-permute-done.12) | non-fusion elementwise | flops 8192 | bytes 98304 | tf_op jit(solution)/shard_map/add | solution.py:324
  (20 shorter events, 2.0 us)
Async XLA Ops:
  0.0 4.5 %copy-start = (bf16[512,5,128]{2,0,1:T(8,128)(2,1)S(1)}, bf16[512,5,128]{2,0,1:T(8,128)(2,1)}, u32[]{:S(2)}) copy-start(bf16[512,5,128]{2,0,1:T(8,128)(2,1)} %param.4) | copy-start | bytes 1966084
  0.0 1.3 %copy-start.1 = (bf16[8,128,512]{2,1,0:T(8,128)(2,1)S(1)}, bf16[8,128,512]{2,1,0:T(8,128)(2,1)}, u32[]{:S(2)}) copy-start(bf16[8,128,512]{2,1,0:T(8,128)(2,1)} %tensor_ref.1) | copy-start | bytes 3145732
  1.4 3.0 %copy-start.2 = (s32[4,5]{1,0:T(4,128)S(1)}, s32[4,5]{1,0:T(4,128)}, u32[]{:S(2)}) copy-start(s32[4,5]{1,0:T(4,128)} %mask_ref.3) | copy-start | bytes 244
  1.4 10.9 %collective-permute-start = (bf16[4,128,256]{2,1,0:T(8,128)(2,1)S(1)}, bf16[4,128,256]{2,1,0:T(8,128)(2,1)S(1)}, u32[]{:S(2)}, u32[]{:S(2)}) collective-permute-start(bf16[4,128,256]{2,1,0:T(8,128)(2,1)S(1)} %get-tuple-element.29), channel_id=1, source_target_pairs={{0,4},{1,5},{2,6},{3,7},{4,0},{5,1},{6,2},{7,3},{8,12},{9,13},{10,... | collective-permute-start | bytes 786440 | tf_op jit(solution)/shard_map/ppermute | solution.py:27
  4.6 6.5 %collective-permute-start.1 = (bf16[192,128]{1,0:T(8,128)(2,1)S(1)}, bf16[192,128]{1,0:T(8,128)(2,1)S(1)}, u32[]{:S(2)}, u32[]{:S(2)}) collective-permute-start(bf16[192,128]{1,0:T(8,128)(2,1)S(1)} %shard_map.38), channel_id=1, source_target_pairs={{0,1},{1,2},{2,3},{3,0},{4,5},{5,6},{6,7},{7,4},{8,9},{9,10},{10,1... | collective-permute-start | bytes 147464 | tf_op jit(solution)/shard_map/ppermute | solution.py:27
  6.2 11.0 %collective-permute-start.4 = (bf16[4,128,256]{2,1,0:T(8,128)(2,1)S(1)}, bf16[4,128,256]{2,1,0:T(8,128)(2,1)S(1)}, u32[]{:S(2)}, u32[]{:S(2)}) collective-permute-start(bf16[4,128,256]{2,1,0:T(8,128)(2,1)S(1)} %get-tuple-element.38), channel_id=1, source_target_pairs={{0,1},{1,2},{2,3},{3,0},{4,5},{5,6},{6,7},{7,4},{8,9},{9,10},{10,1... | collective-permute-start | bytes 786440 | tf_op jit(solution)/shard_map/ppermute | solution.py:27
  11.8 6.4 %collective-permute-start.3 = (bf16[4,128,256]{2,1,0:T(8,128)(2,1)S(1)}, bf16[4,128,256]{2,1,0:T(8,128)(2,1)S(1)}, u32[]{:S(2)}, u32[]{:S(2)}) collective-permute-start(bf16[4,128,256]{2,1,0:T(8,128)(2,1)S(1)} %get-tuple-element.37), channel_id=1, source_target_pairs={{0,4},{1,5},{2,6},{3,7},{4,0},{5,1},{6,2},{7,3},{8,12},{9,13},{10,... | collective-permute-start | bytes 786440 | tf_op jit(solution)/shard_map/ppermute | solution.py:27
  12.3 9.4 %collective-permute-start.2 = (bf16[4,128,256]{2,1,0:T(8,128)(2,1)S(1)}, bf16[4,128,256]{2,1,0:T(8,128)(2,1)S(1)}, u32[]{:S(2)}, u32[]{:S(2)}) collective-permute-start(bf16[4,128,256]{2,1,0:T(8,128)(2,1)S(1)} %collective-permute-done.refs_0_), channel_id=1, source_target_pairs={{0,1},{1,2},{2,3},{3,0},{4,5},{5,6},{6,7},{7,4},{8,9},{9,10},{10,1... | collective-permute-start | bytes 786440 | tf_op jit(solution)/shard_map/ppermute | solution.py:27
  12.7 1.2 %collective-permute-start.5 = (bf16[192,128]{1,0:T(8,128)(2,1)S(1)}, bf16[192,128]{1,0:T(8,128)(2,1)S(1)}, u32[]{:S(2)}, u32[]{:S(2)}) collective-permute-start(bf16[192,128]{1,0:T(8,128)(2,1)S(1)} %collective-permute-done.1.refs_2_), channel_id=1, source_target_pairs={{0,8},{1,9},{2,10},{3,11},{4,12},{5,13},{6,14},{7,15},{8,0},{9,1},... | collective-permute-start | bytes 147464 | tf_op jit(solution)/shard_map/ppermute | solution.py:27
  22.2 1.4 %collective-permute-start.6 = (f32[4,64,128]{2,1,0:T(8,128)S(1)}, f32[4,64,128]{2,1,0:T(8,128)S(1)}, u32[]{:S(2)}, u32[]{:S(2)}) collective-permute-start(f32[4,64,128]{2,1,0:T(8,128)S(1)} %get-tuple-element.52), channel_id=1, source_target_pairs={{0,8},{1,9},{2,10},{3,11},{4,12},{5,13},{6,14},{7,15},{8,0},{9,1},... | collective-permute-start | bytes 393224 | tf_op jit(solution)/shard_map/ppermute | solution.py:27
  23.6 6.1 %collective-permute-start.10 = (f32[64,128]{1,0:T(8,128)S(1)}, f32[64,128]{1,0:T(8,128)S(1)}, u32[]{:S(2)}, u32[]{:S(2)}) collective-permute-start(f32[64,128]{1,0:T(8,128)S(1)} %get-tuple-element.54), channel_id=1, source_target_pairs={{0,6},{1,7},{2,4},{3,5},{4,2},{5,3},{6,0},{7,1},{8,13},{9,12},{10,... | collective-permute-start | bytes 98312 | tf_op jit(solution)/shard_map/ppermute | solution.py:27
  24.7 5.7 %collective-permute-start.7 = (f32[64,128]{1,0:T(8,128)S(1)}, f32[64,128]{1,0:T(8,128)S(1)}, u32[]{:S(2)}, u32[]{:S(2)}) collective-permute-start(f32[64,128]{1,0:T(8,128)S(1)} %get-tuple-element.53), channel_id=1, source_target_pairs={{0,3},{1,2},{2,1},{3,0},{4,7},{5,6},{6,5},{7,4},{8,15},{9,14},{10,... | collective-permute-start | bytes 98312 | tf_op jit(solution)/shard_map/ppermute | solution.py:27
  26.0 4.4 %collective-permute-start.8 = (f32[64,128]{1,0:T(8,128)S(1)}, f32[64,128]{1,0:T(8,128)S(1)}, u32[]{:S(2)}, u32[]{:S(2)}) collective-permute-start(f32[64,128]{1,0:T(8,128)S(1)} %get-tuple-element.56), channel_id=1, source_target_pairs={{8,9},{9,8},{10,11},{11,10},{12,13},{13,12},{14,15},{15,14},{24,25... | collective-permute-start | bytes 98312 | tf_op jit(solution)/shard_map/ppermute | solution.py:27
  26.7 4.0 %collective-permute-start.9 = (f32[64,128]{1,0:T(8,128)S(1)}, f32[64,128]{1,0:T(8,128)S(1)}, u32[]{:S(2)}, u32[]{:S(2)}) collective-permute-start(f32[64,128]{1,0:T(8,128)S(1)} %get-tuple-element.55), channel_id=1, source_target_pairs={{0,4},{1,5},{2,6},{3,7},{4,0},{5,1},{6,2},{7,3},{8,10},{9,11},{10,... | collective-permute-start | bytes 98312 | tf_op jit(solution)/shard_map/ppermute | solution.py:27
  30.7 4.0 %collective-permute-start.11 = (f32[64,128]{1,0:T(8,128)S(1)}, f32[64,128]{1,0:T(8,128)S(1)}, u32[]{:S(2)}, u32[]{:S(2)}) collective-permute-start(f32[64,128]{1,0:T(8,128)S(1)} %add_add_fusion), channel_id=1, source_target_pairs={{0,16},{1,17},{2,18},{3,19},{4,20},{5,21},{6,22},{7,23},{8,24},{9,... | collective-permute-start | bytes 98312 | tf_op jit(solution)/shard_map/ppermute | solution.py:27
  34.6 1.2 %collective-permute-start.12 = (f32[64,128]{1,0:T(8,128)S(1)}, f32[64,128]{1,0:T(8,128)S(1)}, u32[]{:S(2)}, u32[]{:S(2)}) collective-permute-start(f32[64,128]{1,0:T(8,128)S(1)} %add.26), channel_id=1, source_target_pairs={{0,8},{1,9},{2,10},{3,11},{4,12},{5,13},{6,14},{7,15},{8,0},{9,1},... | collective-permute-start | bytes 98312 | tf_op jit(solution)/shard_map/ppermute | solution.py:27

commit v9 on v8

--- a/solution.py
+++ b/solution.py
@@ -40,7 +40,8 @@
     for side in sides:
         side = sorted(side, key=lambda at: (at[0] + at[1], at[0]))
         far = min(side, key=lambda at: (-at[0] - at[1], at[0]))
-        plan.append([far] + [at for at in side if at != far])
+        side.remove(far)
+        plan.append([far, *side[1::-1], *side[2:]])
     return plan
 
 
@@ -274,7 +275,7 @@
     )(mine, local, back)
     halos = [move(after(part, blocks), sizes, forward) for part in edges]
     rests = [
-        move(after(rests[d - 1], mixed), sizes, lambda i, j, k, d=d: (i, j ^ d, k))
+        move(after(rests[d - 1], blocks), sizes, lambda i, j, k, d=d: (i, j ^ d, k))
         for d in range(1, n_row)
     ]
 

time: 36.6 us -> 36.5 us (level)
  waiting for transfers between devices: 18.2 us -> 16.4 us
  starting transfers between devices: 13.4 us -> 15.1 us
    ppermute x13, waiting for transfers between devices: 18.2 us -> 16.4 us  [move(): return lax.ppermute(value, AXES, pairs)]
    ppermute x13, starting transfers between devices: 13.4 us -> 15.1 us  [move(): return lax.ppermute(value, AXES, pairs)]
  transfers between devices with their start and end apart: 13 -> 13, of which waited for: 11 -> 10; matrix products, arithmetic and copies ran while one was open for 0% -> 0% of each run, Pallas kernels for 6% -> 6%
where the time goes in v9:
time: 36.5 us; the launch traced here: 36.4 us
  waiting for transfers between devices  16.4 us (45%)
  starting transfers between devices  15.1 us (41%)
  Pallas kernels  2.82 us (8%)
  local copies, waits for them, and re-layouts  1.31 us (4%)
  other arithmetic  0.65 us (2%)
    ppermute x13, waiting for transfers between devices, move(): return lax.ppermute(value, AXES, pairs)  16.4 us
    ppermute x13, starting transfers between devices, move(): return lax.ppermute(value, AXES, pairs)  15.1 us
    unnamed x6, local copies, waits for them, and re-layouts  1.3 us
    pallas_call x1, Pallas kernels, per_device(): kernel(functools.partial(inner_kernel, n_row, centre), [array((whole, who...  0.9 us
  transfers between devices with their start and end apart: 13, of which 10 were waited for; matrix products, arithmetic and copies ran while one was open for 0% of the time, Pallas kernels for 6%

profile of v9, /device:TPU:0, one launch (start us, length us, event | category | flops | bytes accessed | tf_op | source)
XLA Modules:
  0.0 36.4 jit_solution(6352985567332967501)
XLA Ops:
  0.0 1.3 %copy-done.1 = bf16[8,128,512]{2,1,0:T(8,128)(2,1)S(1)} copy-done((bf16[8,128,512]{2,1,0:T(8,128)(2,1)S(1)}, bf16[8,128,512]{2,1,0:T(8,128)(2,1)}, u32[]{:S(2)}) %copy-start.1) | copy-done | bytes 1048600
  1.4 3.0 %collective-permute-start = (bf16[4,128,256]{2,1,0:T(8,128)(2,1)S(1)}, bf16[4,128,256]{2,1,0:T(8,128)(2,1)S(1)}, u32[]{:S(2)}, u32[]{:S(2)}) collective-permute-start(bf16[4,128,256]{2,1,0:T(8,128)(2,1)S(1)} %get-tuple-element.29), channel_id=1, source_target_pairs={{0,4},{1,5},{2,6},{3,7},{4,0},{5,1},{6,2},{7,3},{8,12},{9,13},{10,... | collective-permute-start | bytes 786440 | tf_op jit(solution)/shard_map/ppermute | solution.py:27
  4.6 1.6 %collective-permute-start.1 = (bf16[192,128]{1,0:T(8,128)(2,1)S(1)}, bf16[192,128]{1,0:T(8,128)(2,1)S(1)}, u32[]{:S(2)}, u32[]{:S(2)}) collective-permute-start(bf16[192,128]{1,0:T(8,128)(2,1)S(1)} %shard_map.38), channel_id=1, source_target_pairs={{0,1},{1,2},{2,3},{3,0},{4,5},{5,6},{6,7},{7,4},{8,9},{9,10},{10,1... | collective-permute-start | bytes 147464 | tf_op jit(solution)/shard_map/ppermute | solution.py:27
  6.2 1.6 %collective-permute-start.4 = (bf16[4,128,256]{2,1,0:T(8,128)(2,1)S(1)}, bf16[4,128,256]{2,1,0:T(8,128)(2,1)S(1)}, u32[]{:S(2)}, u32[]{:S(2)}) collective-permute-start(bf16[4,128,256]{2,1,0:T(8,128)(2,1)S(1)} %get-tuple-element.33), channel_id=1, source_target_pairs={{0,1},{1,2},{2,3},{3,0},{4,5},{5,6},{6,7},{7,4},{8,9},{9,10},{10,1... | collective-permute-start | bytes 786440 | tf_op jit(solution)/shard_map/ppermute | solution.py:27
  7.8 3.3 %collective-permute-done.1.refs_2_ = bf16[192,128]{1,0:T(8,128)(2,1)S(1)} collective-permute-done((bf16[192,128]{1,0:T(8,128)(2,1)S(1)}, bf16[192,128]{1,0:T(8,128)(2,1)S(1)}, u32[]{:S(2)}, u32[]{:S(2)}) %collective-permute-start.1) | collective-permute-done | bytes 49184 | tf_op jit(solution)/shard_map/ppermute | solution.py:27
  11.1 0.4 %collective-permute-start.3 = (bf16[4,128,256]{2,1,0:T(8,128)(2,1)S(1)}, bf16[4,128,256]{2,1,0:T(8,128)(2,1)S(1)}, u32[]{:S(2)}, u32[]{:S(2)}) collective-permute-start(bf16[4,128,256]{2,1,0:T(8,128)(2,1)S(1)} %get-tuple-element.32), channel_id=1, source_target_pairs={{0,4},{1,5},{2,6},{3,7},{4,0},{5,1},{6,2},{7,3},{8,12},{9,13},{10,... | collective-permute-start | bytes 786440 | tf_op jit(solution)/shard_map/ppermute | solution.py:27
  11.5 1.9 %collective-permute-start.2 = (bf16[4,128,256]{2,1,0:T(8,128)(2,1)S(1)}, bf16[4,128,256]{2,1,0:T(8,128)(2,1)S(1)}, u32[]{:S(2)}, u32[]{:S(2)}) collective-permute-start(bf16[4,128,256]{2,1,0:T(8,128)(2,1)S(1)} %collective-permute-done.refs_0_), channel_id=1, source_target_pairs={{0,1},{1,2},{2,3},{3,0},{4,5},{5,6},{6,7},{7,4},{8,9},{9,10},{10,1... | collective-permute-start | bytes 786440 | tf_op jit(solution)/shard_map/ppermute | solution.py:27
  13.7 0.5 %shard_map.40 = (bf16[128,1024]{1,0:T(8,128)(2,1)S(1)}, bf16[128,1024]{1,0:T(8,128)(2,1)S(1)}, f32[512,256]{1,0:T(8,128)S(1)}, bf16[128,1024]{1,0:T(8,128)(2,1)S(1)}, bf16[128,1024]{1,0:T(8,128)(2,1)S(1)}) custom-call(bf16[4,128,512]{2,1,0:T(8,128)(2,1)S(1)} %get-tuple-element.37.own_ref, bf16[512,512]{1,0:T(8,128)(2,1)S(1)} %get-tuple-element.35.local_ref.refs_1_.refs_4_, ...), custom_call_target="tpu_custom_call" | custom-call | flops 1 | bytes 1 | tf_op jit(solution)/shard_map/pallas_call | solution.py:265
  14.2 0.4 %shard_map.41 = (f32[256,128]{1,0:T(8,128)S(1)}, bf16[256,1024]{1,0:T(8,128)(2,1)S(1)}, f32[1,512,512]{2,1,0:T(8,128)S(1)}) custom-call(bf16[4,128,256]{2,1,0:T(8,128)(2,1)S(1)} %collective-permute-done.refs_0_, bf16[512,512]{1,0:T(8,128)(2,1)S(1)} %get-tuple-element.35.local_ref.refs_1_.refs_4_, bf16[128,1024]{1,0:T(8,128)(2,1)S(1)} %get-tuple-element.38.refs_2_, ...), custom_call_target="tpu_custom_call" | custom-call | flops 1 | bytes 1 | tf_op jit(solution)/shard_map/pallas_call | solution.py:282
  14.7 2.6 %collective-permute-done.4.refs_1_ = bf16[4,128,256]{2,1,0:T(8,128)(2,1)S(1)} collective-permute-done((bf16[4,128,256]{2,1,0:T(8,128)(2,1)S(1)}, bf16[4,128,256]{2,1,0:T(8,128)(2,1)S(1)}, u32[]{:S(2)}, u32[]{:S(2)}) %collective-permute-start.4) | collective-permute-done | bytes 262176 | tf_op jit(solution)/shard_map/ppermute | solution.py:27
  17.4 0.9 %shard_map.42 = (f32[256,256]{1,0:T(8,128)S(1)}, bf16[1024,256]{1,0:T(8,128)(2,1)S(1)}, bf16[1024,256]{1,0:T(8,128)(2,1)S(1)}, f32[1,512,256]{2,1,0:T(8,128)S(1)}, bf16[256,256]{1,0:T(8,128)(2,1)S(1)}) custom-call(bf16[4,128,256]{2,1,0:T(8,128)(2,1)S(1)} %collective-permute-done.3.refs_0_, bf16[4,128,256]{2,1,0:T(8,128)(2,1)S(1)} %collective-permute-done.4.refs_1_, ...), custom_call_target="tpu_custom_call" | custom-call | flops 1 | bytes 1 | tf_op jit(solution)/shard_map/pallas_call | solution.py:292
  18.4 3.3 %collective-permute-done.2.refs_0_ = bf16[4,128,256]{2,1,0:T(8,128)(2,1)S(1)} collective-permute-done((bf16[4,128,256]{2,1,0:T(8,128)(2,1)S(1)}, bf16[4,128,256]{2,1,0:T(8,128)(2,1)S(1)}, u32[]{:S(2)}, u32[]{:S(2)}) %collective-permute-start.2) | collective-permute-done | bytes 262176 | tf_op jit(solution)/shard_map/ppermute | solution.py:27
  21.7 0.5 %shard_map.43 = (f32[4,64,128]{2,1,0:T(8,128)S(1)}, f32[4,64,128]{2,1,0:T(8,128)S(1)}) custom-call(bf16[4,128,256]{2,1,0:T(8,128)(2,1)S(1)} %collective-permute-done.2.refs_0_, f32[256,256]{1,0:T(8,128)S(1)} %get-tuple-element.46.refs_1_, bf16[1024,256]{1,0:T(8,128)(2,1)S(1)} %get-tuple-element.47.refs_2_, bf16[1024,256]{1,0:T(8,128)(2,1)S(1)} %get-tuple-element.48.refs_3_, ...), custom_call_target="tpu_custom_call" | custom-call | flops 1 | bytes 1 | tf_op jit(solution)/shard_map/pallas_call | solution.py:306
  22.3 1.3 %collective-permute-done.6 = f32[4,64,128]{2,1,0:T(8,128)S(1)} collective-permute-done((f32[4,64,128]{2,1,0:T(8,128)S(1)}, f32[4,64,128]{2,1,0:T(8,128)S(1)}, u32[]{:S(2)}, u32[]{:S(2)}) %collective-permute-start.6) | collective-permute-done | bytes 131104 | tf_op jit(solution)/shard_map/ppermute | solution.py:27
  23.6 1.0 %collective-permute-start.10 = (f32[64,128]{1,0:T(8,128)S(1)}, f32[64,128]{1,0:T(8,128)S(1)}, u32[]{:S(2)}, u32[]{:S(2)}) collective-permute-start(f32[64,128]{1,0:T(8,128)S(1)} %get-tuple-element.54), channel_id=1, source_target_pairs={{0,6},{1,7},{2,4},{3,5},{4,2},{5,3},{6,0},{7,1},{8,13},{9,12},{10,... | collective-permute-start | bytes 98312 | tf_op jit(solution)/shard_map/ppermute | solution.py:27
  24.7 1.3 %collective-permute-start.7 = (f32[64,128]{1,0:T(8,128)S(1)}, f32[64,128]{1,0:T(8,128)S(1)}, u32[]{:S(2)}, u32[]{:S(2)}) collective-permute-start(f32[64,128]{1,0:T(8,128)S(1)} %get-tuple-element.53), channel_id=1, source_target_pairs={{0,3},{1,2},{2,1},{3,0},{4,7},{5,6},{6,5},{7,4},{8,15},{9,14},{10,... | collective-permute-start | bytes 98312 | tf_op jit(solution)/shard_map/ppermute | solution.py:27
  26.0 1.3 %collective-permute-start.8 = (f32[64,128]{1,0:T(8,128)S(1)}, f32[64,128]{1,0:T(8,128)S(1)}, u32[]{:S(2)}, u32[]{:S(2)}) collective-permute-start(f32[64,128]{1,0:T(8,128)S(1)} %get-tuple-element.55), channel_id=1, source_target_pairs={{0,4},{1,5},{2,6},{3,7},{4,0},{5,1},{6,2},{7,3},{8,10},{9,11},{10,... | collective-permute-start | bytes 98312 | tf_op jit(solution)/shard_map/ppermute | solution.py:27
  27.3 0.7 %collective-permute-start.9 = (f32[64,128]{1,0:T(8,128)S(1)}, f32[64,128]{1,0:T(8,128)S(1)}, u32[]{:S(2)}, u32[]{:S(2)}) collective-permute-start(f32[64,128]{1,0:T(8,128)S(1)} %get-tuple-element.56), channel_id=1, source_target_pairs={{8,9},{9,8},{10,11},{11,10},{12,13},{13,12},{14,15},{15,14},{24,25... | collective-permute-start | bytes 98312 | tf_op jit(solution)/shard_map/ppermute | solution.py:27
  28.0 2.2 %collective-permute-done.10 = f32[64,128]{1,0:T(8,128)S(1)} collective-permute-done((f32[64,128]{1,0:T(8,128)S(1)}, f32[64,128]{1,0:T(8,128)S(1)}, u32[]{:S(2)}, u32[]{:S(2)}) %collective-permute-start.10) | collective-permute-done | bytes 32800 | tf_op jit(solution)/shard_map/ppermute | solution.py:27
  30.4 1.6 %collective-permute-start.11 = (f32[64,128]{1,0:T(8,128)S(1)}, f32[64,128]{1,0:T(8,128)S(1)}, u32[]{:S(2)}, u32[]{:S(2)}) collective-permute-start(f32[64,128]{1,0:T(8,128)S(1)} %add_add_fusion), channel_id=1, source_target_pairs={{0,16},{1,17},{2,18},{3,19},{4,20},{5,21},{6,22},{7,23},{8,24},{9,... | collective-permute-start | bytes 98312 | tf_op jit(solution)/shard_map/ppermute | solution.py:27
  31.9 2.4 %collective-permute-done.11 = f32[64,128]{1,0:T(8,128)S(1)} collective-permute-done((f32[64,128]{1,0:T(8,128)S(1)}, f32[64,128]{1,0:T(8,128)S(1)}, u32[]{:S(2)}, u32[]{:S(2)}) %collective-permute-start.11) | collective-permute-done | bytes 32800 | tf_op jit(solution)/shard_map/ppermute | solution.py:27
  34.4 0.5 %collective-permute-start.12 = (f32[64,128]{1,0:T(8,128)S(1)}, f32[64,128]{1,0:T(8,128)S(1)}, u32[]{:S(2)}, u32[]{:S(2)}) collective-permute-start(f32[64,128]{1,0:T(8,128)S(1)} %add.26), channel_id=1, source_target_pairs={{0,8},{1,9},{2,10},{3,11},{4,12},{5,13},{6,14},{7,15},{8,0},{9,1},... | collective-permute-start | bytes 98312 | tf_op jit(solution)/shard_map/ppermute | solution.py:27
  34.9 0.9 %collective-permute-done.12 = f32[64,128]{1,0:T(8,128)S(1)} collective-permute-done((f32[64,128]{1,0:T(8,128)S(1)}, f32[64,128]{1,0:T(8,128)S(1)}, u32[]{:S(2)}, u32[]{:S(2)}) %collective-permute-start.12) | collective-permute-done | bytes 32800 | tf_op jit(solution)/shard_map/ppermute | solution.py:27
  35.8 0.6 %add.27 = f32[64,128]{1,0:T(8,128)} add(f32[64,128]{1,0:T(8,128)S(1)} %add.26, f32[64,128]{1,0:T(8,128)S(1)} %collective-permute-done.12) | non-fusion elementwise | flops 8192 | bytes 98304 | tf_op jit(solution)/shard_map/add | solution.py:325
  (20 shorter events, 1.0 us)
Async XLA Ops:
  0.0 4.5 %copy-start = (bf16[512,5,128]{2,0,1:T(8,128)(2,1)S(1)}, bf16[512,5,128]{2,0,1:T(8,128)(2,1)}, u32[]{:S(2)}) copy-start(bf16[512,5,128]{2,0,1:T(8,128)(2,1)} %param.4) | copy-start | bytes 1966084
  0.0 1.3 %copy-start.1 = (bf16[8,128,512]{2,1,0:T(8,128)(2,1)S(1)}, bf16[8,128,512]{2,1,0:T(8,128)(2,1)}, u32[]{:S(2)}) copy-start(bf16[8,128,512]{2,1,0:T(8,128)(2,1)} %tensor_ref.1) | copy-start | bytes 3145732
  1.4 3.0 %copy-start.2 = (s32[4,5]{1,0:T(4,128)S(1)}, s32[4,5]{1,0:T(4,128)}, u32[]{:S(2)}) copy-start(s32[4,5]{1,0:T(4,128)} %mask_ref.3) | copy-start | bytes 244
  1.4 10.1 %collective-permute-start = (bf16[4,128,256]{2,1,0:T(8,128)(2,1)S(1)}, bf16[4,128,256]{2,1,0:T(8,128)(2,1)S(1)}, u32[]{:S(2)}, u32[]{:S(2)}) collective-permute-start(bf16[4,128,256]{2,1,0:T(8,128)(2,1)S(1)} %get-tuple-element.29), channel_id=1, source_target_pairs={{0,4},{1,5},{2,6},{3,7},{4,0},{5,1},{6,2},{7,3},{8,12},{9,13},{10,... | collective-permute-start | bytes 786440 | tf_op jit(solution)/shard_map/ppermute | solution.py:27
  4.6 6.5 %collective-permute-start.1 = (bf16[192,128]{1,0:T(8,128)(2,1)S(1)}, bf16[192,128]{1,0:T(8,128)(2,1)S(1)}, u32[]{:S(2)}, u32[]{:S(2)}) collective-permute-start(bf16[192,128]{1,0:T(8,128)(2,1)S(1)} %shard_map.38), channel_id=1, source_target_pairs={{0,1},{1,2},{2,3},{3,0},{4,5},{5,6},{6,7},{7,4},{8,9},{9,10},{10,1... | collective-permute-start | bytes 147464 | tf_op jit(solution)/shard_map/ppermute | solution.py:27
  6.2 11.0 %collective-permute-start.4 = (bf16[4,128,256]{2,1,0:T(8,128)(2,1)S(1)}, bf16[4,128,256]{2,1,0:T(8,128)(2,1)S(1)}, u32[]{:S(2)}, u32[]{:S(2)}) collective-permute-start(bf16[4,128,256]{2,1,0:T(8,128)(2,1)S(1)} %get-tuple-element.33), channel_id=1, source_target_pairs={{0,1},{1,2},{2,3},{3,0},{4,5},{5,6},{6,7},{7,4},{8,9},{9,10},{10,1... | collective-permute-start | bytes 786440 | tf_op jit(solution)/shard_map/ppermute | solution.py:27
  11.1 6.4 %collective-permute-start.3 = (bf16[4,128,256]{2,1,0:T(8,128)(2,1)S(1)}, bf16[4,128,256]{2,1,0:T(8,128)(2,1)S(1)}, u32[]{:S(2)}, u32[]{:S(2)}) collective-permute-start(bf16[4,128,256]{2,1,0:T(8,128)(2,1)S(1)} %get-tuple-element.32), channel_id=1, source_target_pairs={{0,4},{1,5},{2,6},{3,7},{4,0},{5,1},{6,2},{7,3},{8,12},{9,13},{10,... | collective-permute-start | bytes 786440 | tf_op jit(solution)/shard_map/ppermute | solution.py:27
  11.5 10.1 %collective-permute-start.2 = (bf16[4,128,256]{2,1,0:T(8,128)(2,1)S(1)}, bf16[4,128,256]{2,1,0:T(8,128)(2,1)S(1)}, u32[]{:S(2)}, u32[]{:S(2)}) collective-permute-start(bf16[4,128,256]{2,1,0:T(8,128)(2,1)S(1)} %collective-permute-done.refs_0_), channel_id=1, source_target_pairs={{0,1},{1,2},{2,3},{3,0},{4,5},{5,6},{6,7},{7,4},{8,9},{9,10},{10,1... | collective-permute-start | bytes 786440 | tf_op jit(solution)/shard_map/ppermute | solution.py:27
  13.5 1.2 %collective-permute-start.5 = (bf16[192,128]{1,0:T(8,128)(2,1)S(1)}, bf16[192,128]{1,0:T(8,128)(2,1)S(1)}, u32[]{:S(2)}, u32[]{:S(2)}) collective-permute-start(bf16[192,128]{1,0:T(8,128)(2,1)S(1)} %collective-permute-done.1.refs_2_), channel_id=1, source_target_pairs={{0,8},{1,9},{2,10},{3,11},{4,12},{5,13},{6,14},{7,15},{8,0},{9,1},... | collective-permute-start | bytes 147464 | tf_op jit(solution)/shard_map/ppermute | solution.py:27
  22.2 1.4 %collective-permute-start.6 = (f32[4,64,128]{2,1,0:T(8,128)S(1)}, f32[4,64,128]{2,1,0:T(8,128)S(1)}, u32[]{:S(2)}, u32[]{:S(2)}) collective-permute-start(f32[4,64,128]{2,1,0:T(8,128)S(1)} %get-tuple-element.52), channel_id=1, source_target_pairs={{0,8},{1,9},{2,10},{3,11},{4,12},{5,13},{6,14},{7,15},{8,0},{9,1},... | collective-permute-start | bytes 393224 | tf_op jit(solution)/shard_map/ppermute | solution.py:27
  23.6 6.5 %collective-permute-start.10 = (f32[64,128]{1,0:T(8,128)S(1)}, f32[64,128]{1,0:T(8,128)S(1)}, u32[]{:S(2)}, u32[]{:S(2)}) collective-permute-start(f32[64,128]{1,0:T(8,128)S(1)} %get-tuple-element.54), channel_id=1, source_target_pairs={{0,6},{1,7},{2,4},{3,5},{4,2},{5,3},{6,0},{7,1},{8,13},{9,12},{10,... | collective-permute-start | bytes 98312 | tf_op jit(solution)/shard_map/ppermute | solution.py:27
  24.7 5.7 %collective-permute-start.7 = (f32[64,128]{1,0:T(8,128)S(1)}, f32[64,128]{1,0:T(8,128)S(1)}, u32[]{:S(2)}, u32[]{:S(2)}) collective-permute-start(f32[64,128]{1,0:T(8,128)S(1)} %get-tuple-element.53), channel_id=1, source_target_pairs={{0,3},{1,2},{2,1},{3,0},{4,7},{5,6},{6,5},{7,4},{8,15},{9,14},{10,... | collective-permute-start | bytes 98312 | tf_op jit(solution)/shard_map/ppermute | solution.py:27
  26.0 4.4 %collective-permute-start.8 = (f32[64,128]{1,0:T(8,128)S(1)}, f32[64,128]{1,0:T(8,128)S(1)}, u32[]{:S(2)}, u32[]{:S(2)}) collective-permute-start(f32[64,128]{1,0:T(8,128)S(1)} %get-tuple-element.55), channel_id=1, source_target_pairs={{0,4},{1,5},{2,6},{3,7},{4,0},{5,1},{6,2},{7,3},{8,10},{9,11},{10,... | collective-permute-start | bytes 98312 | tf_op jit(solution)/shard_map/ppermute | solution.py:27
  27.3 3.1 %collective-permute-start.9 = (f32[64,128]{1,0:T(8,128)S(1)}, f32[64,128]{1,0:T(8,128)S(1)}, u32[]{:S(2)}, u32[]{:S(2)}) collective-permute-start(f32[64,128]{1,0:T(8,128)S(1)} %get-tuple-element.56), channel_id=1, source_target_pairs={{8,9},{9,8},{10,11},{11,10},{12,13},{13,12},{14,15},{15,14},{24,25... | collective-permute-start | bytes 98312 | tf_op jit(solution)/shard_map/ppermute | solution.py:27
  30.4 4.0 %collective-permute-start.11 = (f32[64,128]{1,0:T(8,128)S(1)}, f32[64,128]{1,0:T(8,128)S(1)}, u32[]{:S(2)}, u32[]{:S(2)}) collective-permute-start(f32[64,128]{1,0:T(8,128)S(1)} %add_add_fusion), channel_id=1, source_target_pairs={{0,16},{1,17},{2,18},{3,19},{4,20},{5,21},{6,22},{7,23},{8,24},{9,... | collective-permute-start | bytes 98312 | tf_op jit(solution)/shard_map/ppermute | solution.py:27
  34.4 1.4 %collective-permute-start.12 = (f32[64,128]{1,0:T(8,128)S(1)}, f32[64,128]{1,0:T(8,128)S(1)}, u32[]{:S(2)}, u32[]{:S(2)}) collective-permute-start(f32[64,128]{1,0:T(8,128)S(1)} %add.26), channel_id=1, source_target_pairs={{0,8},{1,9},{2,10},{3,11},{4,12},{5,13},{6,14},{7,15},{8,0},{9,1},... | collective-permute-start | bytes 98312 | tf_op jit(solution)/shard_map/ppermute | solution.py:27

commit v10 on v9

--- a/solution.py
+++ b/solution.py
@@ -193,10 +193,12 @@
     lines = times(jnp.concatenate([side_by_side(halo[...]) for halo in halos], axis=0), behind_ref[...])
     for d in range(count):
         at = slice(d * rows, (d + 1) * rows)
-        kx_ref[d, :rows] = inner_ref[:rows, at]
-        kx_ref[d, rows:] = inner_ref[rows:, at] + lines[:, at]
+        upper, lower = inner_ref[:rows, at], inner_ref[rows:, at] + lines[:, at]
         if d > 0:
-            kx_ref[d] += columns[:, (d - 1) * rows : d * rows]
+            add = columns[:, (d - 1) * rows : d * rows]
+            upper, lower = upper + add[:rows], lower + add[rows:]
+        kx_ref[d, :rows] = upper
+        kx_ref[d, rows:] = lower
     out_rows = count * rows // sizes[2]
     per_group = rows // out_rows
     for ref, side in ((give_ref, 1 - core), (keep_ref, core)):

time: 36.5 us -> 36.5 us (level)
  no operation moved by 1% of the time
where the time goes in v10:
time: 36.5 us; the launch traced here: 36.4 us
  waiting for transfers between devices  16.4 us (45%)
  starting transfers between devices  15.1 us (41%)
  Pallas kernels  2.82 us (8%)
  local copies, waits for them, and re-layouts  1.31 us (4%)
  other arithmetic  0.65 us (2%)
    ppermute x13, waiting for transfers between devices, move(): return lax.ppermute(value, AXES, pairs)  16.4 us
    ppermute x13, starting transfers between devices, move(): return lax.ppermute(value, AXES, pairs)  15.1 us
    unnamed x6, local copies, waits for them, and re-layouts  1.3 us
    pallas_call x1, Pallas kernels, per_device(): kernel(functools.partial(inner_kernel, n_row, centre), [array((whole, who...  0.9 us
  transfers between devices with their start and end apart: 13, of which 10 were waited for; matrix products, arithmetic and copies ran while one was open for 0% of the time, Pallas kernels for 6%

profile of v10, /device:TPU:0, one launch (start us, length us, event | category | flops | bytes accessed | tf_op | source)
XLA Modules:
  0.0 36.4 jit_solution(8196152831387602646)
XLA Ops:
  0.0 1.3 %copy-done.1 = bf16[8,128,512]{2,1,0:T(8,128)(2,1)S(1)} copy-done((bf16[8,128,512]{2,1,0:T(8,128)(2,1)S(1)}, bf16[8,128,512]{2,1,0:T(8,128)(2,1)}, u32[]{:S(2)}) %copy-start.1) | copy-done | bytes 1048600
  1.4 3.0 %collective-permute-start = (bf16[4,128,256]{2,1,0:T(8,128)(2,1)S(1)}, bf16[4,128,256]{2,1,0:T(8,128)(2,1)S(1)}, u32[]{:S(2)}, u32[]{:S(2)}) collective-permute-start(bf16[4,128,256]{2,1,0:T(8,128)(2,1)S(1)} %get-tuple-element.29), channel_id=1, source_target_pairs={{0,4},{1,5},{2,6},{3,7},{4,0},{5,1},{6,2},{7,3},{8,12},{9,13},{10,... | collective-permute-start | bytes 786440 | tf_op jit(solution)/shard_map/ppermute | solution.py:27
  4.6 1.6 %collective-permute-start.1 = (bf16[192,128]{1,0:T(8,128)(2,1)S(1)}, bf16[192,128]{1,0:T(8,128)(2,1)S(1)}, u32[]{:S(2)}, u32[]{:S(2)}) collective-permute-start(bf16[192,128]{1,0:T(8,128)(2,1)S(1)} %shard_map.38), channel_id=1, source_target_pairs={{0,1},{1,2},{2,3},{3,0},{4,5},{5,6},{6,7},{7,4},{8,9},{9,10},{10,1... | collective-permute-start | bytes 147464 | tf_op jit(solution)/shard_map/ppermute | solution.py:27
  6.2 1.6 %collective-permute-start.4 = (bf16[4,128,256]{2,1,0:T(8,128)(2,1)S(1)}, bf16[4,128,256]{2,1,0:T(8,128)(2,1)S(1)}, u32[]{:S(2)}, u32[]{:S(2)}) collective-permute-start(bf16[4,128,256]{2,1,0:T(8,128)(2,1)S(1)} %get-tuple-element.33), channel_id=1, source_target_pairs={{0,1},{1,2},{2,3},{3,0},{4,5},{5,6},{6,7},{7,4},{8,9},{9,10},{10,1... | collective-permute-start | bytes 786440 | tf_op jit(solution)/shard_map/ppermute | solution.py:27
  7.8 3.3 %collective-permute-done.1.refs_2_ = bf16[192,128]{1,0:T(8,128)(2,1)S(1)} collective-permute-done((bf16[192,128]{1,0:T(8,128)(2,1)S(1)}, bf16[192,128]{1,0:T(8,128)(2,1)S(1)}, u32[]{:S(2)}, u32[]{:S(2)}) %collective-permute-start.1) | collective-permute-done | bytes 49184 | tf_op jit(solution)/shard_map/ppermute | solution.py:27
  11.1 0.4 %collective-permute-start.3 = (bf16[4,128,256]{2,1,0:T(8,128)(2,1)S(1)}, bf16[4,128,256]{2,1,0:T(8,128)(2,1)S(1)}, u32[]{:S(2)}, u32[]{:S(2)}) collective-permute-start(bf16[4,128,256]{2,1,0:T(8,128)(2,1)S(1)} %get-tuple-element.32), channel_id=1, source_target_pairs={{0,4},{1,5},{2,6},{3,7},{4,0},{5,1},{6,2},{7,3},{8,12},{9,13},{10,... | collective-permute-start | bytes 786440 | tf_op jit(solution)/shard_map/ppermute | solution.py:27
  11.5 1.9 %collective-permute-start.2 = (bf16[4,128,256]{2,1,0:T(8,128)(2,1)S(1)}, bf16[4,128,256]{2,1,0:T(8,128)(2,1)S(1)}, u32[]{:S(2)}, u32[]{:S(2)}) collective-permute-start(bf16[4,128,256]{2,1,0:T(8,128)(2,1)S(1)} %collective-permute-done.refs_0_), channel_id=1, source_target_pairs={{0,1},{1,2},{2,3},{3,0},{4,5},{5,6},{6,7},{7,4},{8,9},{9,10},{10,1... | collective-permute-start | bytes 786440 | tf_op jit(solution)/shard_map/ppermute | solution.py:27
  13.7 0.5 %shard_map.40 = (bf16[128,1024]{1,0:T(8,128)(2,1)S(1)}, bf16[128,1024]{1,0:T(8,128)(2,1)S(1)}, f32[512,256]{1,0:T(8,128)S(1)}, bf16[128,1024]{1,0:T(8,128)(2,1)S(1)}, bf16[128,1024]{1,0:T(8,128)(2,1)S(1)}) custom-call(bf16[4,128,512]{2,1,0:T(8,128)(2,1)S(1)} %get-tuple-element.37.own_ref, bf16[512,512]{1,0:T(8,128)(2,1)S(1)} %get-tuple-element.35.local_ref.refs_1_.refs_4_, ...), custom_call_target="tpu_custom_call" | custom-call | flops 1 | bytes 1 | tf_op jit(solution)/shard_map/pallas_call | solution.py:267
  14.2 0.4 %shard_map.41 = (f32[256,128]{1,0:T(8,128)S(1)}, bf16[256,1024]{1,0:T(8,128)(2,1)S(1)}, f32[1,512,512]{2,1,0:T(8,128)S(1)}) custom-call(bf16[4,128,256]{2,1,0:T(8,128)(2,1)S(1)} %collective-permute-done.refs_0_, bf16[512,512]{1,0:T(8,128)(2,1)S(1)} %get-tuple-element.35.local_ref.refs_1_.refs_4_, bf16[128,1024]{1,0:T(8,128)(2,1)S(1)} %get-tuple-element.38.refs_2_, ...), custom_call_target="tpu_custom_call" | custom-call | flops 1 | bytes 1 | tf_op jit(solution)/shard_map/pallas_call | solution.py:284
  14.7 2.6 %collective-permute-done.4.refs_1_ = bf16[4,128,256]{2,1,0:T(8,128)(2,1)S(1)} collective-permute-done((bf16[4,128,256]{2,1,0:T(8,128)(2,1)S(1)}, bf16[4,128,256]{2,1,0:T(8,128)(2,1)S(1)}, u32[]{:S(2)}, u32[]{:S(2)}) %collective-permute-start.4) | collective-permute-done | bytes 262176 | tf_op jit(solution)/shard_map/ppermute | solution.py:27
  17.4 0.9 %shard_map.42 = (f32[256,256]{1,0:T(8,128)S(1)}, bf16[1024,256]{1,0:T(8,128)(2,1)S(1)}, bf16[1024,256]{1,0:T(8,128)(2,1)S(1)}, f32[1,512,256]{2,1,0:T(8,128)S(1)}, bf16[256,256]{1,0:T(8,128)(2,1)S(1)}) custom-call(bf16[4,128,256]{2,1,0:T(8,128)(2,1)S(1)} %collective-permute-done.3.refs_0_, bf16[4,128,256]{2,1,0:T(8,128)(2,1)S(1)} %collective-permute-done.4.refs_1_, ...), custom_call_target="tpu_custom_call" | custom-call | flops 1 | bytes 1 | tf_op jit(solution)/shard_map/pallas_call | solution.py:294
  18.4 3.3 %collective-permute-done.2.refs_0_ = bf16[4,128,256]{2,1,0:T(8,128)(2,1)S(1)} collective-permute-done((bf16[4,128,256]{2,1,0:T(8,128)(2,1)S(1)}, bf16[4,128,256]{2,1,0:T(8,128)(2,1)S(1)}, u32[]{:S(2)}, u32[]{:S(2)}) %collective-permute-start.2) | collective-permute-done | bytes 262176 | tf_op jit(solution)/shard_map/ppermute | solution.py:27
  21.7 0.5 %shard_map.43 = (f32[4,64,128]{2,1,0:T(8,128)S(1)}, f32[4,64,128]{2,1,0:T(8,128)S(1)}) custom-call(bf16[4,128,256]{2,1,0:T(8,128)(2,1)S(1)} %collective-permute-done.2.refs_0_, f32[256,256]{1,0:T(8,128)S(1)} %get-tuple-element.46.refs_1_, bf16[1024,256]{1,0:T(8,128)(2,1)S(1)} %get-tuple-element.47.refs_2_, bf16[1024,256]{1,0:T(8,128)(2,1)S(1)} %get-tuple-element.48.refs_3_, ...), custom_call_target="tpu_custom_call" | custom-call | flops 1 | bytes 1 | tf_op jit(solution)/shard_map/pallas_call | solution.py:308
  22.3 1.3 %collective-permute-done.6 = f32[4,64,128]{2,1,0:T(8,128)S(1)} collective-permute-done((f32[4,64,128]{2,1,0:T(8,128)S(1)}, f32[4,64,128]{2,1,0:T(8,128)S(1)}, u32[]{:S(2)}, u32[]{:S(2)}) %collective-permute-start.6) | collective-permute-done | bytes 131104 | tf_op jit(solution)/shard_map/ppermute | solution.py:27
  23.6 1.0 %collective-permute-start.10 = (f32[64,128]{1,0:T(8,128)S(1)}, f32[64,128]{1,0:T(8,128)S(1)}, u32[]{:S(2)}, u32[]{:S(2)}) collective-permute-start(f32[64,128]{1,0:T(8,128)S(1)} %get-tuple-element.54), channel_id=1, source_target_pairs={{0,6},{1,7},{2,4},{3,5},{4,2},{5,3},{6,0},{7,1},{8,13},{9,12},{10,... | collective-permute-start | bytes 98312 | tf_op jit(solution)/shard_map/ppermute | solution.py:27
  24.7 1.3 %collective-permute-start.7 = (f32[64,128]{1,0:T(8,128)S(1)}, f32[64,128]{1,0:T(8,128)S(1)}, u32[]{:S(2)}, u32[]{:S(2)}) collective-permute-start(f32[64,128]{1,0:T(8,128)S(1)} %get-tuple-element.53), channel_id=1, source_target_pairs={{0,3},{1,2},{2,1},{3,0},{4,7},{5,6},{6,5},{7,4},{8,15},{9,14},{10,... | collective-permute-start | bytes 98312 | tf_op jit(solution)/shard_map/ppermute | solution.py:27
  26.0 1.3 %collective-permute-start.8 = (f32[64,128]{1,0:T(8,128)S(1)}, f32[64,128]{1,0:T(8,128)S(1)}, u32[]{:S(2)}, u32[]{:S(2)}) collective-permute-start(f32[64,128]{1,0:T(8,128)S(1)} %get-tuple-element.55), channel_id=1, source_target_pairs={{0,4},{1,5},{2,6},{3,7},{4,0},{5,1},{6,2},{7,3},{8,10},{9,11},{10,... | collective-permute-start | bytes 98312 | tf_op jit(solution)/shard_map/ppermute | solution.py:27
  27.3 0.7 %collective-permute-start.9 = (f32[64,128]{1,0:T(8,128)S(1)}, f32[64,128]{1,0:T(8,128)S(1)}, u32[]{:S(2)}, u32[]{:S(2)}) collective-permute-start(f32[64,128]{1,0:T(8,128)S(1)} %get-tuple-element.56), channel_id=1, source_target_pairs={{8,9},{9,8},{10,11},{11,10},{12,13},{13,12},{14,15},{15,14},{24,25... | collective-permute-start | bytes 98312 | tf_op jit(solution)/shard_map/ppermute | solution.py:27
  28.0 2.2 %collective-permute-done.10 = f32[64,128]{1,0:T(8,128)S(1)} collective-permute-done((f32[64,128]{1,0:T(8,128)S(1)}, f32[64,128]{1,0:T(8,128)S(1)}, u32[]{:S(2)}, u32[]{:S(2)}) %collective-permute-start.10) | collective-permute-done | bytes 32800 | tf_op jit(solution)/shard_map/ppermute | solution.py:27
  30.4 1.6 %collective-permute-start.11 = (f32[64,128]{1,0:T(8,128)S(1)}, f32[64,128]{1,0:T(8,128)S(1)}, u32[]{:S(2)}, u32[]{:S(2)}) collective-permute-start(f32[64,128]{1,0:T(8,128)S(1)} %add_add_fusion), channel_id=1, source_target_pairs={{0,16},{1,17},{2,18},{3,19},{4,20},{5,21},{6,22},{7,23},{8,24},{9,... | collective-permute-start | bytes 98312 | tf_op jit(solution)/shard_map/ppermute | solution.py:27
  31.9 2.4 %collective-permute-done.11 = f32[64,128]{1,0:T(8,128)S(1)} collective-permute-done((f32[64,128]{1,0:T(8,128)S(1)}, f32[64,128]{1,0:T(8,128)S(1)}, u32[]{:S(2)}, u32[]{:S(2)}) %collective-permute-start.11) | collective-permute-done | bytes 32800 | tf_op jit(solution)/shard_map/ppermute | solution.py:27
  34.4 0.5 %collective-permute-start.12 = (f32[64,128]{1,0:T(8,128)S(1)}, f32[64,128]{1,0:T(8,128)S(1)}, u32[]{:S(2)}, u32[]{:S(2)}) collective-permute-start(f32[64,128]{1,0:T(8,128)S(1)} %add.26), channel_id=1, source_target_pairs={{0,8},{1,9},{2,10},{3,11},{4,12},{5,13},{6,14},{7,15},{8,0},{9,1},... | collective-permute-start | bytes 98312 | tf_op jit(solution)/shard_map/ppermute | solution.py:27
  34.9 0.9 %collective-permute-done.12 = f32[64,128]{1,0:T(8,128)S(1)} collective-permute-done((f32[64,128]{1,0:T(8,128)S(1)}, f32[64,128]{1,0:T(8,128)S(1)}, u32[]{:S(2)}, u32[]{:S(2)}) %collective-permute-start.12) | collective-permute-done | bytes 32800 | tf_op jit(solution)/shard_map/ppermute | solution.py:27
  35.8 0.6 %add.27 = f32[64,128]{1,0:T(8,128)} add(f32[64,128]{1,0:T(8,128)S(1)} %add.26, f32[64,128]{1,0:T(8,128)S(1)} %collective-permute-done.12) | non-fusion elementwise | flops 8192 | bytes 98304 | tf_op jit(solution)/shard_map/add | solution.py:327
  (20 shorter events, 1.0 us)
Async XLA Ops:
  0.0 4.5 %copy-start = (bf16[512,5,128]{2,0,1:T(8,128)(2,1)S(1)}, bf16[512,5,128]{2,0,1:T(8,128)(2,1)}, u32[]{:S(2)}) copy-start(bf16[512,5,128]{2,0,1:T(8,128)(2,1)} %param.4) | copy-start | bytes 1966084
  0.0 1.3 %copy-start.1 = (bf16[8,128,512]{2,1,0:T(8,128)(2,1)S(1)}, bf16[8,128,512]{2,1,0:T(8,128)(2,1)}, u32[]{:S(2)}) copy-start(bf16[8,128,512]{2,1,0:T(8,128)(2,1)} %tensor_ref.1) | copy-start | bytes 3145732
  1.4 3.0 %copy-start.2 = (s32[4,5]{1,0:T(4,128)S(1)}, s32[4,5]{1,0:T(4,128)}, u32[]{:S(2)}) copy-start(s32[4,5]{1,0:T(4,128)} %mask_ref.3) | copy-start | bytes 244
  1.4 10.1 %collective-permute-start = (bf16[4,128,256]{2,1,0:T(8,128)(2,1)S(1)}, bf16[4,128,256]{2,1,0:T(8,128)(2,1)S(1)}, u32[]{:S(2)}, u32[]{:S(2)}) collective-permute-start(bf16[4,128,256]{2,1,0:T(8,128)(2,1)S(1)} %get-tuple-element.29), channel_id=1, source_target_pairs={{0,4},{1,5},{2,6},{3,7},{4,0},{5,1},{6,2},{7,3},{8,12},{9,13},{10,... | collective-permute-start | bytes 786440 | tf_op jit(solution)/shard_map/ppermute | solution.py:27
  4.6 6.5 %collective-permute-start.1 = (bf16[192,128]{1,0:T(8,128)(2,1)S(1)}, bf16[192,128]{1,0:T(8,128)(2,1)S(1)}, u32[]{:S(2)}, u32[]{:S(2)}) collective-permute-start(bf16[192,128]{1,0:T(8,128)(2,1)S(1)} %shard_map.38), channel_id=1, source_target_pairs={{0,1},{1,2},{2,3},{3,0},{4,5},{5,6},{6,7},{7,4},{8,9},{9,10},{10,1... | collective-permute-start | bytes 147464 | tf_op jit(solution)/shard_map/ppermute | solution.py:27
  6.2 11.0 %collective-permute-start.4 = (bf16[4,128,256]{2,1,0:T(8,128)(2,1)S(1)}, bf16[4,128,256]{2,1,0:T(8,128)(2,1)S(1)}, u32[]{:S(2)}, u32[]{:S(2)}) collective-permute-start(bf16[4,128,256]{2,1,0:T(8,128)(2,1)S(1)} %get-tuple-element.33), channel_id=1, source_target_pairs={{0,1},{1,2},{2,3},{3,0},{4,5},{5,6},{6,7},{7,4},{8,9},{9,10},{10,1... | collective-permute-start | bytes 786440 | tf_op jit(solution)/shard_map/ppermute | solution.py:27
  11.1 6.4 %collective-permute-start.3 = (bf16[4,128,256]{2,1,0:T(8,128)(2,1)S(1)}, bf16[4,128,256]{2,1,0:T(8,128)(2,1)S(1)}, u32[]{:S(2)}, u32[]{:S(2)}) collective-permute-start(bf16[4,128,256]{2,1,0:T(8,128)(2,1)S(1)} %get-tuple-element.32), channel_id=1, source_target_pairs={{0,4},{1,5},{2,6},{3,7},{4,0},{5,1},{6,2},{7,3},{8,12},{9,13},{10,... | collective-permute-start | bytes 786440 | tf_op jit(solution)/shard_map/ppermute | solution.py:27
  11.5 10.1 %collective-permute-start.2 = (bf16[4,128,256]{2,1,0:T(8,128)(2,1)S(1)}, bf16[4,128,256]{2,1,0:T(8,128)(2,1)S(1)}, u32[]{:S(2)}, u32[]{:S(2)}) collective-permute-start(bf16[4,128,256]{2,1,0:T(8,128)(2,1)S(1)} %collective-permute-done.refs_0_), channel_id=1, source_target_pairs={{0,1},{1,2},{2,3},{3,0},{4,5},{5,6},{6,7},{7,4},{8,9},{9,10},{10,1... | collective-permute-start | bytes 786440 | tf_op jit(solution)/shard_map/ppermute | solution.py:27
  13.5 1.2 %collective-permute-start.5 = (bf16[192,128]{1,0:T(8,128)(2,1)S(1)}, bf16[192,128]{1,0:T(8,128)(2,1)S(1)}, u32[]{:S(2)}, u32[]{:S(2)}) collective-permute-start(bf16[192,128]{1,0:T(8,128)(2,1)S(1)} %collective-permute-done.1.refs_2_), channel_id=1, source_target_pairs={{0,8},{1,9},{2,10},{3,11},{4,12},{5,13},{6,14},{7,15},{8,0},{9,1},... | collective-permute-start | bytes 147464 | tf_op jit(solution)/shard_map/ppermute | solution.py:27
  22.2 1.4 %collective-permute-start.6 = (f32[4,64,128]{2,1,0:T(8,128)S(1)}, f32[4,64,128]{2,1,0:T(8,128)S(1)}, u32[]{:S(2)}, u32[]{:S(2)}) collective-permute-start(f32[4,64,128]{2,1,0:T(8,128)S(1)} %get-tuple-element.52), channel_id=1, source_target_pairs={{0,8},{1,9},{2,10},{3,11},{4,12},{5,13},{6,14},{7,15},{8,0},{9,1},... | collective-permute-start | bytes 393224 | tf_op jit(solution)/shard_map/ppermute | solution.py:27
  23.6 6.5 %collective-permute-start.10 = (f32[64,128]{1,0:T(8,128)S(1)}, f32[64,128]{1,0:T(8,128)S(1)}, u32[]{:S(2)}, u32[]{:S(2)}) collective-permute-start(f32[64,128]{1,0:T(8,128)S(1)} %get-tuple-element.54), channel_id=1, source_target_pairs={{0,6},{1,7},{2,4},{3,5},{4,2},{5,3},{6,0},{7,1},{8,13},{9,12},{10,... | collective-permute-start | bytes 98312 | tf_op jit(solution)/shard_map/ppermute | solution.py:27
  24.7 5.7 %collective-permute-start.7 = (f32[64,128]{1,0:T(8,128)S(1)}, f32[64,128]{1,0:T(8,128)S(1)}, u32[]{:S(2)}, u32[]{:S(2)}) collective-permute-start(f32[64,128]{1,0:T(8,128)S(1)} %get-tuple-element.53), channel_id=1, source_target_pairs={{0,3},{1,2},{2,1},{3,0},{4,7},{5,6},{6,5},{7,4},{8,15},{9,14},{10,... | collective-permute-start | bytes 98312 | tf_op jit(solution)/shard_map/ppermute | solution.py:27
  26.0 4.4 %collective-permute-start.8 = (f32[64,128]{1,0:T(8,128)S(1)}, f32[64,128]{1,0:T(8,128)S(1)}, u32[]{:S(2)}, u32[]{:S(2)}) collective-permute-start(f32[64,128]{1,0:T(8,128)S(1)} %get-tuple-element.55), channel_id=1, source_target_pairs={{0,4},{1,5},{2,6},{3,7},{4,0},{5,1},{6,2},{7,3},{8,10},{9,11},{10,... | collective-permute-start | bytes 98312 | tf_op jit(solution)/shard_map/ppermute | solution.py:27
  27.3 3.1 %collective-permute-start.9 = (f32[64,128]{1,0:T(8,128)S(1)}, f32[64,128]{1,0:T(8,128)S(1)}, u32[]{:S(2)}, u32[]{:S(2)}) collective-permute-start(f32[64,128]{1,0:T(8,128)S(1)} %get-tuple-element.56), channel_id=1, source_target_pairs={{8,9},{9,8},{10,11},{11,10},{12,13},{13,12},{14,15},{15,14},{24,25... | collective-permute-start | bytes 98312 | tf_op jit(solution)/shard_map/ppermute | solution.py:27
  30.4 4.0 %collective-permute-start.11 = (f32[64,128]{1,0:T(8,128)S(1)}, f32[64,128]{1,0:T(8,128)S(1)}, u32[]{:S(2)}, u32[]{:S(2)}) collective-permute-start(f32[64,128]{1,0:T(8,128)S(1)} %add_add_fusion), channel_id=1, source_target_pairs={{0,16},{1,17},{2,18},{3,19},{4,20},{5,21},{6,22},{7,23},{8,24},{9,... | collective-permute-start | bytes 98312 | tf_op jit(solution)/shard_map/ppermute | solution.py:27
  34.4 1.4 %collective-permute-start.12 = (f32[64,128]{1,0:T(8,128)S(1)}, f32[64,128]{1,0:T(8,128)S(1)}, u32[]{:S(2)}, u32[]{:S(2)}) collective-permute-start(f32[64,128]{1,0:T(8,128)S(1)} %add.26), channel_id=1, source_target_pairs={{0,8},{1,9},{2,10},{3,11},{4,12},{5,13},{6,14},{7,15},{8,0},{9,1},... | collective-permute-start | bytes 98312 | tf_op jit(solution)/shard_map/ppermute | solution.py:27
